TPU v7x, 512 devices: a whole 4x8x8 slice. The times are simulated.
512 devices in a mesh: front: 16 (over y_lo, x, core), row: 4 (over y_hi), col: 8 (over z).
Axes of the slice: x: 4, y: 8 (y_hi: 4, y_lo: 2; y = y_hi * 2 + y_lo), z: 8, core: 2. Of those that a mesh axis runs over, the one named last changes fastest.
Arguments:
- assembled: float32 [16, 4096, 4096], P('front', ('row', 'col')), may hold values from -6 to 6
- update: bfloat16 [16, 1536, 1536], P('front', ('row', 'col')), may hold values from -6 to 6
- blocks: int32 [16, 12], P('front'), may hold values from 16 to 31, as said below
- inverses: bfloat16 [16, 2, 512, 512], P('front'), as said below
Outputs:
- factor: bfloat16 [16, 4096, 1024], P('front', ('row', 'col'))
- schur: float32 [16, 4096, 3072], P('front', ('row', 'col'))
Inputs may be any that keep to these rules, and one draw needn't show every extreme that they name: `blocks`: for each front the entries are strictly increasing, the first is 16 and the last 31. `inverses`: each 512 x 512 matrix is upper triangular.
All inputs are finite; a program needn't handle non-finite values.
Results may differ from a plain program's by a relative error of at most 0.0034.
Values may be sent and summed in bfloat16 or wider, within the bound.
No kernel may reach another device: no remote copies, remote signals or barrier semaphores. Data moves between devices by JAX's collectives and lax.ppermute only.
A program may use at most 64 MiB of HBM per device.

v0:
```python
import jax
import jax.numpy as jnp
from jax import lax
from jax.sharding import PartitionSpec as P

ORDER = 4096
BLOCK = 128
PARENT_BLOCKS = 32
CHILD_BLOCKS = 12


def partner(x, axis, bit):
    return lax.ppermute(x, axis, [(i, i ^ 1 << bit) for i in range(lax.axis_size(axis))])


def make_picker(child_targets, global_rows, piece):
    select = (global_rows[:, None] == child_targets[None, :]).astype(jnp.bfloat16)
    return jnp.dot(select, piece[0], preferred_element_type=jnp.float32)


def on_device(assembled, update, blocks, inverses):
    rows_here = assembled.shape[1]
    width = inverses.shape[2]
    frontal_own = assembled[0]
    first_row = lax.axis_index(("row", "col")) * rows_here
    global_rows = first_row + jnp.arange(rows_here, dtype=jnp.int32)
    offsets = jnp.arange(BLOCK, dtype=jnp.int32)
    child_targets = (blocks[0][:, None] * BLOCK + offsets[None, :]).reshape(-1)
    incoming = partner(update, "front", 0)
    picked = make_picker(
        child_targets, global_rows, lax.all_gather(incoming, ("row", "col"), axis=1, tiled=True)
    )
    block_map = blocks[0]
    placing = (block_map[:, None] == jnp.arange(PARENT_BLOCKS, dtype=jnp.int32)[None, :]).astype(
        jnp.float32
    )
    spread_out = jnp.einsum(
        "rak,ap->rpk",
        picked.reshape(rows_here, CHILD_BLOCKS, BLOCK),
        placing,
        precision=lax.Precision.HIGHEST,
    )
    frontal = frontal_own + spread_out.reshape(rows_here, ORDER)
    inverse_one = inverses[0, 0].astype(jnp.float32)
    inverse_two = inverses[0, 1].astype(jnp.float32)
    first = jnp.dot(
        frontal[:, :width],
        inverse_one,
        precision=lax.Precision.HIGHEST,
        preferred_element_type=jnp.float32,
    ).astype(jnp.bfloat16)
    below = global_rows[:, None] >= width
    every_first = lax.all_gather(first, ("row", "col"), axis=0, tiled=True)
    second = frontal[:, width:] - jnp.dot(
        first, every_first[width:].T, preferred_element_type=jnp.float32
    )
    raw_panel = jnp.dot(
        second[:, :width],
        inverse_two,
        precision=lax.Precision.HIGHEST,
        preferred_element_type=jnp.float32,
    )
    panel = jnp.where(below, raw_panel, jnp.zeros_like(raw_panel)).astype(jnp.bfloat16)
    every_panel = lax.all_gather(panel, ("row", "col"), axis=0, tiled=True)
    schur = second[:, width:] - jnp.dot(
        panel, every_panel[2 * width :].T, preferred_element_type=jnp.float32
    )
    factor = jnp.concatenate([first, panel], axis=1)
    return (factor[None], schur[None])


def solution(mesh):
    return jax.shard_map(
        on_device,
        mesh=mesh,
        in_specs=(
            P("front", ("row", "col"), None),
            P("front", ("row", "col"), None),
            P("front", None),
            P("front", None, None, None),
        ),
        out_specs=(P("front", ("row", "col"), None), P("front", ("row", "col"), None)),
        check_vma=False,
    )
```

profile of v0, /device:TPU:1, one launch (start us, length us, event | category | flops | bytes accessed | tf_op | source)
XLA Modules:
  0.0 352.3 jit_solution(14798689473032236077)
XLA Ops:
  7.2 0.0 all-gather.4.cloned.1.call-start
  7.2 8.8 %collective-permute-start = (bf16[1,48,1536]{2,1,0:T(8,128)(2,1)}, bf16[1,48,1536]{2,1,0:T(8,128)(2,1)S(1)}, u32[]{:S(2)}, u32[]{:S(2)}) collective-permute-start(bf16[1,48,1536]{2,1,0:T(8,128)(2,1)} %param.5), channel_id=1, source_target_pairs={{0,32},{32,0},{64,96},{96,64},{128,160},{160,128},{192,224},{224,1... | collective-permute-start | bytes 442376 | tf_op jit(solution)/shard_map/ppermute | solution.py:13
  16.0 1.2 collective-permute-done
  17.2 0.0 copy-start.4
  17.2 0.7 copy-done.4
  17.9 0.0 all-gather.4.cloned.1.call-update
  17.9 0.0 all-gather.6.cloned.1.call-start
  18.0 0.7 broadcast_multiply_fusion
  18.6 0.1 add_bitcast_fusion
  18.7 104.3 %all-gather.4.cloned.1.call-done = bf16[1,1536,1536]{2,1,0:T(8,128)(2,1)} async-done(((bf16[1,48,1536]{2,1,0:T(8,128)(2,1)}), bf16[1,1536,1536]{2,1,0:T(8,128)(2,1)}) %all-gather.4.cloned.1.call-update) | async-done | bytes 4718608 | tf_op jit(solution)/shard_map/all_gather | solution.py:31
  122.9 6.7 %copy.7 = bf16[1,1536,1536]{1,2,0:T(8,128)(2,1)} copy(bf16[1,1536,1536]{2,1,0:T(8,128)(2,1)} %all-gather.4.cloned.1.call-done) | data formatting | bytes 9437184 | tf_op jit(solution)/shard_map/all_gather | solution.py:31
  129.7 0.0 copy-start.5
  129.7 4.0 %fusion.6 = f32[128,12,128]{2,0,1:T(8,128)S(1)} fusion(bf16[12,128,1536]{2,1,0:T(8,128)(2,1)} %bitcast.34, s32[1536]{0:T(1024)S(1)} %add_bitcast_fusion, s32[128]{0:T(128)S(1)} %iota_add_fusion), kind=kOutput, calls=%fused_computation.11 | convolution fusion | flops 604176384 | bytes 5511680 | tf_op jit(solution)/shard_map/dot_general | solution.py:18
  133.7 0.0 copy-start.2
  133.7 0.0 copy-done.5
  133.7 1.4 fusion.4
  135.1 0.2 copy-done.2
  135.3 0.0 copy-start.3
  135.3 1.8 bitcast_add_fusion
  137.1 0.0 copy-done.3
  137.1 1.0 convolution_convert_fusion
  138.1 0.0 all-gather.6.cloned.1.call-update
  138.2 0.0 all-gather.8.cloned.1.call-start
  138.2 0.0 copy-start.1
  138.2 98.2 %all-gather.6.cloned.1.call-done = bf16[4096,512]{1,0:T(8,128)(2,1)} async-done(((bf16[128,512]{1,0:T(8,128)(2,1)}), bf16[4096,512]{1,0:T(8,128)(2,1)}) %all-gather.6.cloned.1.call-update) | async-done | bytes 4194320 | tf_op jit(solution)/shard_map/all_gather | solution.py:53
  236.5 3.4 convolution_subtract_fusion
  239.9 0.0 copy-start
  239.9 1.2 copy-done
  241.2 1.0 fusion.3
  242.2 0.0 all-gather.8.cloned.1.call-update
  242.2 0.0 copy-done.1
  242.2 1.6 maximum_bitcast_fusion
  243.9 97.3 %all-gather.8.cloned.1.call-done = bf16[4096,512]{1,0:T(8,128)(2,1)} async-done(((bf16[128,512]{1,0:T(8,128)(2,1)}), bf16[4096,512]{1,0:T(8,128)(2,1)}) %all-gather.8.cloned.1.call-update) | async-done | bytes 4194320 | tf_op jit(solution)/shard_map/all_gather | solution.py:64
  341.1 4.7 %fusion = f32[1,128,3072]{2,1,0:T(8,128)} fusion(bf16[128,512]{1,0:T(8,128)(2,1)} %fusion.3, bf16[4096,512]{1,0:T(8,128)(2,1)} %all-gather.8.cloned.1.call-done, f32[128,3584]{1,0:T(8,128)} %copy-done), kind=kOutput, calls=%fused_computation.2 | convolution fusion | flops 403046400 | bytes 6422528 | tf_op jit(solution)/shard_map/dot_general | solution.py:65
  (2 shorter events, 0.0 us)
Async XLA Ops:
  7.2 115.8 %all-gather.4.cloned.1.call-start = ((), (), s32[]{:S(2)}) async-start(), calls=%async_computation | async-start | bytes 4866048 | tf_op jit(solution)/shard_map/all_gather | solution.py:31
  7.2 10.0 %collective-permute-start = (bf16[1,48,1536]{2,1,0:T(8,128)(2,1)}, bf16[1,48,1536]{2,1,0:T(8,128)(2,1)S(1)}, u32[]{:S(2)}, u32[]{:S(2)}) collective-permute-start(bf16[1,48,1536]{2,1,0:T(8,128)(2,1)} %param.5), channel_id=1, source_target_pairs={{0,32},{32,0},{64,96},{96,64},{128,160},{160,128},{192,224},{224,1... | collective-permute-start | bytes 442376 | tf_op jit(solution)/shard_map/ppermute | solution.py:13
  17.2 0.7 copy-start.4
  17.9 218.6 %all-gather.6.cloned.1.call-start = ((), (), s32[]{:S(2)}) async-start(), calls=%async_computation.1 | async-start | bytes 4325376 | tf_op jit(solution)/shard_map/all_gather | solution.py:53
  129.7 4.0 %copy-start.5 = (s32[1,12]{1,0:T(1,128)S(1)}, s32[1,12]{1,0:T(1,128)}, u32[]{:S(2)}) copy-start(s32[1,12]{1,0:T(1,128)} %param.6) | copy-start | bytes 148
  133.7 1.6 copy-start.2
  135.3 1.8 copy-start.3
  138.2 202.9 %all-gather.8.cloned.1.call-start = ((), (), s32[]{:S(2)}) async-start(), calls=%async_computation.2 | async-start | bytes 4325376 | tf_op jit(solution)/shard_map/all_gather | solution.py:64
  138.2 104.0 %copy-start.1 = (bf16[128,512]{1,0:T(8,128)(2,1)S(1)}, bf16[128,512]{1,0:T(8,128)(2,1)}, u32[]{:S(2)}) copy-start(bf16[128,512]{1,0:T(8,128)(2,1)} %convolution_convert_fusion) | copy-start | bytes 393220
  239.9 1.3 copy-start
Sparse Core Ops, SparseCore 0:
  18.0 104.8 all-gather.3
  138.3 98.1 all-gather.5
  242.3 98.7 all-gather.7
where the time goes:
time: 354 us; the launch traced here: 352 us
  waiting for transfers between devices  301 us (85%)
  matrix products  15.6 us (4%)
  between operations  13.9 us (4%)
  starting transfers between devices  8.91 us (3%)
  local copies, waits for them, and re-layouts  8.79 us (2%)
  other arithmetic  4.18 us (1%)
    all_gather x1, waiting for transfers between devices, on_device(): lax.all_gather(incoming, ('row', 'col'), axis=1, tiled=True)  104 us
    all_gather x1, waiting for transfers between devices, on_device(): every_first = lax.all_gather(first, ('row', 'col'), axis=0, tiled=True)  98.2 us
    all_gather x1, waiting for transfers between devices, on_device(): every_panel = lax.all_gather(panel, ('row', 'col'), axis=0, tiled=True)  97.3 us
    ppermute x1, starting transfers between devices, partner(): lax.ppermute(x, axis, [(i, i ^ 1 << bit) for i in range(lax.axis_size(axi...  8.79 us
  transfers between devices with their start and end apart: 4, of which 4 were waited for; matrix products, arithmetic and copies ran while one was open for 1% of the time, Pallas kernels for 0%

commit v1 on v0

v1 whole, which is shorter than its diff:
```python
import jax
import jax.numpy as jnp
from jax import lax
from jax.experimental import pallas as pl
from jax.experimental.pallas import tpu as pltpu
from jax.sharding import PartitionSpec as P

WIDTH = 512
ROWS = 128
GROUP = 1024
CHILD = 1536
CHILD_BLOCKS = 12
CHILD_ROWS = 48
VMEM_LIMIT = 48 * 1024 * 1024

F32 = jnp.float32
BF16 = jnp.bfloat16


def dot(a, b):
    return jnp.dot(a, b, preferred_element_type=F32)


def dot_t(a, b):
    return lax.dot_general(a, b, (((1,), (1,)), ((), ())), preferred_element_type=F32)


def dot_split(a, b, terms):
    total = None
    for _ in range(terms):
        part = a.astype(BF16)
        a = a - part.astype(F32)
        product = dot(part, b)
        total = product if total is None else total + product
    return total


def first_kernel(front_ref, inverse_ref, both_ref, first_ref, next_ref):
    first = dot_split(front_ref[0, :, :WIDTH], inverse_ref[0, 0], 3).astype(BF16)
    following = front_ref[0, :, WIDTH:].astype(BF16)
    first_ref[...] = first
    next_ref[...] = following
    both_ref[:, :WIDTH] = first
    both_ref[:, WIDTH:] = following


def first_panel(assembled, inverses):
    return pl.pallas_call(
        first_kernel,
        grid=(1,),
        in_specs=[
            pl.BlockSpec((1, ROWS, 2 * WIDTH), lambda i: (0, 0, 0)),
            pl.BlockSpec((1, 1, WIDTH, WIDTH), lambda i: (0, 0, 0, 0)),
        ],
        out_specs=[
            pl.BlockSpec((ROWS, 2 * WIDTH), lambda i: (0, 0)),
            pl.BlockSpec((ROWS, WIDTH), lambda i: (0, 0)),
            pl.BlockSpec((ROWS, WIDTH), lambda i: (0, 0)),
        ],
        out_shape=[
            jax.ShapeDtypeStruct((ROWS, 2 * WIDTH), BF16),
            jax.ShapeDtypeStruct((ROWS, WIDTH), BF16),
            jax.ShapeDtypeStruct((ROWS, WIDTH), BF16),
        ],
        compiler_params=pltpu.CompilerParams(vmem_limit_bytes=VMEM_LIMIT),
        name="first_panel",
    )(assembled, inverses)


def piece_of(z):
    return jnp.where(z < 4, z ^ 1, z - 4)


def product_kernel(
    where_ref, front_ref, inverse_ref, first_ref, firsts_ref, nexts_ref, column_ref,
    mine_ref, beside_ref, across_ref, product_ref, factor_ref, second_ref, rows_ref,
):
    r, z = where_ref[0], where_ref[1]
    other = jnp.where(z % 2 == 1, (z + 1) % 8, (z + 7) % 8)
    here, there = piece_of(z), piece_of(other)

    def put(piece, value):
        second_ref[pl.ds(pl.multiple_of(piece * ROWS, ROWS), ROWS), :] = value

    put(here, mine_ref[...])
    put(here ^ 1, beside_ref[...])
    put(there, across_ref[:ROWS])
    put(there ^ 1, across_ref[ROWS:])
    inverse = inverse_ref[0, 0]

    own = front_ref[0] - dot_t(first_ref[...], second_ref[...])
    own = dot_split(own, inverse, 3)
    own = jnp.where((r == 0) & (z < 4), jnp.zeros_like(own), own)
    factor_ref[0, :, :WIDTH] = first_ref[...]
    factor_ref[0, :, WIDTH:] = own.astype(BF16)

    for k in range(4):
        panel = nexts_ref[k].astype(F32) - dot_t(firsts_ref[k], second_ref[...])
        panel = dot_split(panel, inverse, 2)
        if k == 0:
            panel = jnp.where(z < 4, jnp.zeros_like(panel), panel)
        rows_ref[pl.ds(k * ROWS, ROWS), :WIDTH] = firsts_ref[k]
        rows_ref[pl.ds(k * ROWS, ROWS), WIDTH:] = panel.astype(BF16)

    def column(j, carry):
        first = column_ref[j, :, :WIDTH]
        panel = column_ref[j, :, WIDTH:].astype(F32) - dot_t(first, second_ref[...])
        panel = dot_split(panel, inverse, 2).astype(BF16)
        place = pl.ds(pl.multiple_of(j * ROWS, ROWS), ROWS)
        for k in range(4):
            rows = rows_ref[pl.ds(k * ROWS, ROWS), :]
            total = dot_t(rows[:, :WIDTH], first) + dot_t(rows[:, WIDTH:], panel)
            product_ref[k, :, place] = total.astype(BF16)
        return carry

    lax.fori_loop(0, 8, column, 0)


def products(where, assembled, inverses, first, firsts, nexts, columns, mine, beside, across):
    whole = lambda *shape: pl.BlockSpec(shape, lambda i, w: (0,) * len(shape))
    return pl.pallas_call(
        product_kernel,
        grid_spec=pltpu.PrefetchScalarGridSpec(
            num_scalar_prefetch=1,
            grid=(1,),
            in_specs=[
                pl.BlockSpec((1, ROWS, WIDTH), lambda i, w: (0, 0, 1)),
                pl.BlockSpec((1, 1, WIDTH, WIDTH), lambda i, w: (0, 1, 0, 0)),
                whole(ROWS, WIDTH),
                whole(4, ROWS, WIDTH),
                whole(4, ROWS, WIDTH),
                whole(8, ROWS, 2 * WIDTH),
                whole(ROWS, WIDTH),
                whole(ROWS, WIDTH),
                whole(2 * ROWS, WIDTH),
            ],
            out_specs=[whole(4, ROWS, GROUP), whole(1, ROWS, 2 * WIDTH)],
            scratch_shapes=[
                pltpu.VMEM((WIDTH, WIDTH), BF16),
                pltpu.VMEM((4 * ROWS, 2 * WIDTH), BF16),
            ],
        ),
        out_shape=[
            jax.ShapeDtypeStruct((4, ROWS, GROUP), BF16),
            jax.ShapeDtypeStruct((1, ROWS, 2 * WIDTH), BF16),
        ],
        compiler_params=pltpu.CompilerParams(vmem_limit_bytes=VMEM_LIMIT),
        name="products",
    )(where, assembled, inverses, first, firsts, nexts, columns, mine, beside, across)


PIECES = (
    ((0, 0, 48, 0), (1, 0, 48, 48), (2, 0, 32, 96)),
    ((2, 32, 16, 0), (3, 0, 48, 16), (4, 0, 48, 64), (5, 0, 16, 112)),
    ((5, 16, 32, 0), (6, 0, 48, 32), (7, 0, 48, 80)),
)


def final_kernel(where_ref, front_ref, product_ref, child_ref, schur_ref, block_ref, sems):
    step = pl.program_id(0)
    r, z = where_ref[0], where_ref[1]
    target = r * 8 + z
    found, child = jnp.int32(0), jnp.int32(0)
    for b in range(CHILD_BLOCKS):
        hit = (where_ref[2 + b] == target).astype(jnp.int32)
        found, child = found + hit, child + hit * b
    slot = jnp.clip(r - child // 3, 0, 2)
    turn = child % 3

    def copies(j):
        return [
            pltpu.make_async_copy(
                child_ref.at[z_from, slot, pl.ds(start, rows), :],
                block_ref.at[pl.ds(place, rows), :],
                sems.at[i],
            )
            for i, (z_from, start, rows, place) in enumerate(PIECES[j])
        ]

    for j in range(3):
        @pl.when((step == 0) & (found > 0) & (turn == j))
        def _():
            for copy in copies(j):
                copy.start()

    schur_ref[0] = front_ref[0] - product_ref[0].astype(F32)

    for j in range(3):
        @pl.when((step == 1) & (found > 0) & (turn == j))
        def _():
            for copy in copies(j):
                copy.wait()

    for b in range(CHILD_BLOCKS):
        parent = where_ref[2 + b]
        @pl.when((found > 0) & (step > 0) & (parent // 8 == step + 1))
        def _():
            place = pl.ds(pl.multiple_of((parent % 8) * ROWS, ROWS), ROWS)
            schur_ref[0, :, place] += block_ref[:, b * ROWS : (b + 1) * ROWS].astype(F32)


def final(where, assembled, product, children):
    return pl.pallas_call(
        final_kernel,
        grid_spec=pltpu.PrefetchScalarGridSpec(
            num_scalar_prefetch=1,
            grid=(3,),
            in_specs=[
                pl.BlockSpec((1, ROWS, GROUP), lambda i, w: (0, 0, i + 1)),
                pl.BlockSpec((1, ROWS, GROUP), lambda i, w: (i + 1, 0, 0)),
                pl.BlockSpec(memory_space=pl.ANY),
            ],
            out_specs=pl.BlockSpec((1, ROWS, GROUP), lambda i, w: (0, 0, i)),
            scratch_shapes=[
                pltpu.VMEM((ROWS, CHILD), BF16),
                pltpu.SemaphoreType.DMA((4,)),
            ],
        ),
        out_shape=jax.ShapeDtypeStruct((1, ROWS, 3 * GROUP), F32),
        compiler_params=pltpu.CompilerParams(vmem_limit_bytes=VMEM_LIMIT),
        name="final",
    )(where, assembled, product, children)


def send_child(update):
    received = []
    for distance in range(3):
        pairs = [
            (front * 4 + k, (front ^ 1) * 4 + k + distance)
            for front in range(16)
            for k in range(4)
            if 2 <= k + distance <= 3
        ]
        received.append(lax.ppermute(update[0], ("front", "row"), pairs))
    return jnp.stack(received)


def on_device(assembled, update, blocks, inverses):
    r, z = lax.axis_index("row"), lax.axis_index("col")
    where = jnp.concatenate([jnp.stack([r, z]).astype(jnp.int32), blocks[0]])

    both, first, following = first_panel(assembled, inverses)
    columns = lax.all_gather(both, "col", axis=0)
    firsts = lax.all_gather(first, "row", axis=0)

    top = firsts[0]
    passed = lax.ppermute(top, "col", [(4, 1), (5, 0), (6, 3), (7, 2)])
    mine = jnp.where(z < 4, passed, top)
    beside = lax.ppermute(mine, "col", [(i, i ^ 1) for i in range(8)])
    across = lax.ppermute(
        jnp.concatenate([mine, beside]),
        "col",
        [(i, (i + 1) % 8 if i % 2 else (i + 7) % 8) for i in range(8)],
    )
    nexts = lax.all_gather(following, "row", axis=0)
    arriving = send_child(update)
    arriving, columns = lax.optimization_barrier((arriving, columns))
    children = lax.all_gather(arriving, "col", axis=0)

    product, factor = products(
        where, assembled, inverses, first, firsts, nexts, columns, mine, beside, across
    )
    product = lax.all_to_all(product, "row", 0, 0)
    return factor, final(where, assembled, product, children)


def solution(mesh):
    return jax.shard_map(
        on_device,
        mesh=mesh,
        in_specs=(
            P("front", ("row", "col"), None),
            P("front", ("row", "col"), None),
            P("front", None),
            P("front", None, None, None),
        ),
        out_specs=(P("front", ("row", "col"), None), P("front", ("row", "col"), None)),
        check_vma=False,
    )
```

time: 354 us -> 167 us (0.47)
  the two profiles are of different devices: /device:TPU:1 before, /device:TPU:60 now
where the time goes in v1:
time: 167 us
  waiting for transfers between devices  60.2 us (36%)
  blocking collectives  56.5 us (34%)
  Pallas kernels  16.5 us (10%)
  between operations  14.2 us (9%)
  starting transfers between devices  12.1 us (7%)
  local copies, waits for them, and re-layouts  5.32 us (3%)
  other arithmetic  1.82 us (1%)
    all_gather x1, waiting for transfers between devices, on_device(): columns = lax.all_gather(both, 'col', axis=0)  31.1 us
    all_to_all x1, blocking collectives, on_device(): product = lax.all_to_all(product, 'row', 0, 0)  25.4 us
    all_gather x1, blocking collectives, on_device(): firsts = lax.all_gather(first, 'row', axis=0)  15.9 us
    all_gather x1, blocking collectives, on_device(): nexts = lax.all_gather(following, 'row', axis=0)  15.2 us
    pallas_call x1, Pallas kernels, products(): pl.pallas_call(product_kernel, grid_spec=pltpu.PrefetchScalarGridSpec(num...  12.2 us
    ppermute x3, waiting for transfers between devices, send_child(): received.append(lax.ppermute(update[0], ('front', 'row'), pairs))  12 us
    ppermute x1, waiting for transfers between devices, on_device(): passed = lax.ppermute(top, 'col', [(4, 1), (5, 0), (6, 3), (7, 2)])  11.3 us
    ppermute x1, waiting for transfers between devices, on_device(): beside = lax.ppermute(mine, 'col', [(i, i ^ 1) for i in range(8)])  5.71 us
  transfers between devices with their start and end apart: 8, of which 5 were waited for; matrix products, arithmetic and copies ran while one was open for 1% of the time, Pallas kernels for 7%

profile of v1, /device:TPU:60, one launch (start us, length us, event | category | flops | bytes accessed | tf_op | source)
XLA Modules:
  0.0 166.7 jit_solution(9826709653338560568)
XLA Ops:
  7.2 0.0 all-gather.7.cloned.1.call-start
  7.2 0.0 copy-start
  7.2 1.6 copy-done
  8.8 0.0 copy-start.2
  8.8 1.2 copy-done.2
  10.0 0.0 copy-start.8
  10.0 1.1 first_panel.1
  11.1 0.0 copy-start.6
  11.1 0.7 copy-done.6
  11.8 0.0 copy-start.7
  11.8 0.0 copy-start.1
  11.8 0.0 copy-start.3
  11.8 0.0 all-gather.7.cloned.1.call-update
  11.8 0.0 all-gather.9.cloned.1.call-start
  11.8 0.0 copy-done.8
  11.9 1.6 collective-permute-start.2
  13.4 1.3 collective-permute-start.1
  14.7 1.9 %collective-permute-start = (bf16[48,1536]{1,0:T(8,128)(2,1)S(1)}, bf16[48,1536]{1,0:T(8,128)(2,1)S(1)}, u32[]{:S(2)}, u32[]{:S(2)}) collective-permute-start(bf16[48,1536]{1,0:T(8,128)(2,1)S(1)} %bitcast.21), channel_id=1, source_target_pairs={{16,48},{24,56},{48,16},{56,24},{80,112},{88,120},{112,80},{120,88... | collective-permute-start | bytes 442376 | tf_op jit(solution)/shard_map/ppermute | solution.py:234
  16.7 7.5 %collective-permute-done.2 = bf16[48,1536]{1,0:T(8,128)(2,1)S(1)} collective-permute-done((bf16[48,1536]{1,0:T(8,128)(2,1)S(1)}, bf16[48,1536]{1,0:T(8,128)(2,1)S(1)}, u32[]{:S(2)}, u32[]{:S(2)}) %collective-permute-start.2) | collective-permute-done | bytes 147488 | tf_op jit(solution)/shard_map/ppermute | solution.py:234
  24.2 4.5 %collective-permute-done.1 = bf16[48,1536]{1,0:T(8,128)(2,1)S(1)} collective-permute-done((bf16[48,1536]{1,0:T(8,128)(2,1)S(1)}, bf16[48,1536]{1,0:T(8,128)(2,1)S(1)}, u32[]{:S(2)}, u32[]{:S(2)}) %collective-permute-start.1) | collective-permute-done | bytes 147488 | tf_op jit(solution)/shard_map/ppermute | solution.py:234
  28.7 0.0 collective-permute-done
  28.7 0.8 pad_maximum_fusion
  29.5 31.1 %all-gather.7.cloned.1.call-done = bf16[1024,1024]{1,0:T(8,128)(2,1)} async-done(((bf16[128,1024]{1,0:T(8,128)(2,1)}), bf16[1024,1024]{1,0:T(8,128)(2,1)}) %all-gather.7.cloned.1.call-update) | async-done | bytes 2097168 | tf_op jit(solution)/shard_map/all_gather | solution.py:243
  60.6 0.0 all-gather.9.cloned.1.call-update
  60.6 15.9 %all-gather = bf16[512,512]{1,0:T(8,128)(2,1)S(1)} all-gather(bf16[128,512]{1,0:T(8,128)(2,1)S(1)} %get-tuple-element.9.first_ref), channel_id=2, replica_groups=mesh['front'=16,'row'=4,'col'=8] {'row'}, dimensions={0}, use_global_device_ids=true | all-gather | bytes 655360 | tf_op jit(solution)/shard_map/all_gather | solution.py:244
  76.5 0.0 copy-start.4
  76.5 0.8 copy-done.4
  77.3 1.3 collective-permute-start.3
  78.6 11.3 %collective-permute-done.3 = bf16[128,512]{1,0:T(8,128)(2,1)S(1)} collective-permute-done((bf16[128,512]{1,0:T(8,128)(2,1)S(1)}, bf16[128,512]{1,0:T(8,128)(2,1)S(1)}, u32[]{:S(2)}, u32[]{:S(2)}) %collective-permute-start.3) | collective-permute-done | bytes 131104 | tf_op jit(solution)/shard_map/ppermute | solution.py:247
  90.0 0.9 broadcast_select_fusion.mine_ref
  90.9 4.1 %collective-permute-start.4 = (bf16[128,512]{1,0:T(8,128)(2,1)S(1)}, bf16[128,512]{1,0:T(8,128)(2,1)S(1)}, u32[]{:S(2)}, u32[]{:S(2)}) collective-permute-start(bf16[128,512]{1,0:T(8,128)(2,1)S(1)} %broadcast_select_fusion.mine_ref), channel_id=1, source_target_pairs={{0,1},{1,0},{2,3},{3,2},{4,5},{5,4},{6,7},{7,6},{8,9},{9,8},{10,11... | collective-permute-start | bytes 393224 | tf_op jit(solution)/shard_map/ppermute | solution.py:249
  95.0 5.7 %collective-permute-done.4.beside_ref = bf16[128,512]{1,0:T(8,128)(2,1)S(1)} collective-permute-done((bf16[128,512]{1,0:T(8,128)(2,1)S(1)}, bf16[128,512]{1,0:T(8,128)(2,1)S(1)}, u32[]{:S(2)}, u32[]{:S(2)}) %collective-permute-start.4) | collective-permute-done | bytes 131104 | tf_op jit(solution)/shard_map/ppermute | solution.py:249
  100.7 1.9 %collective-permute-start.5 = (bf16[256,512]{1,0:T(8,128)(2,1)S(1)}, bf16[256,512]{1,0:T(8,128)(2,1)S(1)}, u32[]{:S(2)}, u32[]{:S(2)}) collective-permute-start(bf16[256,512]{1,0:T(8,128)(2,1)S(1)} %pad_maximum_fusion.1), channel_id=1, source_target_pairs={{0,7},{1,2},{2,1},{3,4},{4,3},{5,6},{6,5},{7,0},{8,15},{9,10},{10,... | collective-permute-start | bytes 786440 | tf_op jit(solution)/shard_map/ppermute | solution.py:250
  102.7 0.0 copy-done.7
  102.7 0.1 pad_add_fusion.where_ref
  102.7 15.2 %all-gather.1 = bf16[512,512]{1,0:T(8,128)(2,1)S(1)} all-gather(bf16[128,512]{1,0:T(8,128)(2,1)} %copy-done.6), channel_id=3, replica_groups=mesh['front'=16,'row'=4,'col'=8] {'row'}, dimensions={0}, use_global_device_ids=true | all-gather | bytes 655360 | tf_op jit(solution)/shard_map/all_gather | solution.py:255
  117.9 0.0 collective-permute-done.5.across_ref
  117.9 0.0 copy-done.1
  117.9 0.0 copy-done.3
  117.9 0.0 copy-start.5
  118.0 1.0 copy-done.5
  119.0 12.2 %products.1 = (bf16[4,128,1024]{2,1,0:T(8,128)(2,1)S(1)}, bf16[1,128,1024]{2,1,0:T(8,128)(2,1)}) custom-call(s32[14]{0:T(128)S(1)} %pad_add_fusion.where_ref, f32[1,128,4096]{2,1,0:T(8,128)S(1)} %copy-done.1, bf16[1,2,512,512]{3,2,1,0:T(8,128)(2,1)S(1)} %copy-done.3, bf16[128,512]{1,0:T(8,128)(2,1)S(1)} %get-tuple-element.9.first_ref, ...), custom_call_target="tpu_custom_call" | custom-call | tf_op jit(solution)/shard_map/products/pallas_call | solution.py:121
  131.2 25.4 %all_to_all.5.product_ref = bf16[4,128,1024]{2,1,0:T(8,128)(2,1)S(1)} all-to-all(bf16[4,128,1024]{2,1,0:T(8,128)(2,1)S(1)} %get-tuple-element.14), channel_id=1, replica_groups=mesh['front'=16,'row'=4,'col'=8] {'row'}, dimensions={0} | all-to-all | bytes 2097152 | tf_op jit(solution)/shard_map/all_to_all | solution.py:263
  156.6 0.0 all-gather.9.cloned.1.call-done
  156.6 3.2 %final.1 = f32[1,128,3072]{2,1,0:T(8,128)} custom-call(s32[14]{0:T(128)S(1)} %pad_add_fusion.where_ref, f32[1,128,4096]{2,1,0:T(8,128)S(1)} %copy-done.1, bf16[4,128,1024]{2,1,0:T(8,128)(2,1)S(1)} %all_to_all.5.product_ref, bf16[8,3,48,1536]{3,2,1,0:T(8,128)(2,1)} %bitcast.13), custom_call_target="tpu_custom_call" | custom-call | tf_op jit(solution)/shard_map/final/pallas_call | solution.py:203
  (2 shorter events, 0.0 us)
Async XLA Ops:
  7.2 53.4 %all-gather.7.cloned.1.call-start = ((), (), s32[]{:S(2)}) async-start(), calls=%async_computation.1 | async-start | bytes 2359296 | tf_op jit(solution)/shard_map/all_gather | solution.py:243
  7.2 1.6 copy-start
  8.8 1.2 copy-start.2
  10.0 1.8 %copy-start.8 = (bf16[1,48,1536]{2,1,0:T(8,128)(2,1)S(1)}, bf16[1,48,1536]{2,1,0:T(8,128)(2,1)}, u32[]{:S(2)}) copy-start(bf16[1,48,1536]{2,1,0:T(8,128)(2,1)} %param.5) | copy-start | bytes 442372
  11.1 0.7 copy-start.6
  11.8 90.9 %copy-start.7 = (s32[1,12]{1,0:T(1,128)S(1)}, s32[1,12]{1,0:T(1,128)}, u32[]{:S(2)}) copy-start(s32[1,12]{1,0:T(1,128)} %param.6) | copy-start | bytes 148
  11.8 106.2 %copy-start.1 = (f32[1,128,4096]{2,1,0:T(8,128)S(1)}, f32[1,128,4096]{2,1,0:T(8,128)}, u32[]{:S(2)}) copy-start(f32[1,128,4096]{2,1,0:T(8,128)} %front_ref.5) | copy-start | bytes 6291460
  11.8 106.2 %copy-start.3 = (bf16[1,2,512,512]{3,2,1,0:T(8,128)(2,1)S(1)}, bf16[1,2,512,512]{3,2,1,0:T(8,128)(2,1)}, u32[]{:S(2)}) copy-start(bf16[1,2,512,512]{3,2,1,0:T(8,128)(2,1)} %inverse_ref.3) | copy-start | bytes 3145732
  11.8 144.8 %all-gather.9.cloned.1.call-start = ((), (), s32[]{:S(2)}) async-start(), calls=%async_computation.2 | async-start | bytes 3981312 | tf_op jit(solution)/shard_map/all_gather | solution.py:258
  11.9 12.3 %collective-permute-start.2 = (bf16[48,1536]{1,0:T(8,128)(2,1)S(1)}, bf16[48,1536]{1,0:T(8,128)(2,1)S(1)}, u32[]{:S(2)}, u32[]{:S(2)}) collective-permute-start(bf16[48,1536]{1,0:T(8,128)(2,1)S(1)} %bitcast.19), channel_id=1, source_target_pairs={{0,48},{8,56},{32,16},{40,24},{64,112},{72,120},{96,80},{104,88},{... | collective-permute-start | bytes 442376 | tf_op jit(solution)/shard_map/ppermute | solution.py:234
  13.4 15.2 %collective-permute-start.1 = (bf16[48,1536]{1,0:T(8,128)(2,1)S(1)}, bf16[48,1536]{1,0:T(8,128)(2,1)S(1)}, u32[]{:S(2)}, u32[]{:S(2)}) collective-permute-start(bf16[48,1536]{1,0:T(8,128)(2,1)S(1)} %bitcast.20), channel_id=1, source_target_pairs={{8,48},{16,56},{40,16},{48,24},{72,112},{80,120},{104,80},{112,88}... | collective-permute-start | bytes 442376 | tf_op jit(solution)/shard_map/ppermute | solution.py:234
  14.7 13.9 %collective-permute-start = (bf16[48,1536]{1,0:T(8,128)(2,1)S(1)}, bf16[48,1536]{1,0:T(8,128)(2,1)S(1)}, u32[]{:S(2)}, u32[]{:S(2)}) collective-permute-start(bf16[48,1536]{1,0:T(8,128)(2,1)S(1)} %bitcast.21), channel_id=1, source_target_pairs={{16,48},{24,56},{48,16},{56,24},{80,112},{88,120},{112,80},{120,88... | collective-permute-start | bytes 442376 | tf_op jit(solution)/shard_map/ppermute | solution.py:234
  76.5 0.8 copy-start.4
  77.3 12.7 %collective-permute-start.3 = (bf16[128,512]{1,0:T(8,128)(2,1)S(1)}, bf16[128,512]{1,0:T(8,128)(2,1)S(1)}, u32[]{:S(2)}, u32[]{:S(2)}) collective-permute-start(bf16[128,512]{1,0:T(8,128)(2,1)S(1)} %slice.5), channel_id=1, source_target_pairs={{4,1},{5,0},{6,3},{7,2},{12,9},{13,8},{14,11},{15,10},{20,17},{21,... | collective-permute-start | bytes 393224 | tf_op jit(solution)/shard_map/ppermute | solution.py:247
  90.9 9.8 %collective-permute-start.4 = (bf16[128,512]{1,0:T(8,128)(2,1)S(1)}, bf16[128,512]{1,0:T(8,128)(2,1)S(1)}, u32[]{:S(2)}, u32[]{:S(2)}) collective-permute-start(bf16[128,512]{1,0:T(8,128)(2,1)S(1)} %broadcast_select_fusion.mine_ref), channel_id=1, source_target_pairs={{0,1},{1,0},{2,3},{3,2},{4,5},{5,4},{6,7},{7,6},{8,9},{9,8},{10,11... | collective-permute-start | bytes 393224 | tf_op jit(solution)/shard_map/ppermute | solution.py:249
  100.7 17.2 %collective-permute-start.5 = (bf16[256,512]{1,0:T(8,128)(2,1)S(1)}, bf16[256,512]{1,0:T(8,128)(2,1)S(1)}, u32[]{:S(2)}, u32[]{:S(2)}) collective-permute-start(bf16[256,512]{1,0:T(8,128)(2,1)S(1)} %pad_maximum_fusion.1), channel_id=1, source_target_pairs={{0,7},{1,2},{2,1},{3,4},{4,3},{5,6},{6,5},{7,0},{8,15},{9,10},{10,... | collective-permute-start | bytes 786440 | tf_op jit(solution)/shard_map/ppermute | solution.py:250
  117.9 1.0 copy-start.5
Sparse Core Ops, SparseCore 0:
  11.9 48.6 all-gather.6
  62.7 59.3 all-gather.8

commit v2 on v1

v2 whole, which is shorter than its diff:
```python
import jax
import jax.numpy as jnp
from jax import lax
from jax.experimental import pallas as pl
from jax.experimental.pallas import tpu as pltpu
from jax.sharding import PartitionSpec as P

WIDTH = 512
ROWS = 128
GROUP = 1024
CHILD = 1536
CHILD_BLOCKS = 12
CHILD_ROWS = 48
PART_ROWS = ROWS + 3 * CHILD_ROWS
VMEM_LIMIT = 60 * 1024 * 1024

F32 = jnp.float32
BF16 = jnp.bfloat16


def dot(a, b):
    return jnp.dot(a, b, preferred_element_type=F32)


def dot_t(a, b):
    return lax.dot_general(a, b, (((1,), (1,)), ((), ())), preferred_element_type=F32)


def dot_split(a, b, terms):
    total = None
    for _ in range(terms):
        part = a.astype(BF16)
        a = a - part.astype(F32)
        product = dot(part, b)
        total = product if total is None else total + product
    return total


def first_kernel(front_ref, inverse_ref, child_ref, both_ref, first_ref, parts_ref):
    first = dot_split(front_ref[0, :, :WIDTH], inverse_ref[0, 0], 3).astype(BF16)
    following = front_ref[0, :, WIDTH:].astype(BF16)
    both_ref[:, :WIDTH] = first
    both_ref[:, WIDTH:] = following
    first_ref[...] = first
    for k in range(4):
        parts_ref[k, :ROWS] = following
        for part in range(3):
            start = ROWS + part * CHILD_ROWS
            parts_ref[k, start : start + CHILD_ROWS] = child_ref[:, part * WIDTH : (part + 1) * WIDTH]


def first_panel(assembled, inverses, child):
    return pl.pallas_call(
        first_kernel,
        grid=(1,),
        in_specs=[
            pl.BlockSpec((1, ROWS, 2 * WIDTH), lambda i: (0, 0, 0)),
            pl.BlockSpec((1, 1, WIDTH, WIDTH), lambda i: (0, 0, 0, 0)),
            pl.BlockSpec((CHILD_ROWS, CHILD), lambda i: (0, 0)),
        ],
        out_specs=[
            pl.BlockSpec((ROWS, 2 * WIDTH), lambda i: (0, 0)),
            pl.BlockSpec((ROWS, WIDTH), lambda i: (0, 0)),
            pl.BlockSpec((4, PART_ROWS, WIDTH), lambda i: (0, 0, 0)),
        ],
        out_shape=[
            jax.ShapeDtypeStruct((ROWS, 2 * WIDTH), BF16),
            jax.ShapeDtypeStruct((ROWS, WIDTH), BF16),
            jax.ShapeDtypeStruct((4, PART_ROWS, WIDTH), BF16),
        ],
        compiler_params=pltpu.CompilerParams(vmem_limit_bytes=VMEM_LIMIT),
        name="first_panel",
    )(assembled, inverses, child)


def piece_of(z):
    return jnp.where(z < 4, z ^ 1, z - 4)


def product_kernel(
    where_ref, front_ref, inverse_ref, first_ref, firsts_ref, nexts_ref, column_ref, mine_ref, beside_ref, across_ref,
    zero_ref, one_ref, two_ref, three_ref, factor_ref, second_ref, weight_ref, rows_ref, columns_ref, held_ref, sem,
):
    copy = pltpu.make_async_copy(column_ref, held_ref, sem)
    copy.start()
    r, z = where_ref[0], where_ref[1]
    other = jnp.where(z % 2 == 1, (z + 1) % 8, (z + 7) % 8)
    here, there = piece_of(z), piece_of(other)

    def put(piece, value):
        second_ref[pl.ds(pl.multiple_of(piece * ROWS, ROWS), ROWS), :] = value

    put(here, mine_ref[...])
    put(here ^ 1, beside_ref[...])
    put(there, across_ref[:ROWS])
    put(there ^ 1, across_ref[ROWS:])
    inverse = inverse_ref[0, 0]

    turned = lax.dot_general(
        second_ref[...], inverse, (((0,), (0,)), ((), ())), preferred_element_type=F32
    )
    high = turned.astype(BF16)
    weight_ref[0] = high
    weight_ref[1] = (turned - high.astype(F32)).astype(BF16)

    def panel_of(first, following):
        lost = dot(first, weight_ref[0]) + dot(first, weight_ref[1])
        return dot(following, inverse) - lost

    own = front_ref[0] - dot_t(first_ref[...], second_ref[...])
    own = dot_split(own, inverse, 3)
    own = jnp.where((r == 0) & (z < 4), jnp.zeros_like(own), own)
    factor_ref[0, :, :WIDTH] = first_ref[...]
    factor_ref[0, :, WIDTH:] = own.astype(BF16)

    first = firsts_ref[...].reshape(4 * ROWS, WIDTH)
    panel = panel_of(first, nexts_ref[...].reshape(4 * ROWS, WIDTH))
    above = lax.broadcasted_iota(jnp.int32, (4 * ROWS, WIDTH), 0) < jnp.where(z < 4, ROWS, 0)
    panel = jnp.where(above, jnp.zeros_like(panel), panel).astype(BF16)
    for k in range(4):
        place = pl.ds(pl.multiple_of(((k - r + 4) % 4) * ROWS, ROWS), ROWS)
        rows_ref[place, :WIDTH] = first[k * ROWS : (k + 1) * ROWS]
        rows_ref[place, WIDTH:] = panel[k * ROWS : (k + 1) * ROWS]
    copy.wait()
    for half in range(2):
        place = pl.ds(half * 4 * ROWS, 4 * ROWS)
        first = held_ref[4 * half : 4 * half + 4].reshape(4 * ROWS, 2 * WIDTH)
        columns_ref[place, :WIDTH] = first[:, :WIDTH]
        columns_ref[place, WIDTH:] = panel_of(first[:, :WIDTH], first[:, WIDTH:]).astype(BF16)
    for part in range(4):
        place = pl.ds(part * 256, 256)
        total = dot_t(rows_ref[...], columns_ref[place, :]).astype(BF16)
        for k, ref in enumerate((zero_ref, one_ref, two_ref, three_ref)):
            ref[:, place] = total[k * ROWS : (k + 1) * ROWS]


def products(where, assembled, inverses, first, firsts, nexts, columns, mine, beside, across):
    whole = lambda *shape: pl.BlockSpec(shape, lambda i, w: (0,) * len(shape))
    return pl.pallas_call(
        product_kernel,
        grid_spec=pltpu.PrefetchScalarGridSpec(
            num_scalar_prefetch=1,
            grid=(1,),
            in_specs=[
                pl.BlockSpec((1, ROWS, WIDTH), lambda i, w: (0, 0, 1)),
                pl.BlockSpec((1, 1, WIDTH, WIDTH), lambda i, w: (0, 1, 0, 0)),
                whole(ROWS, WIDTH),
                whole(4, ROWS, WIDTH),
                whole(4, ROWS, WIDTH),
                pl.BlockSpec(memory_space=pl.ANY),
                whole(ROWS, WIDTH),
                whole(ROWS, WIDTH),
                whole(2 * ROWS, WIDTH),
            ],
            out_specs=[whole(ROWS, GROUP)] * 4 + [whole(1, ROWS, 2 * WIDTH)],
            scratch_shapes=[
                pltpu.VMEM((WIDTH, WIDTH), BF16),
                pltpu.VMEM((2, WIDTH, WIDTH), BF16),
                pltpu.VMEM((4 * ROWS, 2 * WIDTH), BF16),
                pltpu.VMEM((8 * ROWS, 2 * WIDTH), BF16),
                pltpu.VMEM((8, ROWS, 2 * WIDTH), BF16),
                pltpu.SemaphoreType.DMA,
            ],
        ),
        out_shape=[jax.ShapeDtypeStruct((ROWS, GROUP), BF16)] * 4
        + [jax.ShapeDtypeStruct((1, ROWS, 2 * WIDTH), BF16)],
        compiler_params=pltpu.CompilerParams(vmem_limit_bytes=VMEM_LIMIT),
        name="products",
    )(where, assembled, inverses, first, firsts, nexts, columns, mine, beside, across)


PIECES = (
    ((0, 0, 48, 0), (1, 0, 48, 48), (2, 0, 32, 96)),
    ((2, 32, 16, 0), (3, 0, 48, 16), (4, 0, 48, 64), (5, 0, 16, 112)),
    ((5, 16, 32, 0), (6, 0, 48, 32), (7, 0, 48, 80)),
)


def final_kernel(
    where_ref, front_ref, zero_ref, one_ref, two_ref, three_ref, child_ref, schur_ref, block_ref, sems
):
    step = pl.program_id(0)
    r, z = where_ref[0], where_ref[1]
    target = r * 8 + z
    found, child = jnp.int32(0), jnp.int32(0)
    for b in range(CHILD_BLOCKS):
        hit = (where_ref[2 + b] == target).astype(jnp.int32)
        found, child = found + hit, child + hit * b
    turn = child % 3

    def copies(j):
        return [
            pltpu.make_async_copy(
                child_ref.at[z_from, pl.ds(start, rows), :],
                block_ref.at[pl.ds(place, rows), :],
                sems.at[i],
            )
            for i, (z_from, start, rows, place) in enumerate(PIECES[j])
        ]

    for j in range(3):
        @pl.when((step == 0) & (found > 0) & (turn == j))
        def _():
            for copy in copies(j):
                copy.start()

    for k, ref in enumerate((zero_ref, one_ref, two_ref, three_ref)):
        @pl.when((r - step + 3) % 4 == k)
        def _():
            schur_ref[0] = front_ref[0] - ref[...].astype(F32)

    for j in range(3):
        @pl.when((step == 1) & (found > 0) & (turn == j))
        def _():
            for copy in copies(j):
                copy.wait()

    for b in range(CHILD_BLOCKS):
        parent = where_ref[2 + b]
        @pl.when((found > 0) & (step > 0) & (parent // 8 == step + 1))
        def _():
            place = pl.ds(pl.multiple_of((parent % 8) * ROWS, ROWS), ROWS)
            schur_ref[0, :, place] += block_ref[:, b * ROWS : (b + 1) * ROWS].astype(F32)


def final(where, assembled, pieces, children):
    return pl.pallas_call(
        final_kernel,
        grid_spec=pltpu.PrefetchScalarGridSpec(
            num_scalar_prefetch=1,
            grid=(3,),
            in_specs=[pl.BlockSpec((1, ROWS, GROUP), lambda i, w: (0, 0, i + 1))]
            + [pl.BlockSpec((ROWS, GROUP), lambda i, w: (0, 0))] * 4
            + [pl.BlockSpec(memory_space=pl.ANY)],
            out_specs=pl.BlockSpec((1, ROWS, GROUP), lambda i, w: (0, 0, i)),
            scratch_shapes=[
                pltpu.VMEM((ROWS, CHILD), BF16),
                pltpu.SemaphoreType.DMA((4,)),
            ],
        ),
        out_shape=jax.ShapeDtypeStruct((1, ROWS, 3 * GROUP), F32),
        compiler_params=pltpu.CompilerParams(vmem_limit_bytes=VMEM_LIMIT),
        name="final",
    )(where, assembled, *pieces, children)


def wanted_kernel(where_ref, parts_ref, out_ref):
    r = where_ref[0]
    for z in range(8):
        child = jnp.int32(0)
        for b in range(CHILD_BLOCKS):
            child = child + jnp.where(where_ref[2 + b] == r * 8 + z, b, 0)
        for part in range(3):
            start = ROWS + part * CHILD_ROWS
            piece = parts_ref[child // 3, start : start + CHILD_ROWS]
            out_ref[z, :, part * WIDTH : (part + 1) * WIDTH] = piece


def wanted(where, parts):
    whole = lambda *shape: pl.BlockSpec(shape, lambda i, w: (0,) * len(shape))
    return pl.pallas_call(
        wanted_kernel,
        grid_spec=pltpu.PrefetchScalarGridSpec(
            num_scalar_prefetch=1,
            grid=(1,),
            in_specs=[whole(4, PART_ROWS, WIDTH)],
            out_specs=whole(8, CHILD_ROWS, CHILD),
        ),
        out_shape=jax.ShapeDtypeStruct((8, CHILD_ROWS, CHILD), BF16),
        compiler_params=pltpu.CompilerParams(vmem_limit_bytes=VMEM_LIMIT),
        name="wanted",
    )(where, parts)


def on_device(assembled, update, blocks, inverses):
    r, z = lax.axis_index("row"), lax.axis_index("col")
    where = jnp.concatenate([jnp.stack([r, z]).astype(jnp.int32), blocks[0]])

    child = lax.ppermute(update[0], "front", [(i, i ^ 1) for i in range(16)])
    both, first, parts = first_panel(assembled, inverses, child)
    columns = lax.all_gather(both, "col", axis=0)
    firsts = lax.all_gather(first, "row", axis=0)

    top = firsts[0]
    parts, top = lax.optimization_barrier((parts, top))
    parts = lax.all_to_all(parts, "row", 0, 0)
    passed = lax.ppermute(top, "col", [(4, 1), (5, 0), (6, 3), (7, 2)])
    mine = jnp.where(z < 4, passed, top)
    beside = lax.ppermute(mine, "col", [(i, i ^ 1) for i in range(8)])
    across = lax.ppermute(
        jnp.concatenate([mine, beside]),
        "col",
        [(i, (i + 1) % 8 if i % 2 else (i + 7) % 8) for i in range(8)],
    )
    pieces = wanted(where, parts)
    across, pieces = lax.optimization_barrier((across, pieces))
    children = lax.all_to_all(pieces, "col", 0, 0)

    *pieces, factor = products(
        where, assembled, inverses, first, firsts, parts, columns, mine, beside, across
    )
    for s in range(1, 4):
        pairs = [(i, (i + s) % 4) for i in range(1, 4)]
        pieces[s] = lax.ppermute(pieces[s], "row", pairs)
    return factor, final(where, assembled, pieces, children)


def solution(mesh):
    return jax.shard_map(
        on_device,
        mesh=mesh,
        in_specs=(
            P("front", ("row", "col"), None),
            P("front", ("row", "col"), None),
            P("front", None),
            P("front", None, None, None),
        ),
        out_specs=(P("front", ("row", "col"), None), P("front", ("row", "col"), None)),
        check_vma=False,
    )
```

time: 167 us -> 132 us (0.79)
  the two profiles are of different devices: /device:TPU:60 before, /device:TPU:1 now
where the time goes in v2:
time: 132 us; the launch traced here: 130 us
  waiting for transfers between devices  44.2 us (33%)
  starting transfers between devices  34.5 us (26%)
  Pallas kernels  19.7 us (15%)
  between operations  14.2 us (11%)
  blocking collectives  13.6 us (10%)
  local copies, waits for them, and re-layouts  3.19 us (2%)
    all_to_all x1, waiting for transfers between devices, on_device(): children = lax.all_to_all(pieces, 'col', 0, 0)  18.7 us
    all_gather x1, blocking collectives, on_device(): firsts = lax.all_gather(first, 'row', axis=0)  13.6 us
    ppermute x1, waiting for transfers between devices, on_device(): passed = lax.ppermute(top, 'col', [(4, 1), (5, 0), (6, 3), (7, 2)])  10.4 us
    all_to_all x1, starting transfers between devices, on_device(): children = lax.all_to_all(pieces, 'col', 0, 0)  9.37 us
    pallas_call x1, Pallas kernels, products(): pl.pallas_call(product_kernel, grid_spec=pltpu.PrefetchScalarGridSpec(num...  9.33 us
    ppermute x1, starting transfers between devices, on_device(): child = lax.ppermute(update[0], 'front', [(i, i ^ 1) for i in range(16)])  8.79 us
    ppermute x3, waiting for transfers between devices, on_device(): pieces[s] = lax.ppermute(pieces[s], 'row', pairs)  7.51 us
    ppermute x1, waiting for transfers between devices, on_device(): beside = lax.ppermute(mine, 'col', [(i, i ^ 1) for i in range(8)])  4.69 us
  transfers between devices with their start and end apart: 10, of which 7 were waited for; matrix products, arithmetic and copies ran while one was open for 0% of the time, Pallas kernels for 10%

profile of v2, /device:TPU:1, one launch (start us, length us, event | category | flops | bytes accessed | tf_op | source)
XLA Modules:
  0.0 130.1 jit_solution(6952431939196423638)
XLA Ops:
  7.2 0.0 all-gather.4.cloned.1.call-start
  7.2 8.8 %collective-permute-start = (bf16[48,1536]{1,0:T(8,128)(2,1)}, bf16[48,1536]{1,0:T(8,128)(2,1)S(1)}, u32[]{:S(2)}, u32[]{:S(2)}) collective-permute-start(bf16[48,1536]{1,0:T(8,128)(2,1)} %bitcast.9), channel_id=1, source_target_pairs={{0,32},{32,0},{64,96},{96,64},{128,160},{160,128},{192,224},{224,1... | collective-permute-start | bytes 442376 | tf_op jit(solution)/shard_map/ppermute | solution.py:279
  16.0 1.2 collective-permute-done.child_ref
  17.2 0.7 copy-done.9
  17.9 2.7 %first_panel.1 = (bf16[128,1024]{1,0:T(8,128)(2,1)}, bf16[128,512]{1,0:T(8,128)(2,1)}, bf16[4,272,512]{2,1,0:T(8,128)(2,1)}) custom-call(f32[1,128,4096]{2,1,0:T(8,128)} %front_ref.5, bf16[1,2,512,512]{3,2,1,0:T(8,128)(2,1)} %inverse_ref.3, bf16[48,1536]{1,0:T(8,128)(2,1)} %copy-done.9), custom_call_target="tpu_custom_call" | custom-call | tf_op jit(solution)/shard_map/first_panel/pallas_call | solution.py:53
  20.6 0.0 all-gather.4.cloned.1.call-update
  20.6 13.6 %all-gather = bf16[512,512]{1,0:T(8,128)(2,1)S(1)} all-gather(bf16[128,512]{1,0:T(8,128)(2,1)} %get-tuple-element.14.first_ref), channel_id=2, replica_groups=mesh['front'=16,'row'=4,'col'=8] {'row'}, dimensions={0}, use_global_device_ids=true | all-gather | bytes 655360 | tf_op jit(solution)/shard_map/all_gather | solution.py:282
  34.2 0.0 copy-start.2
  34.2 0.0 copy-start.10
  34.2 0.8 copy-done.2
  35.0 4.0 %all-to-all-start = ((bf16[4,272,512]{2,1,0:T(8,128)(2,1)}), bf16[4,272,512]{2,1,0:T(8,128)(2,1)S(1)}, u32[]{:S(2)}, u32[]{:S(2)}) async-start(bf16[4,272,512]{2,1,0:T(8,128)(2,1)} %get-tuple-element.16), calls=%async_computation | async-start | bytes 2228224 | tf_op jit(solution)/shard_map/all_to_all | solution.py:286
  39.0 1.3 collective-permute-start.1
  40.3 10.4 %collective-permute-done.1 = bf16[128,512]{1,0:T(8,128)(2,1)S(1)} collective-permute-done((bf16[128,512]{1,0:T(8,128)(2,1)S(1)}, bf16[128,512]{1,0:T(8,128)(2,1)S(1)}, u32[]{:S(2)}, u32[]{:S(2)}) %collective-permute-start.1) | collective-permute-done | bytes 131104 | tf_op jit(solution)/shard_map/ppermute | solution.py:287
  50.7 0.0 copy-start.3
  50.7 2.7 %collective-permute-start.2 = (bf16[128,512]{1,0:T(8,128)(2,1)S(1)}, bf16[128,512]{1,0:T(8,128)(2,1)S(1)}, u32[]{:S(2)}, u32[]{:S(2)}) collective-permute-start(bf16[128,512]{1,0:T(8,128)(2,1)S(1)} %broadcast_select_fusion.mine_ref), channel_id=1, source_target_pairs={{0,1},{1,0},{2,3},{3,2},{4,5},{5,4},{6,7},{7,6},{8,9},{9,8},{10,11... | collective-permute-start | bytes 393224 | tf_op jit(solution)/shard_map/ppermute | solution.py:289
  53.4 4.7 %collective-permute-done.2.beside_ref = bf16[128,512]{1,0:T(8,128)(2,1)S(1)} collective-permute-done((bf16[128,512]{1,0:T(8,128)(2,1)S(1)}, bf16[128,512]{1,0:T(8,128)(2,1)S(1)}, u32[]{:S(2)}, u32[]{:S(2)}) %collective-permute-start.2) | collective-permute-done | bytes 131104 | tf_op jit(solution)/shard_map/ppermute | solution.py:289
  58.1 0.0 copy-start.4
  58.1 4.5 %collective-permute-start.3 = (bf16[256,512]{1,0:T(8,128)(2,1)S(1)}, bf16[256,512]{1,0:T(8,128)(2,1)S(1)}, u32[]{:S(2)}, u32[]{:S(2)}) collective-permute-start(bf16[256,512]{1,0:T(8,128)(2,1)S(1)} %pad_maximum_fusion), channel_id=1, source_target_pairs={{0,7},{1,2},{2,1},{3,4},{4,3},{5,6},{6,5},{7,0},{8,15},{9,10},{10,... | collective-permute-start | bytes 786440 | tf_op jit(solution)/shard_map/ppermute | solution.py:290
  62.7 0.0 copy-done.10
  62.7 0.6 pad_add_fusion.where_ref
  63.2 1.6 %all-to-all-done.parts_ref.nexts_ref = bf16[4,272,512]{2,1,0:T(8,128)(2,1)S(1)} async-done(((bf16[4,272,512]{2,1,0:T(8,128)(2,1)}), bf16[4,272,512]{2,1,0:T(8,128)(2,1)S(1)}, u32[]{:S(2)}, u32[]{:S(2)}) %all-to-all-start) | async-done | bytes 1114144 | tf_op jit(solution)/shard_map/all_to_all | solution.py:286
  64.9 0.0 copy-start
  64.9 1.0 copy-done
  65.9 3.0 %wanted.1 = bf16[8,48,1536]{2,1,0:T(8,128)(2,1)} custom-call(s32[14]{0:T(128)} %pad_add_fusion.where_ref, bf16[4,272,512]{2,1,0:T(8,128)(2,1)} %copy-done), custom_call_target="tpu_custom_call" | custom-call | tf_op jit(solution)/shard_map/wanted/pallas_call | solution.py:261
  68.9 0.0 copy-done.3
  68.9 0.0 copy-done.4
  68.9 0.0 collective-permute-done.3.across_ref
  68.9 0.0 copy-start.8
  69.0 9.4 %all-to-all-start.1 = ((bf16[8,48,1536]{2,1,0:T(8,128)(2,1)}), bf16[8,48,1536]{2,1,0:T(8,128)(2,1)S(1)}, u32[]{:S(2)}, u32[]{:S(2)}) async-start(bf16[8,48,1536]{2,1,0:T(8,128)(2,1)} %wanted.1), calls=%async_computation.1 | async-start | bytes 2359296 | tf_op jit(solution)/shard_map/all_to_all | solution.py:297
  78.3 0.0 all-gather.4.cloned.1.call-done
  78.3 0.0 copy-done.8
  78.4 9.3 %products.1 = (bf16[128,1024]{1,0:T(8,128)(2,1)}, bf16[128,1024]{1,0:T(8,128)(2,1)}, bf16[128,1024]{1,0:T(8,128)(2,1)}, bf16[128,1024]{1,0:T(8,128)(2,1)}, bf16[1,128,1024]{2,1,0:T(8,128)(2,1)}) custom-call(s32[14]{0:T(128)} %pad_add_fusion.where_ref, f32[1,128,4096]{2,1,0:T(8,128)} %front_ref.5, bf16[1,2,512,512]{3,2,1,0:T(8,128)(2,1)} %inverse_ref.3, ...), custom_call_target="tpu_custom_call" | custom-call | tf_op jit(solution)/shard_map/products/pallas_call | solution.py:139
  87.7 1.3 collective-permute-start.4
  89.0 1.3 collective-permute-start.5
  90.3 1.3 collective-permute-start.6
  91.6 18.7 %all-to-all-done.1.child_ref = bf16[8,48,1536]{2,1,0:T(8,128)(2,1)S(1)} async-done(((bf16[8,48,1536]{2,1,0:T(8,128)(2,1)}), bf16[8,48,1536]{2,1,0:T(8,128)(2,1)S(1)}, u32[]{:S(2)}, u32[]{:S(2)}) %all-to-all-start.1) | async-done | bytes 1179680 | tf_op jit(solution)/shard_map/all_to_all | solution.py:297
  110.3 0.0 copy-start.1
  110.3 0.0 collective-permute-done.4.one_ref
  110.3 0.0 copy-start.5
  110.3 4.4 %collective-permute-done.5.two_ref = bf16[128,1024]{1,0:T(8,128)(2,1)S(1)} collective-permute-done((bf16[128,1024]{1,0:T(8,128)(2,1)}, bf16[128,1024]{1,0:T(8,128)(2,1)S(1)}, u32[]{:S(2)}, u32[]{:S(2)}) %collective-permute-start.5) | collective-permute-done | bytes 262176 | tf_op jit(solution)/shard_map/ppermute | solution.py:304
  114.8 0.0 copy-start.6
  114.8 3.1 %collective-permute-done.6.three_ref = bf16[128,1024]{1,0:T(8,128)(2,1)S(1)} collective-permute-done((bf16[128,1024]{1,0:T(8,128)(2,1)}, bf16[128,1024]{1,0:T(8,128)(2,1)S(1)}, u32[]{:S(2)}, u32[]{:S(2)}) %collective-permute-start.6) | collective-permute-done | bytes 262176 | tf_op jit(solution)/shard_map/ppermute | solution.py:304
  117.8 0.0 copy-start.7
  117.8 0.0 copy-done.1
  117.8 0.0 copy-done.5
  117.8 0.0 copy-done.6
  117.9 0.7 copy-done.7
  118.6 4.6 %final.1 = f32[1,128,3072]{2,1,0:T(8,128)} custom-call(s32[14]{0:T(128)} %pad_add_fusion.where_ref, f32[1,128,4096]{2,1,0:T(8,128)} %front_ref.5, bf16[128,1024]{1,0:T(8,128)(2,1)} %get-tuple-element.21.zero_ref, bf16[128,1024]{1,0:T(8,128)(2,1)} %copy-done.5, bf16[128,1024]{1,0:T(8,128)(2,1)} %copy-done.6, bf16[128,1024]{1,0:T(8,128)(2,1)} %copy-done.7, ...), custom_call_target="tpu_custom_call" | custom-call | tf_op jit(solution)/shard_map/final/pallas_call | solution.py:227
  (4 shorter events, 0.0 us)
Async XLA Ops:
  7.2 71.2 %all-gather.4.cloned.1.call-start = ((), (), s32[]{:S(2)}) async-start(), calls=%async_computation.2 | async-start | bytes 2359296 | tf_op jit(solution)/shard_map/all_gather | solution.py:281
  7.2 10.0 %collective-permute-start = (bf16[48,1536]{1,0:T(8,128)(2,1)}, bf16[48,1536]{1,0:T(8,128)(2,1)S(1)}, u32[]{:S(2)}, u32[]{:S(2)}) collective-permute-start(bf16[48,1536]{1,0:T(8,128)(2,1)} %bitcast.9), channel_id=1, source_target_pairs={{0,32},{32,0},{64,96},{96,64},{128,160},{160,128},{192,224},{224,1... | collective-permute-start | bytes 442376 | tf_op jit(solution)/shard_map/ppermute | solution.py:279
  17.2 0.7 copy-start.9
  34.2 0.8 copy-start.2
  34.2 28.4 %copy-start.10 = (s32[1,12]{1,0:T(1,128)S(1)}, s32[1,12]{1,0:T(1,128)}, u32[]{:S(2)}) copy-start(s32[1,12]{1,0:T(1,128)} %param.6) | copy-start | bytes 148
  35.0 29.9 %all-to-all-start = ((bf16[4,272,512]{2,1,0:T(8,128)(2,1)}), bf16[4,272,512]{2,1,0:T(8,128)(2,1)S(1)}, u32[]{:S(2)}, u32[]{:S(2)}) async-start(bf16[4,272,512]{2,1,0:T(8,128)(2,1)} %get-tuple-element.16), calls=%async_computation | async-start | bytes 2228224 | tf_op jit(solution)/shard_map/all_to_all | solution.py:286
  39.0 11.7 %collective-permute-start.1 = (bf16[128,512]{1,0:T(8,128)(2,1)S(1)}, bf16[128,512]{1,0:T(8,128)(2,1)S(1)}, u32[]{:S(2)}, u32[]{:S(2)}) collective-permute-start(bf16[128,512]{1,0:T(8,128)(2,1)S(1)} %slice.5), channel_id=1, source_target_pairs={{4,1},{5,0},{6,3},{7,2},{12,9},{13,8},{14,11},{15,10},{20,17},{21,... | collective-permute-start | bytes 393224 | tf_op jit(solution)/shard_map/ppermute | solution.py:287
  50.7 18.3 %copy-start.3 = (bf16[128,512]{1,0:T(8,128)(2,1)}, bf16[128,512]{1,0:T(8,128)(2,1)S(1)}, u32[]{:S(2)}) copy-start(bf16[128,512]{1,0:T(8,128)(2,1)S(1)} %broadcast_select_fusion.mine_ref) | copy-start | bytes 393220
  50.7 7.4 %collective-permute-start.2 = (bf16[128,512]{1,0:T(8,128)(2,1)S(1)}, bf16[128,512]{1,0:T(8,128)(2,1)S(1)}, u32[]{:S(2)}, u32[]{:S(2)}) collective-permute-start(bf16[128,512]{1,0:T(8,128)(2,1)S(1)} %broadcast_select_fusion.mine_ref), channel_id=1, source_target_pairs={{0,1},{1,0},{2,3},{3,2},{4,5},{5,4},{6,7},{7,6},{8,9},{9,8},{10,11... | collective-permute-start | bytes 393224 | tf_op jit(solution)/shard_map/ppermute | solution.py:289
  58.1 10.9 %copy-start.4 = (bf16[128,512]{1,0:T(8,128)(2,1)}, bf16[128,512]{1,0:T(8,128)(2,1)S(1)}, u32[]{:S(2)}) copy-start(bf16[128,512]{1,0:T(8,128)(2,1)S(1)} %collective-permute-done.2.beside_ref) | copy-start | bytes 393220
  58.1 10.8 %collective-permute-start.3 = (bf16[256,512]{1,0:T(8,128)(2,1)S(1)}, bf16[256,512]{1,0:T(8,128)(2,1)S(1)}, u32[]{:S(2)}, u32[]{:S(2)}) collective-permute-start(bf16[256,512]{1,0:T(8,128)(2,1)S(1)} %pad_maximum_fusion), channel_id=1, source_target_pairs={{0,7},{1,2},{2,1},{3,4},{4,3},{5,6},{6,5},{7,0},{8,15},{9,10},{10,... | collective-permute-start | bytes 786440 | tf_op jit(solution)/shard_map/ppermute | solution.py:290
  64.9 1.0 copy-start
  68.9 9.4 %copy-start.8 = (bf16[256,512]{1,0:T(8,128)(2,1)}, bf16[256,512]{1,0:T(8,128)(2,1)S(1)}, u32[]{:S(2)}) copy-start(bf16[256,512]{1,0:T(8,128)(2,1)S(1)} %collective-permute-done.3.across_ref) | copy-start | bytes 786436
  69.0 41.4 %all-to-all-start.1 = ((bf16[8,48,1536]{2,1,0:T(8,128)(2,1)}), bf16[8,48,1536]{2,1,0:T(8,128)(2,1)S(1)}, u32[]{:S(2)}, u32[]{:S(2)}) async-start(bf16[8,48,1536]{2,1,0:T(8,128)(2,1)} %wanted.1), calls=%async_computation.1 | async-start | bytes 2359296 | tf_op jit(solution)/shard_map/all_to_all | solution.py:297
  87.7 22.6 %collective-permute-start.4 = (bf16[128,1024]{1,0:T(8,128)(2,1)}, bf16[128,1024]{1,0:T(8,128)(2,1)S(1)}, u32[]{:S(2)}, u32[]{:S(2)}) collective-permute-start(bf16[128,1024]{1,0:T(8,128)(2,1)} %get-tuple-element.22), channel_id=1, source_target_pairs={{8,16},{16,24},{24,0},{9,17},{17,25},{25,1},{10,18},{18,26},{26,2}... | collective-permute-start | bytes 786440 | tf_op jit(solution)/shard_map/ppermute | solution.py:304
  89.0 25.8 %collective-permute-start.5 = (bf16[128,1024]{1,0:T(8,128)(2,1)}, bf16[128,1024]{1,0:T(8,128)(2,1)S(1)}, u32[]{:S(2)}, u32[]{:S(2)}) collective-permute-start(bf16[128,1024]{1,0:T(8,128)(2,1)} %get-tuple-element.23), channel_id=1, source_target_pairs={{8,24},{16,0},{24,8},{9,25},{17,1},{25,9},{10,26},{18,2},{26,10},{... | collective-permute-start | bytes 786440 | tf_op jit(solution)/shard_map/ppermute | solution.py:304
  90.3 27.5 %collective-permute-start.6 = (bf16[128,1024]{1,0:T(8,128)(2,1)}, bf16[128,1024]{1,0:T(8,128)(2,1)S(1)}, u32[]{:S(2)}, u32[]{:S(2)}) collective-permute-start(bf16[128,1024]{1,0:T(8,128)(2,1)} %get-tuple-element.24), channel_id=1, source_target_pairs={{8,0},{16,8},{24,16},{9,1},{17,9},{25,17},{10,2},{18,10},{26,18},{... | collective-permute-start | bytes 786440 | tf_op jit(solution)/shard_map/ppermute | solution.py:304
  110.3 7.5 %copy-start.1 = (bf16[8,48,1536]{2,1,0:T(8,128)(2,1)}, bf16[8,48,1536]{2,1,0:T(8,128)(2,1)S(1)}, u32[]{:S(2)}) copy-start(bf16[8,48,1536]{2,1,0:T(8,128)(2,1)S(1)} %all-to-all-done.1.child_ref) | copy-start | bytes 3538948
  110.3 7.5 %copy-start.5 = (bf16[128,1024]{1,0:T(8,128)(2,1)}, bf16[128,1024]{1,0:T(8,128)(2,1)S(1)}, u32[]{:S(2)}) copy-start(bf16[128,1024]{1,0:T(8,128)(2,1)S(1)} %collective-permute-done.4.one_ref) | copy-start | bytes 786436
  114.8 3.1 %copy-start.6 = (bf16[128,1024]{1,0:T(8,128)(2,1)}, bf16[128,1024]{1,0:T(8,128)(2,1)S(1)}, u32[]{:S(2)}) copy-start(bf16[128,1024]{1,0:T(8,128)(2,1)S(1)} %collective-permute-done.5.two_ref) | copy-start | bytes 786436
  117.8 0.7 copy-start.7
Sparse Core Ops, SparseCore 0:
  20.7 45.4 all-gather.3

commit v3 on v2

v3 whole, which is shorter than its diff:
```python
import jax
import jax.numpy as jnp
from jax import lax
from jax.experimental import pallas as pl
from jax.experimental.pallas import tpu as pltpu
from jax.sharding import PartitionSpec as P

WIDTH = 512
ROWS = 128
GROUP = 1024
CHILD = 1536
CHILD_BLOCKS = 12
CHILD_ROWS = 48
PART_ROWS = ROWS + 3 * CHILD_ROWS
VMEM_LIMIT = 60 * 1024 * 1024

F32 = jnp.float32
BF16 = jnp.bfloat16


def dot(a, b):
    return jnp.dot(a, b, preferred_element_type=F32)


def dot_t(a, b):
    return lax.dot_general(a, b, (((1,), (1,)), ((), ())), preferred_element_type=F32)


def dot_split(a, b, terms):
    total = None
    for _ in range(terms):
        part = a.astype(BF16)
        a = a - part.astype(F32)
        product = dot(part, b)
        total = product if total is None else total + product
    return total


def first_kernel(front_ref, inverse_ref, both_ref, first_ref):
    first = dot_split(front_ref[0, :, :WIDTH], inverse_ref[0, 0], 3).astype(BF16)
    both_ref[:, :WIDTH] = first
    both_ref[:, WIDTH:] = front_ref[0, :, WIDTH:].astype(BF16)
    first_ref[...] = first


def first_panel(assembled, inverses):
    return pl.pallas_call(
        first_kernel,
        grid=(1,),
        in_specs=[
            pl.BlockSpec((1, ROWS, 2 * WIDTH), lambda i: (0, 0, 0)),
            pl.BlockSpec((1, 1, WIDTH, WIDTH), lambda i: (0, 0, 0, 0)),
        ],
        out_specs=[
            pl.BlockSpec((ROWS, 2 * WIDTH), lambda i: (0, 0)),
            pl.BlockSpec((ROWS, WIDTH), lambda i: (0, 0)),
        ],
        out_shape=[
            jax.ShapeDtypeStruct((ROWS, 2 * WIDTH), BF16),
            jax.ShapeDtypeStruct((ROWS, WIDTH), BF16),
        ],
        compiler_params=pltpu.CompilerParams(vmem_limit_bytes=VMEM_LIMIT),
        name="first_panel",
    )(assembled, inverses)


def pack_kernel(both_ref, child_ref, parts_ref):
    for k in range(4):
        parts_ref[k, :ROWS] = both_ref[...]
        for part in range(3):
            start = ROWS + part * CHILD_ROWS
            parts_ref[k, start : start + CHILD_ROWS] = child_ref[:, part * WIDTH : (part + 1) * WIDTH]


def pack(both, child):
    return pl.pallas_call(
        pack_kernel,
        grid=(1,),
        in_specs=[
            pl.BlockSpec((ROWS, WIDTH), lambda i: (0, 1)),
            pl.BlockSpec((CHILD_ROWS, CHILD), lambda i: (0, 0)),
        ],
        out_specs=pl.BlockSpec((4, PART_ROWS, WIDTH), lambda i: (0, 0, 0)),
        out_shape=jax.ShapeDtypeStruct((4, PART_ROWS, WIDTH), BF16),
        compiler_params=pltpu.CompilerParams(vmem_limit_bytes=VMEM_LIMIT),
        name="pack",
    )(both, child)


def piece_of(z):
    return jnp.where(z < 4, z ^ 1, z - 4)


def put_second(z, second_ref, mine_ref, beside_ref, across_ref):
    here, there = piece_of(z), piece_of((z + 2 * (z % 2) + 7) % 8)
    pieces = (
        (here, mine_ref[...]),
        (here ^ 1, beside_ref[...]),
        (there, across_ref[:ROWS]),
        (there ^ 1, across_ref[ROWS:]),
    )
    for piece, value in pieces:
        second_ref[pl.ds(pl.multiple_of(piece * ROWS, ROWS), ROWS), :] = value


def factor_kernel(
    where_ref, front_ref, inverse_ref, first_ref, mine_ref, beside_ref, across_ref, factor_ref, second_ref
):
    r, z = where_ref[0], where_ref[1]
    put_second(z, second_ref, mine_ref, beside_ref, across_ref)
    own = front_ref[0] - dot_t(first_ref[...], second_ref[...])
    own = dot_split(own, inverse_ref[0, 0], 3)
    own = jnp.where((r == 0) & (z < 4), jnp.zeros_like(own), own)
    factor_ref[0, :, :WIDTH] = first_ref[...]
    factor_ref[0, :, WIDTH:] = own.astype(BF16)


def own_factor(where, assembled, inverses, first, relay):
    whole = lambda *shape: pl.BlockSpec(shape, lambda i, w: (0,) * len(shape))
    return pl.pallas_call(
        factor_kernel,
        grid_spec=pltpu.PrefetchScalarGridSpec(
            num_scalar_prefetch=1,
            grid=(1,),
            in_specs=[
                pl.BlockSpec((1, ROWS, WIDTH), lambda i, w: (0, 0, 1)),
                pl.BlockSpec((1, 1, WIDTH, WIDTH), lambda i, w: (0, 1, 0, 0)),
                whole(ROWS, WIDTH),
                whole(ROWS, WIDTH),
                whole(ROWS, WIDTH),
                whole(2 * ROWS, WIDTH),
            ],
            out_specs=whole(1, ROWS, 2 * WIDTH),
            scratch_shapes=[pltpu.VMEM((WIDTH, WIDTH), BF16)],
        ),
        out_shape=jax.ShapeDtypeStruct((1, ROWS, 2 * WIDTH), BF16),
        compiler_params=pltpu.CompilerParams(vmem_limit_bytes=VMEM_LIMIT),
        cost_estimate=pl.CostEstimate(flops=2**28, bytes_accessed=2**21, transcendentals=0),
        name="own_factor",
    )(where, assembled, inverses, first, *relay)


def product_kernel(
    where_ref, inverse_ref, firsts_ref, nexts_ref, column_ref, mine_ref, beside_ref, across_ref,
    zero_ref, one_ref, two_ref, three_ref, second_ref, weight_ref, rows_ref, columns_ref, held_ref, sem,
):
    copy = pltpu.make_async_copy(column_ref, held_ref, sem)
    copy.start()
    r, z = where_ref[0], where_ref[1]
    put_second(z, second_ref, mine_ref, beside_ref, across_ref)
    inverse = inverse_ref[0, 0]

    turned = lax.dot_general(
        second_ref[...], inverse, (((0,), (0,)), ((), ())), preferred_element_type=F32
    )
    high = turned.astype(BF16)
    weight_ref[0] = high
    weight_ref[1] = (turned - high.astype(F32)).astype(BF16)

    def panel_of(first, following):
        lost = dot(first, weight_ref[0]) + dot(first, weight_ref[1])
        return dot(following, inverse) - lost

    first = firsts_ref[...].reshape(4 * ROWS, WIDTH)
    panel = panel_of(first, nexts_ref[...].reshape(4 * ROWS, WIDTH))
    above = lax.broadcasted_iota(jnp.int32, (4 * ROWS, WIDTH), 0) < jnp.where(z < 4, ROWS, 0)
    panel = jnp.where(above, jnp.zeros_like(panel), panel).astype(BF16)
    for k in range(4):
        place = pl.ds(pl.multiple_of(((k - r + 4) % 4) * ROWS, ROWS), ROWS)
        rows_ref[place, :WIDTH] = first[k * ROWS : (k + 1) * ROWS]
        rows_ref[place, WIDTH:] = panel[k * ROWS : (k + 1) * ROWS]
    copy.wait()
    for half in range(2):
        place = pl.ds(half * 4 * ROWS, 4 * ROWS)
        first = held_ref[4 * half : 4 * half + 4].reshape(4 * ROWS, 2 * WIDTH)
        columns_ref[place, :WIDTH] = first[:, :WIDTH]
        columns_ref[place, WIDTH:] = panel_of(first[:, :WIDTH], first[:, WIDTH:]).astype(BF16)
    for part in range(4):
        place = pl.ds(part * 256, 256)
        total = dot_t(rows_ref[...], columns_ref[place, :]).astype(BF16)
        for k, ref in enumerate((zero_ref, one_ref, two_ref, three_ref)):
            ref[:, place] = total[k * ROWS : (k + 1) * ROWS]


def products(where, inverses, firsts, nexts, columns, relay):
    whole = lambda *shape: pl.BlockSpec(shape, lambda i, w: (0,) * len(shape))
    return pl.pallas_call(
        product_kernel,
        grid_spec=pltpu.PrefetchScalarGridSpec(
            num_scalar_prefetch=1,
            grid=(1,),
            in_specs=[
                pl.BlockSpec((1, 1, WIDTH, WIDTH), lambda i, w: (0, 1, 0, 0)),
                whole(4, ROWS, WIDTH),
                whole(4, ROWS, WIDTH),
                pl.BlockSpec(memory_space=pl.ANY),
                whole(ROWS, WIDTH),
                whole(ROWS, WIDTH),
                whole(2 * ROWS, WIDTH),
            ],
            out_specs=[whole(ROWS, GROUP)] * 4,
            scratch_shapes=[
                pltpu.VMEM((WIDTH, WIDTH), BF16),
                pltpu.VMEM((2, WIDTH, WIDTH), BF16),
                pltpu.VMEM((4 * ROWS, 2 * WIDTH), BF16),
                pltpu.VMEM((8 * ROWS, 2 * WIDTH), BF16),
                pltpu.VMEM((8, ROWS, 2 * WIDTH), BF16),
                pltpu.SemaphoreType.DMA,
            ],
        ),
        out_shape=[jax.ShapeDtypeStruct((ROWS, GROUP), BF16)] * 4,
        compiler_params=pltpu.CompilerParams(vmem_limit_bytes=VMEM_LIMIT),
        name="products",
    )(where, inverses, firsts, nexts, columns, *relay)


PIECES = (
    ((0, 0, 48, 0), (1, 0, 48, 48), (2, 0, 32, 96)),
    ((2, 32, 16, 0), (3, 0, 48, 16), (4, 0, 48, 64), (5, 0, 16, 112)),
    ((5, 16, 32, 0), (6, 0, 48, 32), (7, 0, 48, 80)),
)


def final_kernel(
    where_ref, front_ref, zero_ref, one_ref, two_ref, three_ref, child_ref, schur_ref,
    held_ref, product_ref, block_ref, read_sems, child_sems, write_sems,
):
    r, z = where_ref[0], where_ref[1]
    target = r * 8 + z
    found, child = jnp.int32(0), jnp.int32(0)
    for b in range(CHILD_BLOCKS):
        hit = (where_ref[2 + b] == target).astype(jnp.int32)
        found, child = found + hit, child + hit * b
    turn = child % 3

    def read_front(g):
        place = pl.ds((g + 1) * GROUP, GROUP)
        return pltpu.make_async_copy(front_ref.at[0, :, place], held_ref.at[g], read_sems.at[0, g])

    def read_product(g, ref):
        return pltpu.make_async_copy(ref, product_ref.at[g], read_sems.at[1, g])

    def write(g):
        place = pl.ds(g * GROUP, GROUP)
        return pltpu.make_async_copy(held_ref.at[g], schur_ref.at[0, :, place], write_sems.at[g])

    def read_child(j):
        return [
            pltpu.make_async_copy(
                child_ref.at[z_from, pl.ds(part * CHILD_ROWS + start, rows), :],
                block_ref.at[pl.ds(place, rows), pl.ds(part * WIDTH, WIDTH)],
                child_sems.at[i, part],
            )
            for i, (z_from, start, rows, place) in enumerate(PIECES[j])
            for part in range(3)
        ]

    for g in range(3):
        read_front(g).start()
        for k, ref in enumerate((zero_ref, one_ref, two_ref, three_ref)):
            @pl.when((r - g + 3) % 4 == k)
            def _():
                read_product(g, ref).start()
    for j in range(3):
        @pl.when((found > 0) & (turn == j))
        def _():
            for copy in read_child(j):
                copy.start()

    for g in range(3):
        read_front(g).wait()
        read_product(g, zero_ref).wait()
        held_ref[g] = held_ref[g] - product_ref[g].astype(F32)
        if g == 1:
            for j in range(3):
                @pl.when((found > 0) & (turn == j))
                def _():
                    for copy in read_child(j):
                        copy.wait()
        if g >= 1:
            for b in range(CHILD_BLOCKS):
                parent = where_ref[2 + b]
                @pl.when((found > 0) & (parent // 8 == g + 1))
                def _():
                    place = pl.ds(pl.multiple_of((parent % 8) * ROWS, ROWS), ROWS)
                    held_ref[g, :, place] += block_ref[:, b * ROWS : (b + 1) * ROWS].astype(F32)
        write(g).start()
    for g in range(3):
        write(g).wait()


def final(where, assembled, pieces, children):
    return pl.pallas_call(
        final_kernel,
        grid_spec=pltpu.PrefetchScalarGridSpec(
            num_scalar_prefetch=1,
            grid=(1,),
            in_specs=[pl.BlockSpec(memory_space=pl.ANY)] * 6,
            out_specs=pl.BlockSpec(memory_space=pl.ANY),
            scratch_shapes=[
                pltpu.VMEM((3, ROWS, GROUP), F32),
                pltpu.VMEM((3, ROWS, GROUP), BF16),
                pltpu.VMEM((ROWS, CHILD), BF16),
                pltpu.SemaphoreType.DMA((2, 3)),
                pltpu.SemaphoreType.DMA((4, 3)),
                pltpu.SemaphoreType.DMA((3,)),
            ],
        ),
        out_shape=jax.ShapeDtypeStruct((1, ROWS, 3 * GROUP), F32),
        compiler_params=pltpu.CompilerParams(vmem_limit_bytes=VMEM_LIMIT),
        name="final",
    )(where, assembled, *pieces, children)


def wanted_kernel(where_ref, parts_ref, out_ref, sems):
    r = where_ref[0]
    copies = []
    for z in range(8):
        child = jnp.int32(0)
        for b in range(CHILD_BLOCKS):
            child = child + jnp.where(where_ref[2 + b] == r * 8 + z, b, 0)
        source = parts_ref.at[jnp.minimum(child // 3, 3), pl.ds(ROWS, 3 * CHILD_ROWS), :]
        copies.append(pltpu.make_async_copy(source, out_ref.at[z], sems.at[z]))
        copies[z].start()
    for copy in copies:
        copy.wait()


def wanted(where, parts):
    return pl.pallas_call(
        wanted_kernel,
        grid_spec=pltpu.PrefetchScalarGridSpec(
            num_scalar_prefetch=1,
            grid=(1,),
            in_specs=[pl.BlockSpec((4, PART_ROWS, WIDTH), lambda i, w: (0, 0, 0))],
            out_specs=pl.BlockSpec(memory_space=pl.ANY),
            scratch_shapes=[pltpu.SemaphoreType.DMA((8,))],
        ),
        out_shape=jax.ShapeDtypeStruct((8, 3 * CHILD_ROWS, WIDTH), BF16),
        compiler_params=pltpu.CompilerParams(vmem_limit_bytes=VMEM_LIMIT),
        name="wanted",
    )(where, parts)


def on_device(assembled, update, blocks, inverses):
    r, z = lax.axis_index("row"), lax.axis_index("col")
    where = jnp.concatenate([jnp.stack([r, z]).astype(jnp.int32), blocks[0]])

    both, first = first_panel(assembled, inverses)
    columns = lax.all_gather(both, "col", axis=0)
    first, update = lax.optimization_barrier((first, update))
    child = lax.ppermute(update[0], "front", [(i, i ^ 1) for i in range(16)])
    firsts = lax.all_gather(first, "row", axis=0)

    top = firsts[0]
    child, top = lax.optimization_barrier((child, top))
    parts = lax.all_to_all(pack(both, child), "row", 0, 0)
    passed = lax.ppermute(top, "col", [(4, 1), (5, 0), (6, 3), (7, 2)])
    mine = jnp.where(z < 4, passed, top)
    beside = lax.ppermute(mine, "col", [(i, i ^ 1) for i in range(8)])
    across = lax.ppermute(
        jnp.concatenate([mine, beside]),
        "col",
        [(i, (i + 1) % 8 if i % 2 else (i + 7) % 8) for i in range(8)],
    )
    relay = mine, beside, across
    pieces = wanted(where, parts)
    relay, pieces = lax.optimization_barrier((relay, pieces))
    children = lax.all_to_all(pieces, "col", 0, 0)

    pieces = list(products(where, inverses, firsts, parts, columns, relay))
    factor = own_factor(where, assembled, inverses, first, relay)
    for s in range(1, 4):
        pairs = [(i, (i + s) % 4) for i in range(1, 4)]
        pieces[s] = lax.ppermute(pieces[s], "row", pairs)
    return factor, final(where, assembled, pieces, children)


def solution(mesh):
    return jax.shard_map(
        on_device,
        mesh=mesh,
        in_specs=(
            P("front", ("row", "col"), None),
            P("front", ("row", "col"), None),
            P("front", None),
            P("front", None, None, None),
        ),
        out_specs=(P("front", ("row", "col"), None), P("front", ("row", "col"), None)),
        check_vma=False,
    )
```

time: 132 us -> 126 us (0.955); the launches traced: 130 us -> 126 us
  waiting for transfers between devices: 44.2 us -> 39.3 us
  Pallas kernels: 19.7 us -> 21.8 us
    pallas_call x0 -> x2, Pallas kernels: none -> 5.38 us  [the longest x1 3.34 us: own_factor(): pl.pallas_call(factor_kernel, grid_spec=pltpu.PrefetchScalarGridSpec(num_...]
    ppermute x3, waiting for transfers between devices: 7.51 us -> 4.63 us  [on_device(): pieces[s] = lax.ppermute(pieces[s], 'row', pairs)]
    ppermute x1, waiting for transfers between devices: 10.4 us -> 12.8 us  [on_device(): passed = lax.ppermute(top, 'col', [(4, 1), (5, 0), (6, 3), (7, 2)])]
    ppermute x1, starting transfers between devices: 2.69 us -> 4.75 us  [on_device(): beside = lax.ppermute(mine, 'col', [(i, i ^ 1) for i in range(8)])]
    pallas_call x1, Pallas kernels: 9.33 us -> 7.55 us  [products(): pl.pallas_call(product_kernel, grid_spec=pltpu.PrefetchScalarGridSpec(num...]
    ppermute x1, starting transfers between devices: 4.54 us -> 2.75 us  [on_device(): lax.ppermute(jnp.concatenate([mine, beside]), 'col', [(i, (i + 1) % 8 if...]
    all_to_all x1, waiting for transfers between devices: 18.7 us -> 17.2 us  [on_device(): children = lax.all_to_all(pieces, 'col', 0, 0)]
    all_to_all x1, waiting for transfers between devices: 1.64 us -> 0.21 us  [on_device(): parts = lax.all_to_all(pack(both, child), 'row', 0, 0)]
  transfers between devices with their start and end apart: 10 -> 10, of which waited for: 7 -> 6; matrix products, arithmetic and copies ran while one was open for 0% -> 1% of each run, Pallas kernels for 10% -> 13%
where the time goes in v3:
time: 126 us
  waiting for transfers between devices  39.3 us (31%)
  starting transfers between devices  33.2 us (26%)
  Pallas kernels  21.8 us (17%)
  between operations  14.2 us (11%)
  blocking collectives  14.1 us (11%)
  local copies, waits for them, and re-layouts  2.57 us (2%)
    all_to_all x1, waiting for transfers between devices, on_device(): children = lax.all_to_all(pieces, 'col', 0, 0)  17.2 us
    all_gather x1, blocking collectives, on_device(): firsts = lax.all_gather(first, 'row', axis=0)  14.1 us
    ppermute x1, waiting for transfers between devices, on_device(): passed = lax.ppermute(top, 'col', [(4, 1), (5, 0), (6, 3), (7, 2)])  12.8 us
    ppermute x1, starting transfers between devices, on_device(): child = lax.ppermute(update[0], 'front', [(i, i ^ 1) for i in range(16)])  8.79 us
    all_to_all x1, starting transfers between devices, on_device(): children = lax.all_to_all(pieces, 'col', 0, 0)  7.94 us
    pallas_call x1, Pallas kernels, products(): pl.pallas_call(product_kernel, grid_spec=pltpu.PrefetchScalarGridSpec(num...  7.55 us
    ppermute x1, starting transfers between devices, on_device(): beside = lax.ppermute(mine, 'col', [(i, i ^ 1) for i in range(8)])  4.75 us
    ppermute x3, waiting for transfers between devices, on_device(): pieces[s] = lax.ppermute(pieces[s], 'row', pairs)  4.63 us
  transfers between devices with their start and end apart: 10, of which 6 were waited for; matrix products, arithmetic and copies ran while one was open for 1% of the time, Pallas kernels for 13%

profile of v3, /device:TPU:1, one launch (start us, length us, event | category | flops | bytes accessed | tf_op | source)
XLA Modules:
  0.0 125.9 jit_solution(11406299727406894810)
XLA Ops:
  7.2 0.0 copy-start.11
  7.2 0.0 all-gather.4.cloned.1.call-start
  7.2 2.4 %first_panel.1 = (bf16[128,1024]{1,0:T(8,128)(2,1)}, bf16[128,512]{1,0:T(8,128)(2,1)}) custom-call(f32[1,128,4096]{2,1,0:T(8,128)} %front_ref.5, bf16[1,2,512,512]{3,2,1,0:T(8,128)(2,1)} %inverse_ref.5), custom_call_target="tpu_custom_call" | custom-call | tf_op jit(solution)/shard_map/first_panel/pallas_call | solution.py:47
  9.6 0.0 all-gather.4.cloned.1.call-update
  9.6 0.0 copy-done.11
  9.6 8.8 %collective-permute-start = (bf16[48,1536]{1,0:T(8,128)(2,1)S(1)}, bf16[48,1536]{1,0:T(8,128)(2,1)S(1)}, u32[]{:S(2)}, u32[]{:S(2)}) collective-permute-start(bf16[48,1536]{1,0:T(8,128)(2,1)S(1)} %bitcast.9), channel_id=1, source_target_pairs={{0,32},{32,0},{64,96},{96,64},{128,160},{160,128},{192,224},{224,1... | collective-permute-start | bytes 442376 | tf_op jit(solution)/shard_map/ppermute | solution.py:352
  18.4 14.1 %all-gather = bf16[512,512]{1,0:T(8,128)(2,1)S(1)} all-gather(bf16[128,512]{1,0:T(8,128)(2,1)} %get-tuple-element.17.first_ref), channel_id=2, replica_groups=mesh['front'=16,'row'=4,'col'=8] {'row'}, dimensions={0}, use_global_device_ids=true | all-gather | bytes 655360 | tf_op jit(solution)/shard_map/all_gather | solution.py:353
  32.5 0.0 copy-start.2
  32.5 0.0 collective-permute-done.child_ref
  32.6 0.0 copy-start.9
  32.6 0.7 copy-done.9
  33.3 2.0 %pack.1 = bf16[4,272,512]{2,1,0:T(8,128)(2,1)} custom-call(bf16[128,1024]{1,0:T(8,128)(2,1)} %get-tuple-element.20.both_ref, bf16[48,1536]{1,0:T(8,128)(2,1)} %copy-done.9), custom_call_target="tpu_custom_call" | custom-call | tf_op jit(solution)/shard_map/pack/pallas_call | solution.py:76
  35.3 0.0 copy-start.10
  35.3 0.0 copy-done.2
  35.3 3.8 %all-to-all-start = ((bf16[4,272,512]{2,1,0:T(8,128)(2,1)}), bf16[4,272,512]{2,1,0:T(8,128)(2,1)S(1)}, u32[]{:S(2)}, u32[]{:S(2)}) async-start(bf16[4,272,512]{2,1,0:T(8,128)(2,1)} %pack.1), calls=%async_computation | async-start | bytes 2228224 | tf_op jit(solution)/shard_map/all_to_all | solution.py:357
  39.1 1.3 %collective-permute-start.1 = (bf16[128,512]{1,0:T(8,128)(2,1)S(1)}, bf16[128,512]{1,0:T(8,128)(2,1)S(1)}, u32[]{:S(2)}, u32[]{:S(2)}) collective-permute-start(bf16[128,512]{1,0:T(8,128)(2,1)S(1)} %slice.5), channel_id=1, source_target_pairs={{4,1},{5,0},{6,3},{7,2},{12,9},{13,8},{14,11},{15,10},{20,17},{21,... | collective-permute-start | bytes 393224 | tf_op jit(solution)/shard_map/ppermute | solution.py:358
  40.4 12.8 %collective-permute-done.1 = bf16[128,512]{1,0:T(8,128)(2,1)S(1)} collective-permute-done((bf16[128,512]{1,0:T(8,128)(2,1)S(1)}, bf16[128,512]{1,0:T(8,128)(2,1)S(1)}, u32[]{:S(2)}, u32[]{:S(2)}) %collective-permute-start.1) | collective-permute-done | bytes 131104 | tf_op jit(solution)/shard_map/ppermute | solution.py:358
  53.2 0.0 copy-start.3
  53.2 4.8 %collective-permute-start.2 = (bf16[128,512]{1,0:T(8,128)(2,1)S(1)}, bf16[128,512]{1,0:T(8,128)(2,1)S(1)}, u32[]{:S(2)}, u32[]{:S(2)}) collective-permute-start(bf16[128,512]{1,0:T(8,128)(2,1)S(1)} %broadcast_select_fusion.mine_ref), channel_id=1, source_target_pairs={{0,1},{1,0},{2,3},{3,2},{4,5},{5,4},{6,7},{7,6},{8,9},{9,8},{10,11... | collective-permute-start | bytes 393224 | tf_op jit(solution)/shard_map/ppermute | solution.py:360
  58.0 3.8 %collective-permute-done.2.beside_ref = bf16[128,512]{1,0:T(8,128)(2,1)S(1)} collective-permute-done((bf16[128,512]{1,0:T(8,128)(2,1)S(1)}, bf16[128,512]{1,0:T(8,128)(2,1)S(1)}, u32[]{:S(2)}, u32[]{:S(2)}) %collective-permute-start.2) | collective-permute-done | bytes 131104 | tf_op jit(solution)/shard_map/ppermute | solution.py:360
  61.7 0.0 copy-start.4
  61.8 2.8 %collective-permute-start.3 = (bf16[256,512]{1,0:T(8,128)(2,1)S(1)}, bf16[256,512]{1,0:T(8,128)(2,1)S(1)}, u32[]{:S(2)}, u32[]{:S(2)}) collective-permute-start(bf16[256,512]{1,0:T(8,128)(2,1)S(1)} %pad_maximum_fusion), channel_id=1, source_target_pairs={{0,7},{1,2},{2,1},{3,4},{4,3},{5,6},{6,5},{7,0},{8,15},{9,10},{10,... | collective-permute-start | bytes 786440 | tf_op jit(solution)/shard_map/ppermute | solution.py:361
  64.5 0.0 copy-done.10
  64.5 0.7 pad_add_fusion.where_ref
  65.2 0.2 all-to-all-done.parts_ref.nexts_ref
  65.4 0.0 copy-start
  65.4 1.0 copy-done
  66.4 3.0 %wanted.1 = bf16[8,144,512]{2,1,0:T(8,128)(2,1)} custom-call(s32[14]{0:T(128)} %pad_add_fusion.where_ref, bf16[4,272,512]{2,1,0:T(8,128)(2,1)} %copy-done), custom_call_target="tpu_custom_call" | custom-call | tf_op jit(solution)/shard_map/wanted/pallas_call | solution.py:330
  69.4 0.0 copy-done.3
  69.4 0.0 copy-done.4
  69.4 0.7 collective-permute-done.3.across_ref
  70.1 7.9 %all-to-all-start.1 = ((bf16[8,144,512]{2,1,0:T(8,128)(2,1)}), bf16[8,144,512]{2,1,0:T(8,128)(2,1)S(1)}, u32[]{:S(2)}, u32[]{:S(2)}) async-start(bf16[8,144,512]{2,1,0:T(8,128)(2,1)} %wanted.1), calls=%async_computation.1 | async-start | bytes 2359296 | tf_op jit(solution)/shard_map/all_to_all | solution.py:369
  78.0 0.0 all-gather.4.cloned.1.call-done
  78.0 0.0 copy-done.5
  78.1 7.5 %products.1 = (bf16[128,1024]{1,0:T(8,128)(2,1)}, bf16[128,1024]{1,0:T(8,128)(2,1)}, bf16[128,1024]{1,0:T(8,128)(2,1)}, bf16[128,1024]{1,0:T(8,128)(2,1)}) custom-call(s32[14]{0:T(128)} %pad_add_fusion.where_ref, bf16[1,2,512,512]{3,2,1,0:T(8,128)(2,1)} %inverse_ref.5, bf16[4,128,512]{2,1,0:T(8,128)(2,1)} %bitcast.6, bf16[4,272,512]{2,1,0:T(8,128)(2,1)} %copy-done, ...), custom_call_target="tpu_custom_call" | custom-call | tf_op jit(solution)/shard_map/products/pallas_call | solution.py:187
  85.6 1.3 %collective-permute-start.4 = (bf16[128,1024]{1,0:T(8,128)(2,1)}, bf16[128,1024]{1,0:T(8,128)(2,1)S(1)}, u32[]{:S(2)}, u32[]{:S(2)}) collective-permute-start(bf16[128,1024]{1,0:T(8,128)(2,1)} %get-tuple-element.26), channel_id=1, source_target_pairs={{8,16},{16,24},{24,0},{9,17},{17,25},{25,1},{10,18},{18,26},{26,2}... | collective-permute-start | bytes 786440 | tf_op jit(solution)/shard_map/ppermute | solution.py:375
  86.9 1.3 %collective-permute-start.5 = (bf16[128,1024]{1,0:T(8,128)(2,1)}, bf16[128,1024]{1,0:T(8,128)(2,1)S(1)}, u32[]{:S(2)}, u32[]{:S(2)}) collective-permute-start(bf16[128,1024]{1,0:T(8,128)(2,1)} %get-tuple-element.27), channel_id=1, source_target_pairs={{8,24},{16,0},{24,8},{9,25},{17,1},{25,9},{10,26},{18,2},{26,10},{... | collective-permute-start | bytes 786440 | tf_op jit(solution)/shard_map/ppermute | solution.py:375
  88.2 1.3 %collective-permute-start.6 = (bf16[128,1024]{1,0:T(8,128)(2,1)}, bf16[128,1024]{1,0:T(8,128)(2,1)S(1)}, u32[]{:S(2)}, u32[]{:S(2)}) collective-permute-start(bf16[128,1024]{1,0:T(8,128)(2,1)} %get-tuple-element.28), channel_id=1, source_target_pairs={{8,0},{16,8},{24,16},{9,1},{17,9},{25,17},{10,2},{18,10},{26,18},{... | collective-permute-start | bytes 786440 | tf_op jit(solution)/shard_map/ppermute | solution.py:375
  89.5 3.3 %own_factor.1 = bf16[1,128,1024]{2,1,0:T(8,128)(2,1)} custom-call(s32[14]{0:T(128)} %pad_add_fusion.where_ref, f32[1,128,4096]{2,1,0:T(8,128)} %front_ref.5, bf16[1,2,512,512]{3,2,1,0:T(8,128)(2,1)} %inverse_ref.5, bf16[128,512]{1,0:T(8,128)(2,1)} %get-tuple-element.17.first_ref, bf16[128,512]{1,0:T(8,128)(2,1)} %copy-done.3, bf16[128,512]{1,0:T(8,128)(2,1)} %copy-done.4, ...), custom_call_target="tpu_custom_call" | custom-call | flops 268435456 | bytes 2097152 | tf_op jit(solution)/shard_map/own_factor/pallas_call | solution.py:120
  92.9 17.2 %all-to-all-done.1.child_ref = bf16[8,144,512]{2,1,0:T(8,128)(2,1)S(1)} async-done(((bf16[8,144,512]{2,1,0:T(8,128)(2,1)}), bf16[8,144,512]{2,1,0:T(8,128)(2,1)S(1)}, u32[]{:S(2)}, u32[]{:S(2)}) %all-to-all-start.1) | async-done | bytes 1179680 | tf_op jit(solution)/shard_map/all_to_all | solution.py:369
  110.0 0.0 collective-permute-done.4.one_ref
  110.0 4.6 %collective-permute-done.5.two_ref = bf16[128,1024]{1,0:T(8,128)(2,1)S(1)} collective-permute-done((bf16[128,1024]{1,0:T(8,128)(2,1)}, bf16[128,1024]{1,0:T(8,128)(2,1)S(1)}, u32[]{:S(2)}, u32[]{:S(2)}) %collective-permute-start.5) | collective-permute-done | bytes 262176 | tf_op jit(solution)/shard_map/ppermute | solution.py:375
  114.7 0.0 collective-permute-done.6.three_ref
  114.7 0.0 copy-done.1
  114.7 0.0 copy-done.6
  114.7 0.7 copy-done.7
  115.4 0.1 copy-done.8
  115.5 3.5 %final.1 = f32[1,128,3072]{2,1,0:T(8,128)} custom-call(s32[14]{0:T(128)} %pad_add_fusion.where_ref, f32[1,128,4096]{2,1,0:T(8,128)} %front_ref.5, bf16[128,1024]{1,0:T(8,128)(2,1)} %get-tuple-element.25.zero_ref, bf16[128,1024]{1,0:T(8,128)(2,1)} %copy-done.6, bf16[128,1024]{1,0:T(8,128)(2,1)} %copy-done.7, bf16[128,1024]{1,0:T(8,128)(2,1)} %copy-done.8, ...), custom_call_target="tpu_custom_call" | custom-call | tf_op jit(solution)/shard_map/final/pallas_call | solution.py:293
  (8 shorter events, 0.1 us)
Async XLA Ops:
  7.2 2.5 %copy-start.11 = (bf16[1,48,1536]{2,1,0:T(8,128)(2,1)S(1)}, bf16[1,48,1536]{2,1,0:T(8,128)(2,1)}, u32[]{:S(2)}) copy-start(bf16[1,48,1536]{2,1,0:T(8,128)(2,1)} %param.5) | copy-start | bytes 442372
  7.2 70.9 %all-gather.4.cloned.1.call-start = ((), (), s32[]{:S(2)}) async-start(), calls=%async_computation.2 | async-start | bytes 2359296 | tf_op jit(solution)/shard_map/all_gather | solution.py:350
  9.6 22.9 %collective-permute-start = (bf16[48,1536]{1,0:T(8,128)(2,1)S(1)}, bf16[48,1536]{1,0:T(8,128)(2,1)S(1)}, u32[]{:S(2)}, u32[]{:S(2)}) collective-permute-start(bf16[48,1536]{1,0:T(8,128)(2,1)S(1)} %bitcast.9), channel_id=1, source_target_pairs={{0,32},{32,0},{64,96},{96,64},{128,160},{160,128},{192,224},{224,1... | collective-permute-start | bytes 442376 | tf_op jit(solution)/shard_map/ppermute | solution.py:352
  32.5 2.8 %copy-start.2 = (bf16[512,512]{1,0:T(8,128)(2,1)}, bf16[512,512]{1,0:T(8,128)(2,1)S(1)}, u32[]{:S(2)}) copy-start(bf16[512,512]{1,0:T(8,128)(2,1)S(1)} %all-gather) | copy-start | bytes 1572868
  32.6 0.7 copy-start.9
  35.3 29.2 %copy-start.10 = (s32[1,12]{1,0:T(1,128)S(1)}, s32[1,12]{1,0:T(1,128)}, u32[]{:S(2)}) copy-start(s32[1,12]{1,0:T(1,128)} %param.6) | copy-start | bytes 148
  35.3 30.1 %all-to-all-start = ((bf16[4,272,512]{2,1,0:T(8,128)(2,1)}), bf16[4,272,512]{2,1,0:T(8,128)(2,1)S(1)}, u32[]{:S(2)}, u32[]{:S(2)}) async-start(bf16[4,272,512]{2,1,0:T(8,128)(2,1)} %pack.1), calls=%async_computation | async-start | bytes 2228224 | tf_op jit(solution)/shard_map/all_to_all | solution.py:357
  39.1 14.1 %collective-permute-start.1 = (bf16[128,512]{1,0:T(8,128)(2,1)S(1)}, bf16[128,512]{1,0:T(8,128)(2,1)S(1)}, u32[]{:S(2)}, u32[]{:S(2)}) collective-permute-start(bf16[128,512]{1,0:T(8,128)(2,1)S(1)} %slice.5), channel_id=1, source_target_pairs={{4,1},{5,0},{6,3},{7,2},{12,9},{13,8},{14,11},{15,10},{20,17},{21,... | collective-permute-start | bytes 393224 | tf_op jit(solution)/shard_map/ppermute | solution.py:358
  53.2 16.2 %copy-start.3 = (bf16[128,512]{1,0:T(8,128)(2,1)}, bf16[128,512]{1,0:T(8,128)(2,1)S(1)}, u32[]{:S(2)}) copy-start(bf16[128,512]{1,0:T(8,128)(2,1)S(1)} %broadcast_select_fusion.mine_ref) | copy-start | bytes 393220
  53.2 8.5 %collective-permute-start.2 = (bf16[128,512]{1,0:T(8,128)(2,1)S(1)}, bf16[128,512]{1,0:T(8,128)(2,1)S(1)}, u32[]{:S(2)}, u32[]{:S(2)}) collective-permute-start(bf16[128,512]{1,0:T(8,128)(2,1)S(1)} %broadcast_select_fusion.mine_ref), channel_id=1, source_target_pairs={{0,1},{1,0},{2,3},{3,2},{4,5},{5,4},{6,7},{7,6},{8,9},{9,8},{10,11... | collective-permute-start | bytes 393224 | tf_op jit(solution)/shard_map/ppermute | solution.py:360
  61.7 7.7 %copy-start.4 = (bf16[128,512]{1,0:T(8,128)(2,1)}, bf16[128,512]{1,0:T(8,128)(2,1)S(1)}, u32[]{:S(2)}) copy-start(bf16[128,512]{1,0:T(8,128)(2,1)S(1)} %collective-permute-done.2.beside_ref) | copy-start | bytes 393220
  61.8 8.3 %collective-permute-start.3 = (bf16[256,512]{1,0:T(8,128)(2,1)S(1)}, bf16[256,512]{1,0:T(8,128)(2,1)S(1)}, u32[]{:S(2)}, u32[]{:S(2)}) collective-permute-start(bf16[256,512]{1,0:T(8,128)(2,1)S(1)} %pad_maximum_fusion), channel_id=1, source_target_pairs={{0,7},{1,2},{2,1},{3,4},{4,3},{5,6},{6,5},{7,0},{8,15},{9,10},{10,... | collective-permute-start | bytes 786440 | tf_op jit(solution)/shard_map/ppermute | solution.py:361
  65.4 1.0 copy-start
  70.1 8.0 %copy-start.5 = (bf16[256,512]{1,0:T(8,128)(2,1)}, bf16[256,512]{1,0:T(8,128)(2,1)S(1)}, u32[]{:S(2)}) copy-start(bf16[256,512]{1,0:T(8,128)(2,1)S(1)} %collective-permute-done.3.across_ref) | copy-start | bytes 786436
  70.1 39.9 %all-to-all-start.1 = ((bf16[8,144,512]{2,1,0:T(8,128)(2,1)}), bf16[8,144,512]{2,1,0:T(8,128)(2,1)S(1)}, u32[]{:S(2)}, u32[]{:S(2)}) async-start(bf16[8,144,512]{2,1,0:T(8,128)(2,1)} %wanted.1), calls=%async_computation.1 | async-start | bytes 2359296 | tf_op jit(solution)/shard_map/all_to_all | solution.py:369
  85.6 24.4 %collective-permute-start.4 = (bf16[128,1024]{1,0:T(8,128)(2,1)}, bf16[128,1024]{1,0:T(8,128)(2,1)S(1)}, u32[]{:S(2)}, u32[]{:S(2)}) collective-permute-start(bf16[128,1024]{1,0:T(8,128)(2,1)} %get-tuple-element.26), channel_id=1, source_target_pairs={{8,16},{16,24},{24,0},{9,17},{17,25},{25,1},{10,18},{18,26},{26,2}... | collective-permute-start | bytes 786440 | tf_op jit(solution)/shard_map/ppermute | solution.py:375
  86.9 27.7 %collective-permute-start.5 = (bf16[128,1024]{1,0:T(8,128)(2,1)}, bf16[128,1024]{1,0:T(8,128)(2,1)S(1)}, u32[]{:S(2)}, u32[]{:S(2)}) collective-permute-start(bf16[128,1024]{1,0:T(8,128)(2,1)} %get-tuple-element.27), channel_id=1, source_target_pairs={{8,24},{16,0},{24,8},{9,25},{17,1},{25,9},{10,26},{18,2},{26,10},{... | collective-permute-start | bytes 786440 | tf_op jit(solution)/shard_map/ppermute | solution.py:375
  88.2 26.5 %collective-permute-start.6 = (bf16[128,1024]{1,0:T(8,128)(2,1)}, bf16[128,1024]{1,0:T(8,128)(2,1)S(1)}, u32[]{:S(2)}, u32[]{:S(2)}) collective-permute-start(bf16[128,1024]{1,0:T(8,128)(2,1)} %get-tuple-element.28), channel_id=1, source_target_pairs={{8,0},{16,8},{24,16},{9,1},{17,9},{25,17},{10,2},{18,10},{26,18},{... | collective-permute-start | bytes 786440 | tf_op jit(solution)/shard_map/ppermute | solution.py:375
  110.0 4.6 %copy-start.1 = (bf16[8,144,512]{2,1,0:T(8,128)(2,1)}, bf16[8,144,512]{2,1,0:T(8,128)(2,1)S(1)}, u32[]{:S(2)}) copy-start(bf16[8,144,512]{2,1,0:T(8,128)(2,1)S(1)} %all-to-all-done.1.child_ref) | copy-start | bytes 3538948
  110.0 4.6 %copy-start.6 = (bf16[128,1024]{1,0:T(8,128)(2,1)}, bf16[128,1024]{1,0:T(8,128)(2,1)S(1)}, u32[]{:S(2)}) copy-start(bf16[128,1024]{1,0:T(8,128)(2,1)S(1)} %collective-permute-done.4.one_ref) | copy-start | bytes 786436
  114.7 0.7 copy-start.7
  114.7 0.8 copy-start.8
Sparse Core Ops, SparseCore 0:
  10.7 51.1 all-gather.3

commit v4 on v3

--- a/solution.py
+++ b/solution.py
@@ -12,7 +12,8 @@
 CHILD_BLOCKS = 12
 CHILD_ROWS = 48
 PART_ROWS = ROWS + 3 * CHILD_ROWS
-VMEM_LIMIT = 60 * 1024 * 1024
+MIB = 1024 * 1024
+VMEM_LIMIT = 60 * MIB
 
 F32 = jnp.float32
 BF16 = jnp.bfloat16
@@ -82,13 +83,36 @@
         ],
         out_specs=pl.BlockSpec((4, PART_ROWS, WIDTH), lambda i: (0, 0, 0)),
         out_shape=jax.ShapeDtypeStruct((4, PART_ROWS, WIDTH), BF16),
-        compiler_params=pltpu.CompilerParams(vmem_limit_bytes=VMEM_LIMIT),
+        compiler_params=pltpu.CompilerParams(vmem_limit_bytes=8 * MIB),
         name="pack",
     )(both, child)
 
 
 def piece_of(z):
     return jnp.where(z < 4, z ^ 1, z - 4)
+
+
+def mine_kernel(where_ref, passed_ref, top_ref, mine_ref):
+    mine_ref[...] = jnp.where(where_ref[1] < 4, passed_ref[...], top_ref[0])
+
+
+def first_relay(where, passed, firsts):
+    return pl.pallas_call(
+        mine_kernel,
+        grid_spec=pltpu.PrefetchScalarGridSpec(
+            num_scalar_prefetch=1,
+            grid=(1,),
+            in_specs=[
+                pl.BlockSpec((ROWS, WIDTH), lambda i, w: (0, 0)),
+                pl.BlockSpec((1, ROWS, WIDTH), lambda i, w: (0, 0, 0)),
+            ],
+            out_specs=pl.BlockSpec((ROWS, WIDTH), lambda i, w: (0, 0)),
+        ),
+        out_shape=jax.ShapeDtypeStruct((ROWS, WIDTH), BF16),
+        compiler_params=pltpu.CompilerParams(vmem_limit_bytes=8 * MIB),
+        cost_estimate=pl.CostEstimate(flops=11_800_000_000, bytes_accessed=2**20, transcendentals=0),
+        name="first_relay",
+    )(where, passed, firsts)
 
 
 def put_second(z, second_ref, mine_ref, beside_ref, across_ref):
@@ -134,7 +158,7 @@
             scratch_shapes=[pltpu.VMEM((WIDTH, WIDTH), BF16)],
         ),
         out_shape=jax.ShapeDtypeStruct((1, ROWS, 2 * WIDTH), BF16),
-        compiler_params=pltpu.CompilerParams(vmem_limit_bytes=VMEM_LIMIT),
+        compiler_params=pltpu.CompilerParams(vmem_limit_bytes=8 * MIB),
         cost_estimate=pl.CostEstimate(flops=2**28, bytes_accessed=2**21, transcendentals=0),
         name="own_factor",
     )(where, assembled, inverses, first, *relay)
@@ -209,7 +233,7 @@
             ],
         ),
         out_shape=[jax.ShapeDtypeStruct((ROWS, GROUP), BF16)] * 4,
-        compiler_params=pltpu.CompilerParams(vmem_limit_bytes=VMEM_LIMIT),
+        compiler_params=pltpu.CompilerParams(vmem_limit_bytes=58 * MIB),
         name="products",
     )(where, inverses, firsts, nexts, columns, *relay)
 
@@ -307,7 +331,7 @@
             ],
         ),
         out_shape=jax.ShapeDtypeStruct((1, ROWS, 3 * GROUP), F32),
-        compiler_params=pltpu.CompilerParams(vmem_limit_bytes=VMEM_LIMIT),
+        compiler_params=pltpu.CompilerParams(vmem_limit_bytes=8 * MIB),
         name="final",
     )(where, assembled, *pieces, children)
 
@@ -337,7 +361,7 @@
             scratch_shapes=[pltpu.SemaphoreType.DMA((8,))],
         ),
         out_shape=jax.ShapeDtypeStruct((8, 3 * CHILD_ROWS, WIDTH), BF16),
-        compiler_params=pltpu.CompilerParams(vmem_limit_bytes=VMEM_LIMIT),
+        compiler_params=pltpu.CompilerParams(vmem_limit_bytes=8 * MIB),
         name="wanted",
     )(where, parts)
 
@@ -356,7 +380,7 @@
     child, top = lax.optimization_barrier((child, top))
     parts = lax.all_to_all(pack(both, child), "row", 0, 0)
     passed = lax.ppermute(top, "col", [(4, 1), (5, 0), (6, 3), (7, 2)])
-    mine = jnp.where(z < 4, passed, top)
+    mine = first_relay(where, passed, firsts)
     beside = lax.ppermute(mine, "col", [(i, i ^ 1) for i in range(8)])
     across = lax.ppermute(
         jnp.concatenate([mine, beside]),

time: 126 us -> 122 us (0.968)
  Pallas kernels: 21.8 us -> 17.9 us
  local copies, waits for them, and re-layouts: 2.57 us -> 0.77 us
  starting transfers between devices: 33.2 us -> 34.7 us
    ppermute x1, waiting for transfers between devices: 12.8 us -> 7.2 us  [on_device(): passed = lax.ppermute(top, 'col', [(4, 1), (5, 0), (6, 3), (7, 2)])]
    all_to_all x1, waiting for transfers between devices: 0.21 us -> 5.28 us  [on_device(): parts = lax.all_to_all(pack(both, child), 'row', 0, 0)]
    unnamed x24 -> x34, local copies, waits for them, and re-layouts: 2.56 us -> 0.76 us
    pallas_call x1, Pallas kernels: 3.34 us -> 1.94 us  [own_factor(): pl.pallas_call(factor_kernel, grid_spec=pltpu.PrefetchScalarGridSpec(num_...]
    pallas_call x1, Pallas kernels: 2.98 us -> 1.69 us  [wanted(): pl.pallas_call(wanted_kernel, grid_spec=pltpu.PrefetchScalarGridSpec(num_...]
    ppermute x1, waiting for transfers between devices: 3.77 us -> 5.05 us  [on_device(): beside = lax.ppermute(mine, 'col', [(i, i ^ 1) for i in range(8)])]
  transfers between devices with their start and end apart: 10 -> 10, of which waited for: 6 -> 5; matrix products, arithmetic and copies ran while one was open for 1% -> 0% of each run, Pallas kernels for 13% -> 11%
where the time goes in v4:
time: 122 us
  waiting for transfers between devices  39.8 us (33%)
  starting transfers between devices  34.7 us (28%)
  Pallas kernels  17.9 us (15%)
  between operations  14.4 us (12%)
  blocking collectives  14.1 us (12%)
    all_to_all x1, waiting for transfers between devices, on_device(): children = lax.all_to_all(pieces, 'col', 0, 0)  18 us
    all_gather x1, blocking collectives, on_device(): firsts = lax.all_gather(first, 'row', axis=0)  14.1 us
    ppermute x1, starting transfers between devices, on_device(): child = lax.ppermute(update[0], 'front', [(i, i ^ 1) for i in range(16)])  8.92 us
    all_to_all x1, starting transfers between devices, on_device(): children = lax.all_to_all(pieces, 'col', 0, 0)  8.6 us
    pallas_call x1, Pallas kernels, products(): pl.pallas_call(product_kernel, grid_spec=pltpu.PrefetchScalarGridSpec(num...  7.96 us
    ppermute x1, waiting for transfers between devices, on_device(): passed = lax.ppermute(top, 'col', [(4, 1), (5, 0), (6, 3), (7, 2)])  7.2 us
    all_to_all x1, waiting for transfers between devices, on_device(): parts = lax.all_to_all(pack(both, child), 'row', 0, 0)  5.28 us
    ppermute x1, waiting for transfers between devices, on_device(): beside = lax.ppermute(mine, 'col', [(i, i ^ 1) for i in range(8)])  5.05 us
  transfers between devices with their start and end apart: 10, of which 5 were waited for; matrix products, arithmetic and copies ran while one was open for 0% of the time, Pallas kernels for 11%

profile of v4, /device:TPU:1, one launch (start us, length us, event | category | flops | bytes accessed | tf_op | source)
XLA Modules:
  0.0 121.7 jit_solution(5657167458383386833)
XLA Ops:
  7.2 0.0 copy-start.16
  7.2 0.0 all-gather.4.cloned.1.call-start
  7.2 2.4 %first_panel.1 = (bf16[128,1024]{1,0:T(8,128)(2,1)}, bf16[128,512]{1,0:T(8,128)(2,1)}) custom-call(f32[1,128,4096]{2,1,0:T(8,128)} %front_ref.5, bf16[1,2,512,512]{3,2,1,0:T(8,128)(2,1)} %inverse_ref.5), custom_call_target="tpu_custom_call" | custom-call | tf_op jit(solution)/shard_map/first_panel/pallas_call | solution.py:48
  9.6 0.0 all-gather.4.cloned.1.call-update
  9.6 0.0 copy-done.16
  9.6 8.9 %collective-permute-start = (bf16[48,1536]{1,0:T(8,128)(2,1)S(1)}, bf16[48,1536]{1,0:T(8,128)(2,1)S(1)}, u32[]{:S(2)}, u32[]{:S(2)}) collective-permute-start(bf16[48,1536]{1,0:T(8,128)(2,1)S(1)} %bitcast.10), channel_id=1, source_target_pairs={{0,32},{32,0},{64,96},{96,64},{128,160},{160,128},{192,224},{224,1... | collective-permute-start | bytes 442376 | tf_op jit(solution)/shard_map/ppermute | solution.py:376
  18.5 14.1 %all-gather = bf16[512,512]{1,0:T(8,128)(2,1)S(1)} all-gather(bf16[128,512]{1,0:T(8,128)(2,1)} %get-tuple-element.17.first_ref), channel_id=2, replica_groups=mesh['front'=16,'row'=4,'col'=8] {'row'}, dimensions={0}, use_global_device_ids=true | all-gather | bytes 655360 | tf_op jit(solution)/shard_map/all_gather | solution.py:377
  32.7 0.0 collective-permute-done.child_ref
  32.7 1.3 %collective-permute-start.1 = (bf16[128,512]{1,0:T(8,128)(2,1)S(1)}, bf16[128,512]{1,0:T(8,128)(2,1)S(1)}, u32[]{:S(2)}, u32[]{:S(2)}) collective-permute-start(bf16[128,512]{1,0:T(8,128)(2,1)S(1)} %slice.5), channel_id=1, source_target_pairs={{4,1},{5,0},{6,3},{7,2},{12,9},{13,8},{14,11},{15,10},{20,17},{21,... | collective-permute-start | bytes 393224 | tf_op jit(solution)/shard_map/ppermute | solution.py:382
  34.0 0.0 copy-done.10
  34.0 1.1 pack.1
  35.1 3.8 %all-to-all-start = ((bf16[4,272,512]{2,1,0:T(8,128)(2,1)}), bf16[4,272,512]{2,1,0:T(8,128)(2,1)S(1)}, u32[]{:S(2)}, u32[]{:S(2)}) async-start(bf16[4,272,512]{2,1,0:T(8,128)(2,1)} %pack.1), calls=%async_computation | async-start | bytes 2228224 | tf_op jit(solution)/shard_map/all_to_all | solution.py:381
  38.8 0.0 copy-done.15
  38.8 0.1 pad_add_fusion.where_ref
  38.9 7.2 %collective-permute-done.1.passed_ref = bf16[128,512]{1,0:T(8,128)(2,1)S(1)} collective-permute-done((bf16[128,512]{1,0:T(8,128)(2,1)S(1)}, bf16[128,512]{1,0:T(8,128)(2,1)S(1)}, u32[]{:S(2)}, u32[]{:S(2)}) %collective-permute-start.1) | collective-permute-done | bytes 131104 | tf_op jit(solution)/shard_map/ppermute | solution.py:382
  46.1 0.0 copy-done.3
  46.1 0.6 first_relay.1.mine_ref
  46.7 0.0 copy-start.4
  46.7 4.5 %collective-permute-start.2 = (bf16[128,512]{1,0:T(8,128)(2,1)S(1)}, bf16[128,512]{1,0:T(8,128)(2,1)S(1)}, u32[]{:S(2)}, u32[]{:S(2)}) collective-permute-start(bf16[128,512]{1,0:T(8,128)(2,1)S(1)} %first_relay.1.mine_ref), channel_id=1, source_target_pairs={{0,1},{1,0},{2,3},{3,2},{4,5},{5,4},{6,7},{7,6},{8,9},{9,8},{10,11... | collective-permute-start | bytes 393224 | tf_op jit(solution)/shard_map/ppermute | solution.py:384
  51.1 5.0 %collective-permute-done.2.beside_ref = bf16[128,512]{1,0:T(8,128)(2,1)S(1)} collective-permute-done((bf16[128,512]{1,0:T(8,128)(2,1)S(1)}, bf16[128,512]{1,0:T(8,128)(2,1)S(1)}, u32[]{:S(2)}, u32[]{:S(2)}) %collective-permute-start.2) | collective-permute-done | bytes 131104 | tf_op jit(solution)/shard_map/ppermute | solution.py:384
  56.2 3.6 %collective-permute-start.3 = (bf16[256,512]{1,0:T(8,128)(2,1)S(1)}, bf16[256,512]{1,0:T(8,128)(2,1)S(1)}, u32[]{:S(2)}, u32[]{:S(2)}) collective-permute-start(bf16[256,512]{1,0:T(8,128)(2,1)S(1)} %pad_maximum_fusion), channel_id=1, source_target_pairs={{0,7},{1,2},{2,1},{3,4},{4,3},{5,6},{6,5},{7,0},{8,15},{9,10},{10,... | collective-permute-start | bytes 786440 | tf_op jit(solution)/shard_map/ppermute | solution.py:385
  59.9 5.3 %all-to-all-done.parts_ref.nexts_ref = bf16[4,272,512]{2,1,0:T(8,128)(2,1)S(1)} async-done(((bf16[4,272,512]{2,1,0:T(8,128)(2,1)}), bf16[4,272,512]{2,1,0:T(8,128)(2,1)S(1)}, u32[]{:S(2)}, u32[]{:S(2)}) %all-to-all-start) | async-done | bytes 1114144 | tf_op jit(solution)/shard_map/all_to_all | solution.py:381
  65.2 0.0 copy-done.13
  65.2 1.7 %wanted.1 = bf16[8,144,512]{2,1,0:T(8,128)(2,1)} custom-call(s32[14]{0:T(128)S(1)} %pad_add_fusion.where_ref, bf16[4,272,512]{2,1,0:T(8,128)(2,1)S(1)} %all-to-all-done.parts_ref.nexts_ref), custom_call_target="tpu_custom_call" | custom-call | tf_op jit(solution)/shard_map/wanted/pallas_call | solution.py:354
  66.9 0.0 copy-done.4
  66.9 0.0 copy-done.6
  66.9 0.0 collective-permute-done.3.across_ref
  66.9 0.0 copy-start.8
  66.9 0.7 copy-done.8
  67.6 8.6 %all-to-all-start.1 = ((bf16[8,144,512]{2,1,0:T(8,128)(2,1)}), bf16[8,144,512]{2,1,0:T(8,128)(2,1)}, u32[]{:S(2)}, u32[]{:S(2)}) async-start(bf16[8,144,512]{2,1,0:T(8,128)(2,1)} %wanted.1), calls=%async_computation.1 | async-start | bytes 2359296 | tf_op jit(solution)/shard_map/all_to_all | solution.py:393
  76.2 0.0 all-gather.4.cloned.1.call-done
  76.2 0.0 copy-start
  76.2 0.0 copy-start.2
  76.2 0.0 copy-start.5
  76.3 0.0 copy-start.7
  76.3 0.0 copy-start.9
  76.3 0.0 copy-start.11
  76.3 0.0 copy-start.14
  76.3 8.0 %products.1 = (bf16[128,1024]{1,0:T(8,128)(2,1)}, bf16[128,1024]{1,0:T(8,128)(2,1)}, bf16[128,1024]{1,0:T(8,128)(2,1)}, bf16[128,1024]{1,0:T(8,128)(2,1)}) custom-call(s32[14]{0:T(128)} %copy-done.13, bf16[1,2,512,512]{3,2,1,0:T(8,128)(2,1)} %inverse_ref.5, bf16[4,128,512]{2,1,0:T(8,128)(2,1)} %bitcast.7, bf16[4,272,512]{2,1,0:T(8,128)(2,1)} %copy-done.1, ...), custom_call_target="tpu_custom_call" | custom-call | tf_op jit(solution)/shard_map/products/pallas_call | solution.py:211
  84.3 1.3 %collective-permute-start.4 = (bf16[128,1024]{1,0:T(8,128)(2,1)}, bf16[128,1024]{1,0:T(8,128)(2,1)S(1)}, u32[]{:S(2)}, u32[]{:S(2)}) collective-permute-start(bf16[128,1024]{1,0:T(8,128)(2,1)} %get-tuple-element.26), channel_id=1, source_target_pairs={{8,16},{16,24},{24,0},{9,17},{17,25},{25,1},{10,18},{18,26},{26,2}... | collective-permute-start | bytes 786440 | tf_op jit(solution)/shard_map/ppermute | solution.py:399
  85.6 1.3 %collective-permute-start.5 = (bf16[128,1024]{1,0:T(8,128)(2,1)}, bf16[128,1024]{1,0:T(8,128)(2,1)S(1)}, u32[]{:S(2)}, u32[]{:S(2)}) collective-permute-start(bf16[128,1024]{1,0:T(8,128)(2,1)} %get-tuple-element.27), channel_id=1, source_target_pairs={{8,24},{16,0},{24,8},{9,25},{17,1},{25,9},{10,26},{18,2},{26,10},{... | collective-permute-start | bytes 786440 | tf_op jit(solution)/shard_map/ppermute | solution.py:399
  86.9 1.4 %collective-permute-start.6 = (bf16[128,1024]{1,0:T(8,128)(2,1)}, bf16[128,1024]{1,0:T(8,128)(2,1)S(1)}, u32[]{:S(2)}, u32[]{:S(2)}) collective-permute-start(bf16[128,1024]{1,0:T(8,128)(2,1)} %get-tuple-element.28), channel_id=1, source_target_pairs={{8,0},{16,8},{24,16},{9,1},{17,9},{25,17},{10,2},{18,10},{26,18},{... | collective-permute-start | bytes 786440 | tf_op jit(solution)/shard_map/ppermute | solution.py:399
  88.4 1.9 %own_factor.1 = bf16[1,128,1024]{2,1,0:T(8,128)(2,1)} custom-call(s32[14]{0:T(128)S(1)} %copy-done.14, f32[1,128,4096]{2,1,0:T(8,128)S(1)} %copy-done, bf16[1,2,512,512]{3,2,1,0:T(8,128)(2,1)S(1)} %copy-done.2, bf16[128,512]{1,0:T(8,128)(2,1)S(1)} %copy-done.11, bf16[128,512]{1,0:T(8,128)(2,1)S(1)} %copy-done.5, bf16[128,512]{1,0:T(8,128)(2,1)S(1)} %copy-done.7, ...), custom_call_target="tpu_custom_call" | custom-call | flops 268435456 | bytes 2097152 | tf_op jit(solution)/shard_map/own_factor/pallas_call | solution.py:144
  90.3 18.0 %all-to-all-done.1.child_ref = bf16[8,144,512]{2,1,0:T(8,128)(2,1)} async-done(((bf16[8,144,512]{2,1,0:T(8,128)(2,1)}), bf16[8,144,512]{2,1,0:T(8,128)(2,1)}, u32[]{:S(2)}, u32[]{:S(2)}) %all-to-all-start.1) | async-done | bytes 1179680 | tf_op jit(solution)/shard_map/all_to_all | solution.py:393
  108.3 0.0 collective-permute-done.4.one_ref
  108.3 4.2 %collective-permute-done.5.two_ref = bf16[128,1024]{1,0:T(8,128)(2,1)S(1)} collective-permute-done((bf16[128,1024]{1,0:T(8,128)(2,1)}, bf16[128,1024]{1,0:T(8,128)(2,1)S(1)}, u32[]{:S(2)}, u32[]{:S(2)}) %collective-permute-start.5) | collective-permute-done | bytes 262176 | tf_op jit(solution)/shard_map/ppermute | solution.py:399
  112.5 0.0 collective-permute-done.6.three_ref
  112.5 2.3 %final.1 = f32[1,128,3072]{2,1,0:T(8,128)} custom-call(s32[14]{0:T(128)S(1)} %copy-done.14, f32[1,128,4096]{2,1,0:T(8,128)S(1)} %copy-done, bf16[128,1024]{1,0:T(8,128)(2,1)S(1)} %copy-done.12, bf16[128,1024]{1,0:T(8,128)(2,1)S(1)} %collective-permute-done.4.one_ref, bf16[128,1024]{1,0:T(8,128)(2,1)S(1)} %collective-permute-done.5.two_ref, ...), custom_call_target="tpu_custom_call" | custom-call | tf_op jit(solution)/shard_map/final/pallas_call | solution.py:317
  (18 shorter events, 0.1 us)
Async XLA Ops:
  7.2 2.4 %copy-start.16 = (bf16[1,48,1536]{2,1,0:T(8,128)(2,1)S(1)}, bf16[1,48,1536]{2,1,0:T(8,128)(2,1)}, u32[]{:S(2)}) copy-start(bf16[1,48,1536]{2,1,0:T(8,128)(2,1)} %param.5) | copy-start | bytes 442372
  7.2 69.0 %all-gather.4.cloned.1.call-start = ((), (), s32[]{:S(2)}) async-start(), calls=%async_computation.2 | async-start | bytes 2359296 | tf_op jit(solution)/shard_map/all_gather | solution.py:374
  9.6 24.4 %copy-start.10 = (bf16[128,1024]{1,0:T(8,128)(2,1)S(1)}, bf16[128,1024]{1,0:T(8,128)(2,1)}, u32[]{:S(2)}) copy-start(bf16[128,1024]{1,0:T(8,128)(2,1)} %get-tuple-element.20.both_ref) | copy-start | bytes 786436
  9.6 23.1 %collective-permute-start = (bf16[48,1536]{1,0:T(8,128)(2,1)S(1)}, bf16[48,1536]{1,0:T(8,128)(2,1)S(1)}, u32[]{:S(2)}, u32[]{:S(2)}) collective-permute-start(bf16[48,1536]{1,0:T(8,128)(2,1)S(1)} %bitcast.10), channel_id=1, source_target_pairs={{0,32},{32,0},{64,96},{96,64},{128,160},{160,128},{192,224},{224,1... | collective-permute-start | bytes 442376 | tf_op jit(solution)/shard_map/ppermute | solution.py:376
  32.6 13.5 %copy-start.3 = (bf16[512,512]{1,0:T(8,128)(2,1)}, bf16[512,512]{1,0:T(8,128)(2,1)S(1)}, u32[]{:S(2)}) copy-start(bf16[512,512]{1,0:T(8,128)(2,1)S(1)} %all-gather) | copy-start | bytes 1572868
  32.7 13.4 %collective-permute-start.1 = (bf16[128,512]{1,0:T(8,128)(2,1)S(1)}, bf16[128,512]{1,0:T(8,128)(2,1)S(1)}, u32[]{:S(2)}, u32[]{:S(2)}) collective-permute-start(bf16[128,512]{1,0:T(8,128)(2,1)S(1)} %slice.5), channel_id=1, source_target_pairs={{4,1},{5,0},{6,3},{7,2},{12,9},{13,8},{14,11},{15,10},{20,17},{21,... | collective-permute-start | bytes 393224 | tf_op jit(solution)/shard_map/ppermute | solution.py:382
  35.1 3.8 %copy-start.15 = (s32[1,12]{1,0:T(1,128)S(1)}, s32[1,12]{1,0:T(1,128)}, u32[]{:S(2)}) copy-start(s32[1,12]{1,0:T(1,128)} %param.6) | copy-start | bytes 148
  35.1 30.1 %all-to-all-start = ((bf16[4,272,512]{2,1,0:T(8,128)(2,1)}), bf16[4,272,512]{2,1,0:T(8,128)(2,1)S(1)}, u32[]{:S(2)}, u32[]{:S(2)}) async-start(bf16[4,272,512]{2,1,0:T(8,128)(2,1)} %pack.1), calls=%async_computation | async-start | bytes 2228224 | tf_op jit(solution)/shard_map/all_to_all | solution.py:381
  38.9 26.2 %copy-start.13 = (s32[14]{0:T(128)}, s32[14]{0:T(128)S(1)}, u32[]{:S(2)}) copy-start(s32[14]{0:T(128)S(1)} %pad_add_fusion.where_ref) | copy-start | bytes 172
  46.7 20.2 %copy-start.4 = (bf16[128,512]{1,0:T(8,128)(2,1)}, bf16[128,512]{1,0:T(8,128)(2,1)S(1)}, u32[]{:S(2)}) copy-start(bf16[128,512]{1,0:T(8,128)(2,1)S(1)} %first_relay.1.mine_ref) | copy-start | bytes 393220
  46.7 9.5 %collective-permute-start.2 = (bf16[128,512]{1,0:T(8,128)(2,1)S(1)}, bf16[128,512]{1,0:T(8,128)(2,1)S(1)}, u32[]{:S(2)}, u32[]{:S(2)}) collective-permute-start(bf16[128,512]{1,0:T(8,128)(2,1)S(1)} %first_relay.1.mine_ref), channel_id=1, source_target_pairs={{0,1},{1,0},{2,3},{3,2},{4,5},{5,4},{6,7},{7,6},{8,9},{9,8},{10,11... | collective-permute-start | bytes 393224 | tf_op jit(solution)/shard_map/ppermute | solution.py:384
  56.2 10.7 %copy-start.6 = (bf16[128,512]{1,0:T(8,128)(2,1)}, bf16[128,512]{1,0:T(8,128)(2,1)S(1)}, u32[]{:S(2)}) copy-start(bf16[128,512]{1,0:T(8,128)(2,1)S(1)} %collective-permute-done.2.beside_ref) | copy-start | bytes 393220
  56.2 10.7 %collective-permute-start.3 = (bf16[256,512]{1,0:T(8,128)(2,1)S(1)}, bf16[256,512]{1,0:T(8,128)(2,1)S(1)}, u32[]{:S(2)}, u32[]{:S(2)}) collective-permute-start(bf16[256,512]{1,0:T(8,128)(2,1)S(1)} %pad_maximum_fusion), channel_id=1, source_target_pairs={{0,7},{1,2},{2,1},{3,4},{4,3},{5,6},{6,5},{7,0},{8,15},{9,10},{10,... | collective-permute-start | bytes 786440 | tf_op jit(solution)/shard_map/ppermute | solution.py:385
  65.2 1.7 %copy-start.1 = (bf16[4,272,512]{2,1,0:T(8,128)(2,1)}, bf16[4,272,512]{2,1,0:T(8,128)(2,1)S(1)}, u32[]{:S(2)}) copy-start(bf16[4,272,512]{2,1,0:T(8,128)(2,1)S(1)} %all-to-all-done.parts_ref.nexts_ref) | copy-start | bytes 3342340
  66.9 0.7 copy-start.8
  67.6 40.7 %all-to-all-start.1 = ((bf16[8,144,512]{2,1,0:T(8,128)(2,1)}), bf16[8,144,512]{2,1,0:T(8,128)(2,1)}, u32[]{:S(2)}, u32[]{:S(2)}) async-start(bf16[8,144,512]{2,1,0:T(8,128)(2,1)} %wanted.1), calls=%async_computation.1 | async-start | bytes 2359296 | tf_op jit(solution)/shard_map/all_to_all | solution.py:393
  76.2 12.1 %copy-start = (f32[1,128,4096]{2,1,0:T(8,128)S(1)}, f32[1,128,4096]{2,1,0:T(8,128)}, u32[]{:S(2)}) copy-start(f32[1,128,4096]{2,1,0:T(8,128)} %front_ref.5) | copy-start | bytes 6291460
  76.2 12.1 %copy-start.2 = (bf16[1,2,512,512]{3,2,1,0:T(8,128)(2,1)S(1)}, bf16[1,2,512,512]{3,2,1,0:T(8,128)(2,1)}, u32[]{:S(2)}) copy-start(bf16[1,2,512,512]{3,2,1,0:T(8,128)(2,1)} %inverse_ref.5) | copy-start | bytes 3145732
  76.2 12.1 %copy-start.5 = (bf16[128,512]{1,0:T(8,128)(2,1)S(1)}, bf16[128,512]{1,0:T(8,128)(2,1)}, u32[]{:S(2)}) copy-start(bf16[128,512]{1,0:T(8,128)(2,1)} %copy-done.4) | copy-start | bytes 393220
  76.3 12.1 %copy-start.7 = (bf16[128,512]{1,0:T(8,128)(2,1)S(1)}, bf16[128,512]{1,0:T(8,128)(2,1)}, u32[]{:S(2)}) copy-start(bf16[128,512]{1,0:T(8,128)(2,1)} %copy-done.6) | copy-start | bytes 393220
  76.3 12.1 %copy-start.9 = (bf16[256,512]{1,0:T(8,128)(2,1)S(1)}, bf16[256,512]{1,0:T(8,128)(2,1)}, u32[]{:S(2)}) copy-start(bf16[256,512]{1,0:T(8,128)(2,1)} %copy-done.8) | copy-start | bytes 786436
  76.3 12.1 %copy-start.11 = (bf16[128,512]{1,0:T(8,128)(2,1)S(1)}, bf16[128,512]{1,0:T(8,128)(2,1)}, u32[]{:S(2)}) copy-start(bf16[128,512]{1,0:T(8,128)(2,1)} %get-tuple-element.17.first_ref) | copy-start | bytes 393220
  76.3 12.1 %copy-start.14 = (s32[14]{0:T(128)S(1)}, s32[14]{0:T(128)}, u32[]{:S(2)}) copy-start(s32[14]{0:T(128)} %copy-done.13) | copy-start | bytes 172
  84.3 24.0 %collective-permute-start.4 = (bf16[128,1024]{1,0:T(8,128)(2,1)}, bf16[128,1024]{1,0:T(8,128)(2,1)S(1)}, u32[]{:S(2)}, u32[]{:S(2)}) collective-permute-start(bf16[128,1024]{1,0:T(8,128)(2,1)} %get-tuple-element.26), channel_id=1, source_target_pairs={{8,16},{16,24},{24,0},{9,17},{17,25},{25,1},{10,18},{18,26},{26,2}... | collective-permute-start | bytes 786440 | tf_op jit(solution)/shard_map/ppermute | solution.py:399
  85.6 26.9 %collective-permute-start.5 = (bf16[128,1024]{1,0:T(8,128)(2,1)}, bf16[128,1024]{1,0:T(8,128)(2,1)S(1)}, u32[]{:S(2)}, u32[]{:S(2)}) collective-permute-start(bf16[128,1024]{1,0:T(8,128)(2,1)} %get-tuple-element.27), channel_id=1, source_target_pairs={{8,24},{16,0},{24,8},{9,25},{17,1},{25,9},{10,26},{18,2},{26,10},{... | collective-permute-start | bytes 786440 | tf_op jit(solution)/shard_map/ppermute | solution.py:399
  86.9 25.7 %copy-start.12 = (bf16[128,1024]{1,0:T(8,128)(2,1)S(1)}, bf16[128,1024]{1,0:T(8,128)(2,1)}, u32[]{:S(2)}) copy-start(bf16[128,1024]{1,0:T(8,128)(2,1)} %get-tuple-element.25.zero_ref) | copy-start | bytes 786436
  86.9 25.6 %collective-permute-start.6 = (bf16[128,1024]{1,0:T(8,128)(2,1)}, bf16[128,1024]{1,0:T(8,128)(2,1)S(1)}, u32[]{:S(2)}, u32[]{:S(2)}) collective-permute-start(bf16[128,1024]{1,0:T(8,128)(2,1)} %get-tuple-element.28), channel_id=1, source_target_pairs={{8,0},{16,8},{24,16},{9,1},{17,9},{25,17},{10,2},{18,10},{26,18},{... | collective-permute-start | bytes 786440 | tf_op jit(solution)/shard_map/ppermute | solution.py:399
Sparse Core Ops, SparseCore 0:
  10.7 53.1 all-gather.3

commit v5 on v4

--- a/solution.py
+++ b/solution.py
@@ -8,6 +8,7 @@
 WIDTH = 512
 ROWS = 128
 GROUP = 1024
+SENT = GROUP - ROWS
 CHILD = 1536
 CHILD_BLOCKS = 12
 CHILD_ROWS = 48
@@ -166,14 +167,43 @@
 
 def product_kernel(
     where_ref, inverse_ref, firsts_ref, nexts_ref, column_ref, mine_ref, beside_ref, across_ref,
-    zero_ref, one_ref, two_ref, three_ref, second_ref, weight_ref, rows_ref, columns_ref, held_ref, sem,
+    zero_ref, one_ref, two_ref, three_ref, across_groups_ref,
+    held_inverse_ref, second_ref, weight_ref, rows_ref, next_ref, columns_ref, following_ref, sems,
 ):
-    copy = pltpu.make_async_copy(column_ref, held_ref, sem)
-    copy.start()
     r, z = where_ref[0], where_ref[1]
-    put_second(z, second_ref, mine_ref, beside_ref, across_ref)
-    inverse = inverse_ref[0, 0]
-
+
+    def rows_at(place):
+        return pl.ds(pl.multiple_of(place * ROWS, ROWS), ROWS)
+
+    def await_all(ref, sem):
+        pltpu.make_async_copy(ref, ref, sem).wait()
+
+    here, there = piece_of(z), piece_of((z + 2 * (z % 2) + 7) % 8)
+    pieces = (
+        (here, mine_ref),
+        (here ^ 1, beside_ref),
+        (there, across_ref.at[:ROWS]),
+        (there ^ 1, across_ref.at[ROWS:]),
+    )
+    for place, ref in pieces:
+        pltpu.make_async_copy(ref, second_ref.at[rows_at(place)], sems.at[0]).start()
+    pltpu.make_async_copy(inverse_ref.at[0, 1], held_inverse_ref, sems.at[1]).start()
+    for k in range(4):
+        place = rows_at((k - r + 4) % 4)
+        part = rows_ref.at[place, pl.ds(0, WIDTH)]
+        pltpu.make_async_copy(firsts_ref.at[k], part, sems.at[2]).start()
+        part = nexts_ref.at[k, pl.ds(0, ROWS)]
+        pltpu.make_async_copy(part, next_ref.at[place], sems.at[3]).start()
+    for j in range(8):
+        place = rows_at((j - z + 7) % 8)
+        part = column_ref.at[j, :, pl.ds(0, WIDTH)]
+        pltpu.make_async_copy(part, columns_ref.at[place, pl.ds(0, WIDTH)], sems.at[4]).start()
+        part = column_ref.at[j, :, pl.ds(WIDTH, WIDTH)]
+        pltpu.make_async_copy(part, following_ref.at[place], sems.at[5]).start()
+
+    await_all(second_ref, sems.at[0])
+    await_all(held_inverse_ref, sems.at[1])
+    inverse = held_inverse_ref[...]
     turned = lax.dot_general(
         second_ref[...], inverse, (((0,), (0,)), ((), ())), preferred_element_type=F32
     )
@@ -185,54 +215,50 @@
         lost = dot(first, weight_ref[0]) + dot(first, weight_ref[1])
         return dot(following, inverse) - lost
 
-    first = firsts_ref[...].reshape(4 * ROWS, WIDTH)
-    panel = panel_of(first, nexts_ref[...].reshape(4 * ROWS, WIDTH))
-    above = lax.broadcasted_iota(jnp.int32, (4 * ROWS, WIDTH), 0) < jnp.where(z < 4, ROWS, 0)
-    panel = jnp.where(above, jnp.zeros_like(panel), panel).astype(BF16)
-    for k in range(4):
-        place = pl.ds(pl.multiple_of(((k - r + 4) % 4) * ROWS, ROWS), ROWS)
-        rows_ref[place, :WIDTH] = first[k * ROWS : (k + 1) * ROWS]
-        rows_ref[place, WIDTH:] = panel[k * ROWS : (k + 1) * ROWS]
-    copy.wait()
+    await_all(rows_ref.at[:, pl.ds(0, WIDTH)], sems.at[2])
+    await_all(next_ref, sems.at[3])
+    panel = panel_of(rows_ref[:, :WIDTH], next_ref[...])
+    top = jnp.where(z < 4, (4 - r) % 4, 4)
+    above = lax.broadcasted_iota(jnp.int32, (4 * ROWS, WIDTH), 0) // ROWS == top
+    rows_ref[:, WIDTH:] = jnp.where(above, jnp.zeros_like(panel), panel).astype(BF16)
+    await_all(columns_ref.at[:, pl.ds(0, WIDTH)], sems.at[4])
+    await_all(following_ref, sems.at[5])
     for half in range(2):
         place = pl.ds(half * 4 * ROWS, 4 * ROWS)
-        first = held_ref[4 * half : 4 * half + 4].reshape(4 * ROWS, 2 * WIDTH)
-        columns_ref[place, :WIDTH] = first[:, :WIDTH]
-        columns_ref[place, WIDTH:] = panel_of(first[:, :WIDTH], first[:, WIDTH:]).astype(BF16)
+        panel = panel_of(columns_ref[place, :WIDTH], following_ref[place, :])
+        columns_ref[place, WIDTH:] = panel.astype(BF16)
     for part in range(4):
         place = pl.ds(part * 256, 256)
         total = dot_t(rows_ref[...], columns_ref[place, :]).astype(BF16)
-        for k, ref in enumerate((zero_ref, one_ref, two_ref, three_ref)):
-            ref[:, place] = total[k * ROWS : (k + 1) * ROWS]
+        zero_ref[:, place] = total[:ROWS]
+        width = min(256, SENT - part * 256)
+        for k, ref in enumerate((one_ref, two_ref, three_ref), 1):
+            ref[:, part * 256 : part * 256 + width] = total[k * ROWS : (k + 1) * ROWS, :width]
+    across_groups_ref[...] = dot_t(rows_ref[:ROWS, :], rows_ref[...]).astype(BF16)
 
 
 def products(where, inverses, firsts, nexts, columns, relay):
     whole = lambda *shape: pl.BlockSpec(shape, lambda i, w: (0,) * len(shape))
+    widths = GROUP, SENT, SENT, SENT, 4 * ROWS
     return pl.pallas_call(
         product_kernel,
         grid_spec=pltpu.PrefetchScalarGridSpec(
             num_scalar_prefetch=1,
             grid=(1,),
-            in_specs=[
-                pl.BlockSpec((1, 1, WIDTH, WIDTH), lambda i, w: (0, 1, 0, 0)),
-                whole(4, ROWS, WIDTH),
-                whole(4, ROWS, WIDTH),
-                pl.BlockSpec(memory_space=pl.ANY),
-                whole(ROWS, WIDTH),
-                whole(ROWS, WIDTH),
-                whole(2 * ROWS, WIDTH),
-            ],
-            out_specs=[whole(ROWS, GROUP)] * 4,
+            in_specs=[pl.BlockSpec(memory_space=pl.ANY)] * 7,
+            out_specs=[whole(ROWS, width) for width in widths],
             scratch_shapes=[
+                pltpu.VMEM((WIDTH, WIDTH), BF16),
                 pltpu.VMEM((WIDTH, WIDTH), BF16),
                 pltpu.VMEM((2, WIDTH, WIDTH), BF16),
                 pltpu.VMEM((4 * ROWS, 2 * WIDTH), BF16),
+                pltpu.VMEM((4 * ROWS, WIDTH), BF16),
                 pltpu.VMEM((8 * ROWS, 2 * WIDTH), BF16),
-                pltpu.VMEM((8, ROWS, 2 * WIDTH), BF16),
-                pltpu.SemaphoreType.DMA,
+                pltpu.VMEM((8 * ROWS, WIDTH), BF16),
+                pltpu.SemaphoreType.DMA((6,)),
             ],
         ),
-        out_shape=[jax.ShapeDtypeStruct((ROWS, GROUP), BF16)] * 4,
+        out_shape=[jax.ShapeDtypeStruct((ROWS, width), BF16) for width in widths],
         compiler_params=pltpu.CompilerParams(vmem_limit_bytes=58 * MIB),
         name="products",
     )(where, inverses, firsts, nexts, columns, *relay)
@@ -246,7 +272,7 @@
 
 
 def final_kernel(
-    where_ref, front_ref, zero_ref, one_ref, two_ref, three_ref, child_ref, schur_ref,
+    where_ref, front_ref, zero_ref, one_ref, two_ref, three_ref, across_groups_ref, child_ref, schur_ref,
     held_ref, product_ref, block_ref, read_sems, child_sems, write_sems,
 ):
     r, z = where_ref[0], where_ref[1]
@@ -261,8 +287,16 @@
         place = pl.ds((g + 1) * GROUP, GROUP)
         return pltpu.make_async_copy(front_ref.at[0, :, place], held_ref.at[g], read_sems.at[0, g])
 
-    def read_product(g, ref):
-        return pltpu.make_async_copy(ref, product_ref.at[g], read_sems.at[1, g])
+    def read_product(g, k):
+        if k == 0:
+            return [pltpu.make_async_copy(zero_ref, product_ref.at[g], read_sems.at[1, g])]
+        sent = product_ref.at[g, :, pl.ds(0, SENT)]
+        kept = product_ref.at[g, :, pl.ds(SENT, ROWS)]
+        place = pl.ds((4 - k) * ROWS, ROWS)
+        return [
+            pltpu.make_async_copy((one_ref, two_ref, three_ref)[k - 1], sent, read_sems.at[1, g]),
+            pltpu.make_async_copy(across_groups_ref.at[:, place], kept, read_sems.at[1, g]),
+        ]
 
     def write(g):
         place = pl.ds(g * GROUP, GROUP)
@@ -281,10 +315,11 @@
 
     for g in range(3):
         read_front(g).start()
-        for k, ref in enumerate((zero_ref, one_ref, two_ref, three_ref)):
+        for k in range(4):
             @pl.when((r - g + 3) % 4 == k)
             def _():
-                read_product(g, ref).start()
+                for copy in read_product(g, k):
+                    copy.start()
     for j in range(3):
         @pl.when((found > 0) & (turn == j))
         def _():
@@ -293,8 +328,10 @@
 
     for g in range(3):
         read_front(g).wait()
-        read_product(g, zero_ref).wait()
-        held_ref[g] = held_ref[g] - product_ref[g].astype(F32)
+        read_product(g, 0)[0].wait()
+        for i in range(8):
+            place = pl.ds(pl.multiple_of((z + 1 + i) % 8 * ROWS, ROWS), ROWS)
+            held_ref[g, :, place] -= product_ref[g, :, i * ROWS : (i + 1) * ROWS].astype(F32)
         if g == 1:
             for j in range(3):
                 @pl.when((found > 0) & (turn == j))
@@ -319,7 +356,7 @@
         grid_spec=pltpu.PrefetchScalarGridSpec(
             num_scalar_prefetch=1,
             grid=(1,),
-            in_specs=[pl.BlockSpec(memory_space=pl.ANY)] * 6,
+            in_specs=[pl.BlockSpec(memory_space=pl.ANY)] * 7,
             out_specs=pl.BlockSpec(memory_space=pl.ANY),
             scratch_shapes=[
                 pltpu.VMEM((3, ROWS, GROUP), F32),
@@ -392,11 +429,12 @@
     relay, pieces = lax.optimization_barrier((relay, pieces))
     children = lax.all_to_all(pieces, "col", 0, 0)
 
-    pieces = list(products(where, inverses, firsts, parts, columns, relay))
+    zero, one, two, three, across_groups = products(where, inverses, firsts, parts, columns, relay)
     factor = own_factor(where, assembled, inverses, first, relay)
-    for s in range(1, 4):
-        pairs = [(i, (i + s) % 4) for i in range(1, 4)]
-        pieces[s] = lax.ppermute(pieces[s], "row", pairs)
+    two = lax.ppermute(two, "row", [(i, (i + 2) % 4) for i in range(1, 4)])
+    one = lax.ppermute(one, "row", [(i, (i + 1) % 4) for i in range(1, 4)])
+    three = lax.ppermute(three, "row", [(i, (i + 3) % 4) for i in range(1, 4)])
+    pieces = zero, one, two, three, across_groups
     return factor, final(where, assembled, pieces, children)
 
 

time: 122 us -> 120 us (0.984)
  waiting for transfers between devices: 39.8 us -> 37.3 us
    ppermute x3, waiting for transfers between devices: 4.21 us -> 1.47 us  [the longest x1 0.78 us: on_device(): three = lax.ppermute(three, 'row', [(i, (i + 3) % 4) for i in range(1, 4)])]
  transfers between devices with their start and end apart: 10 -> 10, of which waited for: 5 -> 6; matrix products, arithmetic and copies ran while one was open for 0% -> 0% of each run, Pallas kernels for 11% -> 11%
where the time goes in v5:
time: 120 us; the launch traced here: 119 us
  waiting for transfers between devices  37.3 us (31%)
  starting transfers between devices  34.7 us (29%)
  Pallas kernels  17.8 us (15%)
  between operations  14.4 us (12%)
  blocking collectives  14.1 us (12%)
    all_to_all x1, waiting for transfers between devices, on_device(): children = lax.all_to_all(pieces, 'col', 0, 0)  18.3 us
    all_gather x1, blocking collectives, on_device(): firsts = lax.all_gather(first, 'row', axis=0)  14.1 us
    ppermute x1, starting transfers between devices, on_device(): child = lax.ppermute(update[0], 'front', [(i, i ^ 1) for i in range(16)])  8.92 us
    all_to_all x1, starting transfers between devices, on_device(): children = lax.all_to_all(pieces, 'col', 0, 0)  8.6 us
    pallas_call x1, Pallas kernels, products(): pl.pallas_call(product_kernel, grid_spec=pltpu.PrefetchScalarGridSpec(num...  7.68 us
    ppermute x1, waiting for transfers between devices, on_device(): passed = lax.ppermute(top, 'col', [(4, 1), (5, 0), (6, 3), (7, 2)])  7.2 us
    all_to_all x1, waiting for transfers between devices, on_device(): parts = lax.all_to_all(pack(both, child), 'row', 0, 0)  5.28 us
    ppermute x1, waiting for transfers between devices, on_device(): beside = lax.ppermute(mine, 'col', [(i, i ^ 1) for i in range(8)])  5.07 us
  transfers between devices with their start and end apart: 10, of which 6 were waited for; matrix products, arithmetic and copies ran while one was open for 0% of the time, Pallas kernels for 11%

profile of v5, /device:TPU:1, one launch (start us, length us, event | category | flops | bytes accessed | tf_op | source)
XLA Modules:
  0.0 119.2 jit_solution(8256955117087015793)
XLA Ops:
  7.2 0.0 copy-start.17
  7.2 0.0 all-gather.4.cloned.1.call-start
  7.2 2.4 %first_panel.1 = (bf16[128,1024]{1,0:T(8,128)(2,1)}, bf16[128,512]{1,0:T(8,128)(2,1)}) custom-call(f32[1,128,4096]{2,1,0:T(8,128)} %front_ref.5, bf16[1,2,512,512]{3,2,1,0:T(8,128)(2,1)} %inverse_ref.5), custom_call_target="tpu_custom_call" | custom-call | tf_op jit(solution)/shard_map/first_panel/pallas_call | solution.py:49
  9.6 0.0 all-gather.4.cloned.1.call-update
  9.6 0.0 copy-done.17
  9.6 8.9 %collective-permute-start = (bf16[48,1536]{1,0:T(8,128)(2,1)S(1)}, bf16[48,1536]{1,0:T(8,128)(2,1)S(1)}, u32[]{:S(2)}, u32[]{:S(2)}) collective-permute-start(bf16[48,1536]{1,0:T(8,128)(2,1)S(1)} %bitcast.10), channel_id=1, source_target_pairs={{0,32},{32,0},{64,96},{96,64},{128,160},{160,128},{192,224},{224,1... | collective-permute-start | bytes 442376 | tf_op jit(solution)/shard_map/ppermute | solution.py:413
  18.5 14.1 %all-gather = bf16[512,512]{1,0:T(8,128)(2,1)S(1)} all-gather(bf16[128,512]{1,0:T(8,128)(2,1)} %get-tuple-element.18.first_ref), channel_id=2, replica_groups=mesh['front'=16,'row'=4,'col'=8] {'row'}, dimensions={0}, use_global_device_ids=true | all-gather | bytes 655360 | tf_op jit(solution)/shard_map/all_gather | solution.py:414
  32.7 0.0 collective-permute-done.child_ref
  32.7 1.3 %collective-permute-start.1 = (bf16[128,512]{1,0:T(8,128)(2,1)S(1)}, bf16[128,512]{1,0:T(8,128)(2,1)S(1)}, u32[]{:S(2)}, u32[]{:S(2)}) collective-permute-start(bf16[128,512]{1,0:T(8,128)(2,1)S(1)} %slice.5), channel_id=1, source_target_pairs={{4,1},{5,0},{6,3},{7,2},{12,9},{13,8},{14,11},{15,10},{20,17},{21,... | collective-permute-start | bytes 393224 | tf_op jit(solution)/shard_map/ppermute | solution.py:419
  34.0 0.0 copy-done.10
  34.0 1.1 pack.1
  35.1 3.8 %all-to-all-start = ((bf16[4,272,512]{2,1,0:T(8,128)(2,1)}), bf16[4,272,512]{2,1,0:T(8,128)(2,1)S(1)}, u32[]{:S(2)}, u32[]{:S(2)}) async-start(bf16[4,272,512]{2,1,0:T(8,128)(2,1)} %pack.1), calls=%async_computation | async-start | bytes 2228224 | tf_op jit(solution)/shard_map/all_to_all | solution.py:418
  38.8 0.0 copy-done.16
  38.8 0.1 pad_add_fusion.where_ref
  38.9 7.2 %collective-permute-done.1.passed_ref = bf16[128,512]{1,0:T(8,128)(2,1)S(1)} collective-permute-done((bf16[128,512]{1,0:T(8,128)(2,1)S(1)}, bf16[128,512]{1,0:T(8,128)(2,1)S(1)}, u32[]{:S(2)}, u32[]{:S(2)}) %collective-permute-start.1) | collective-permute-done | bytes 131104 | tf_op jit(solution)/shard_map/ppermute | solution.py:419
  46.1 0.0 copy-done.3
  46.1 0.6 first_relay.1.mine_ref
  46.7 0.0 copy-start.4
  46.7 4.5 %collective-permute-start.2 = (bf16[128,512]{1,0:T(8,128)(2,1)S(1)}, bf16[128,512]{1,0:T(8,128)(2,1)S(1)}, u32[]{:S(2)}, u32[]{:S(2)}) collective-permute-start(bf16[128,512]{1,0:T(8,128)(2,1)S(1)} %first_relay.1.mine_ref), channel_id=1, source_target_pairs={{0,1},{1,0},{2,3},{3,2},{4,5},{5,4},{6,7},{7,6},{8,9},{9,8},{10,11... | collective-permute-start | bytes 393224 | tf_op jit(solution)/shard_map/ppermute | solution.py:421
  51.1 5.1 %collective-permute-done.2.beside_ref = bf16[128,512]{1,0:T(8,128)(2,1)S(1)} collective-permute-done((bf16[128,512]{1,0:T(8,128)(2,1)S(1)}, bf16[128,512]{1,0:T(8,128)(2,1)S(1)}, u32[]{:S(2)}, u32[]{:S(2)}) %collective-permute-start.2) | collective-permute-done | bytes 131104 | tf_op jit(solution)/shard_map/ppermute | solution.py:421
  56.2 3.6 %collective-permute-start.3 = (bf16[256,512]{1,0:T(8,128)(2,1)S(1)}, bf16[256,512]{1,0:T(8,128)(2,1)S(1)}, u32[]{:S(2)}, u32[]{:S(2)}) collective-permute-start(bf16[256,512]{1,0:T(8,128)(2,1)S(1)} %pad_maximum_fusion), channel_id=1, source_target_pairs={{0,7},{1,2},{2,1},{3,4},{4,3},{5,6},{6,5},{7,0},{8,15},{9,10},{10,... | collective-permute-start | bytes 786440 | tf_op jit(solution)/shard_map/ppermute | solution.py:422
  59.9 5.3 %all-to-all-done.parts_ref.nexts_ref = bf16[4,272,512]{2,1,0:T(8,128)(2,1)S(1)} async-done(((bf16[4,272,512]{2,1,0:T(8,128)(2,1)}), bf16[4,272,512]{2,1,0:T(8,128)(2,1)S(1)}, u32[]{:S(2)}, u32[]{:S(2)}) %all-to-all-start) | async-done | bytes 1114144 | tf_op jit(solution)/shard_map/all_to_all | solution.py:418
  65.2 0.0 copy-done.14
  65.2 1.7 %wanted.1 = bf16[8,144,512]{2,1,0:T(8,128)(2,1)} custom-call(s32[14]{0:T(128)S(1)} %pad_add_fusion.where_ref, bf16[4,272,512]{2,1,0:T(8,128)(2,1)S(1)} %all-to-all-done.parts_ref.nexts_ref), custom_call_target="tpu_custom_call" | custom-call | tf_op jit(solution)/shard_map/wanted/pallas_call | solution.py:391
  66.9 0.0 copy-done.4
  66.9 0.0 collective-permute-done.3.across_ref
  66.9 0.0 copy-start.8
  66.9 0.0 copy-done.1
  66.9 0.7 copy-done.8
  67.6 8.6 %all-to-all-start.1 = ((bf16[8,144,512]{2,1,0:T(8,128)(2,1)}), bf16[8,144,512]{2,1,0:T(8,128)(2,1)}, u32[]{:S(2)}, u32[]{:S(2)}) async-start(bf16[8,144,512]{2,1,0:T(8,128)(2,1)} %wanted.1), calls=%async_computation.1 | async-start | bytes 2359296 | tf_op jit(solution)/shard_map/all_to_all | solution.py:430
  76.2 0.0 all-gather.4.cloned.1.call-done
  76.2 0.0 copy-start
  76.2 0.0 copy-start.2
  76.2 0.0 copy-start.5
  76.3 0.0 copy-start.7
  76.3 0.0 copy-start.9
  76.3 0.0 copy-start.11
  76.3 0.0 copy-start.15
  76.3 7.7 %products.1 = (bf16[128,1024]{1,0:T(8,128)(2,1)}, bf16[128,896]{1,0:T(8,128)(2,1)}, bf16[128,896]{1,0:T(8,128)(2,1)}, bf16[128,896]{1,0:T(8,128)(2,1)}, bf16[128,512]{1,0:T(8,128)(2,1)}) custom-call(s32[14]{0:T(128)} %copy-done.14, bf16[1,2,512,512]{3,2,1,0:T(8,128)(2,1)} %inverse_ref.5, bf16[4,128,512]{2,1,0:T(8,128)(2,1)} %bitcast.7, ...), custom_call_target="tpu_custom_call" | custom-call | tf_op jit(solution)/shard_map/products/pallas_call | solution.py:243
  84.0 1.3 %collective-permute-start.4 = (bf16[128,896]{1,0:T(8,128)(2,1)}, bf16[128,896]{1,0:T(8,128)(2,1)S(1)}, u32[]{:S(2)}, u32[]{:S(2)}) collective-permute-start(bf16[128,896]{1,0:T(8,128)(2,1)} %get-tuple-element.27), channel_id=1, source_target_pairs={{8,16},{16,24},{24,0},{9,17},{17,25},{25,1},{10,18},{18,26},{26,2}... | collective-permute-start | bytes 688136 | tf_op jit(solution)/shard_map/ppermute | solution.py:435
  85.3 1.3 %collective-permute-start.5 = (bf16[128,896]{1,0:T(8,128)(2,1)}, bf16[128,896]{1,0:T(8,128)(2,1)S(1)}, u32[]{:S(2)}, u32[]{:S(2)}) collective-permute-start(bf16[128,896]{1,0:T(8,128)(2,1)} %get-tuple-element.28), channel_id=1, source_target_pairs={{8,24},{16,0},{24,8},{9,25},{17,1},{25,9},{10,26},{18,2},{26,10},{... | collective-permute-start | bytes 688136 | tf_op jit(solution)/shard_map/ppermute | solution.py:434
  86.6 1.4 %collective-permute-start.6 = (bf16[128,896]{1,0:T(8,128)(2,1)}, bf16[128,896]{1,0:T(8,128)(2,1)S(1)}, u32[]{:S(2)}, u32[]{:S(2)}) collective-permute-start(bf16[128,896]{1,0:T(8,128)(2,1)} %get-tuple-element.29), channel_id=1, source_target_pairs={{8,0},{16,8},{24,16},{9,1},{17,9},{25,17},{10,2},{18,10},{26,18},{... | collective-permute-start | bytes 688136 | tf_op jit(solution)/shard_map/ppermute | solution.py:436
  88.1 1.9 %own_factor.1 = bf16[1,128,1024]{2,1,0:T(8,128)(2,1)} custom-call(s32[14]{0:T(128)S(1)} %copy-done.15, f32[1,128,4096]{2,1,0:T(8,128)S(1)} %copy-done, bf16[1,2,512,512]{3,2,1,0:T(8,128)(2,1)S(1)} %copy-done.2, bf16[128,512]{1,0:T(8,128)(2,1)S(1)} %copy-done.11, bf16[128,512]{1,0:T(8,128)(2,1)S(1)} %copy-done.5, bf16[128,512]{1,0:T(8,128)(2,1)S(1)} %copy-done.7, ...), custom_call_target="tpu_custom_call" | custom-call | flops 268435456 | bytes 2097152 | tf_op jit(solution)/shard_map/own_factor/pallas_call | solution.py:145
  90.0 18.3 %all-to-all-done.1.child_ref = bf16[8,144,512]{2,1,0:T(8,128)(2,1)} async-done(((bf16[8,144,512]{2,1,0:T(8,128)(2,1)}), bf16[8,144,512]{2,1,0:T(8,128)(2,1)}, u32[]{:S(2)}, u32[]{:S(2)}) %all-to-all-start.1) | async-done | bytes 1179680 | tf_op jit(solution)/shard_map/all_to_all | solution.py:430
  108.3 0.0 collective-permute-done.4.one_ref
  108.3 0.7 collective-permute-done.5.two_ref
  109.0 0.8 collective-permute-done.6.three_ref
  109.8 2.6 %final.1 = f32[1,128,3072]{2,1,0:T(8,128)} custom-call(s32[14]{0:T(128)S(1)} %copy-done.15, f32[1,128,4096]{2,1,0:T(8,128)S(1)} %copy-done, bf16[128,1024]{1,0:T(8,128)(2,1)S(1)} %copy-done.12, bf16[128,896]{1,0:T(8,128)(2,1)S(1)} %collective-permute-done.4.one_ref, bf16[128,896]{1,0:T(8,128)(2,1)S(1)} %collective-permute-done.5.two_ref, ...), custom_call_target="tpu_custom_call" | custom-call | tf_op jit(solution)/shard_map/final/pallas_call | solution.py:354
  (20 shorter events, 0.1 us)
Async XLA Ops:
  7.2 2.4 %copy-start.17 = (bf16[1,48,1536]{2,1,0:T(8,128)(2,1)S(1)}, bf16[1,48,1536]{2,1,0:T(8,128)(2,1)}, u32[]{:S(2)}) copy-start(bf16[1,48,1536]{2,1,0:T(8,128)(2,1)} %param.5) | copy-start | bytes 442372
  7.2 69.0 %all-gather.4.cloned.1.call-start = ((), (), s32[]{:S(2)}) async-start(), calls=%async_computation.2 | async-start | bytes 2359296 | tf_op jit(solution)/shard_map/all_gather | solution.py:411
  9.6 24.4 %copy-start.10 = (bf16[128,1024]{1,0:T(8,128)(2,1)S(1)}, bf16[128,1024]{1,0:T(8,128)(2,1)}, u32[]{:S(2)}) copy-start(bf16[128,1024]{1,0:T(8,128)(2,1)} %get-tuple-element.21.both_ref) | copy-start | bytes 786436
  9.6 23.1 %collective-permute-start = (bf16[48,1536]{1,0:T(8,128)(2,1)S(1)}, bf16[48,1536]{1,0:T(8,128)(2,1)S(1)}, u32[]{:S(2)}, u32[]{:S(2)}) collective-permute-start(bf16[48,1536]{1,0:T(8,128)(2,1)S(1)} %bitcast.10), channel_id=1, source_target_pairs={{0,32},{32,0},{64,96},{96,64},{128,160},{160,128},{192,224},{224,1... | collective-permute-start | bytes 442376 | tf_op jit(solution)/shard_map/ppermute | solution.py:413
  32.6 13.5 %copy-start.3 = (bf16[512,512]{1,0:T(8,128)(2,1)}, bf16[512,512]{1,0:T(8,128)(2,1)S(1)}, u32[]{:S(2)}) copy-start(bf16[512,512]{1,0:T(8,128)(2,1)S(1)} %all-gather) | copy-start | bytes 1572868
  32.7 13.4 %collective-permute-start.1 = (bf16[128,512]{1,0:T(8,128)(2,1)S(1)}, bf16[128,512]{1,0:T(8,128)(2,1)S(1)}, u32[]{:S(2)}, u32[]{:S(2)}) collective-permute-start(bf16[128,512]{1,0:T(8,128)(2,1)S(1)} %slice.5), channel_id=1, source_target_pairs={{4,1},{5,0},{6,3},{7,2},{12,9},{13,8},{14,11},{15,10},{20,17},{21,... | collective-permute-start | bytes 393224 | tf_op jit(solution)/shard_map/ppermute | solution.py:419
  35.1 3.8 %copy-start.16 = (s32[1,12]{1,0:T(1,128)S(1)}, s32[1,12]{1,0:T(1,128)}, u32[]{:S(2)}) copy-start(s32[1,12]{1,0:T(1,128)} %param.6) | copy-start | bytes 148
  35.1 30.1 %all-to-all-start = ((bf16[4,272,512]{2,1,0:T(8,128)(2,1)}), bf16[4,272,512]{2,1,0:T(8,128)(2,1)S(1)}, u32[]{:S(2)}, u32[]{:S(2)}) async-start(bf16[4,272,512]{2,1,0:T(8,128)(2,1)} %pack.1), calls=%async_computation | async-start | bytes 2228224 | tf_op jit(solution)/shard_map/all_to_all | solution.py:418
  38.9 26.2 %copy-start.14 = (s32[14]{0:T(128)}, s32[14]{0:T(128)S(1)}, u32[]{:S(2)}) copy-start(s32[14]{0:T(128)S(1)} %pad_add_fusion.where_ref) | copy-start | bytes 172
  46.7 20.2 %copy-start.4 = (bf16[128,512]{1,0:T(8,128)(2,1)}, bf16[128,512]{1,0:T(8,128)(2,1)S(1)}, u32[]{:S(2)}) copy-start(bf16[128,512]{1,0:T(8,128)(2,1)S(1)} %first_relay.1.mine_ref) | copy-start | bytes 393220
  46.7 9.5 %collective-permute-start.2 = (bf16[128,512]{1,0:T(8,128)(2,1)S(1)}, bf16[128,512]{1,0:T(8,128)(2,1)S(1)}, u32[]{:S(2)}, u32[]{:S(2)}) collective-permute-start(bf16[128,512]{1,0:T(8,128)(2,1)S(1)} %first_relay.1.mine_ref), channel_id=1, source_target_pairs={{0,1},{1,0},{2,3},{3,2},{4,5},{5,4},{6,7},{7,6},{8,9},{9,8},{10,11... | collective-permute-start | bytes 393224 | tf_op jit(solution)/shard_map/ppermute | solution.py:421
  56.2 10.7 %copy-start.6 = (bf16[128,512]{1,0:T(8,128)(2,1)}, bf16[128,512]{1,0:T(8,128)(2,1)S(1)}, u32[]{:S(2)}) copy-start(bf16[128,512]{1,0:T(8,128)(2,1)S(1)} %collective-permute-done.2.beside_ref) | copy-start | bytes 393220
  56.2 10.6 %collective-permute-start.3 = (bf16[256,512]{1,0:T(8,128)(2,1)S(1)}, bf16[256,512]{1,0:T(8,128)(2,1)S(1)}, u32[]{:S(2)}, u32[]{:S(2)}) collective-permute-start(bf16[256,512]{1,0:T(8,128)(2,1)S(1)} %pad_maximum_fusion), channel_id=1, source_target_pairs={{0,7},{1,2},{2,1},{3,4},{4,3},{5,6},{6,5},{7,0},{8,15},{9,10},{10,... | collective-permute-start | bytes 786440 | tf_op jit(solution)/shard_map/ppermute | solution.py:422
  65.2 1.7 %copy-start.1 = (bf16[4,272,512]{2,1,0:T(8,128)(2,1)}, bf16[4,272,512]{2,1,0:T(8,128)(2,1)S(1)}, u32[]{:S(2)}) copy-start(bf16[4,272,512]{2,1,0:T(8,128)(2,1)S(1)} %all-to-all-done.parts_ref.nexts_ref) | copy-start | bytes 3342340
  66.9 0.7 copy-start.8
  67.6 40.7 %all-to-all-start.1 = ((bf16[8,144,512]{2,1,0:T(8,128)(2,1)}), bf16[8,144,512]{2,1,0:T(8,128)(2,1)}, u32[]{:S(2)}, u32[]{:S(2)}) async-start(bf16[8,144,512]{2,1,0:T(8,128)(2,1)} %wanted.1), calls=%async_computation.1 | async-start | bytes 2359296 | tf_op jit(solution)/shard_map/all_to_all | solution.py:430
  76.2 11.8 %copy-start = (f32[1,128,4096]{2,1,0:T(8,128)S(1)}, f32[1,128,4096]{2,1,0:T(8,128)}, u32[]{:S(2)}) copy-start(f32[1,128,4096]{2,1,0:T(8,128)} %front_ref.5) | copy-start | bytes 6291460
  76.2 11.8 %copy-start.2 = (bf16[1,2,512,512]{3,2,1,0:T(8,128)(2,1)S(1)}, bf16[1,2,512,512]{3,2,1,0:T(8,128)(2,1)}, u32[]{:S(2)}) copy-start(bf16[1,2,512,512]{3,2,1,0:T(8,128)(2,1)} %inverse_ref.5) | copy-start | bytes 3145732
  76.2 11.8 %copy-start.5 = (bf16[128,512]{1,0:T(8,128)(2,1)S(1)}, bf16[128,512]{1,0:T(8,128)(2,1)}, u32[]{:S(2)}) copy-start(bf16[128,512]{1,0:T(8,128)(2,1)} %copy-done.4) | copy-start | bytes 393220
  76.3 11.8 %copy-start.7 = (bf16[128,512]{1,0:T(8,128)(2,1)S(1)}, bf16[128,512]{1,0:T(8,128)(2,1)}, u32[]{:S(2)}) copy-start(bf16[128,512]{1,0:T(8,128)(2,1)} %copy-done.6) | copy-start | bytes 393220
  76.3 11.8 %copy-start.9 = (bf16[256,512]{1,0:T(8,128)(2,1)S(1)}, bf16[256,512]{1,0:T(8,128)(2,1)}, u32[]{:S(2)}) copy-start(bf16[256,512]{1,0:T(8,128)(2,1)} %copy-done.8) | copy-start | bytes 786436
  76.3 11.8 %copy-start.11 = (bf16[128,512]{1,0:T(8,128)(2,1)S(1)}, bf16[128,512]{1,0:T(8,128)(2,1)}, u32[]{:S(2)}) copy-start(bf16[128,512]{1,0:T(8,128)(2,1)} %get-tuple-element.18.first_ref) | copy-start | bytes 393220
  76.3 11.8 %copy-start.15 = (s32[14]{0:T(128)S(1)}, s32[14]{0:T(128)}, u32[]{:S(2)}) copy-start(s32[14]{0:T(128)} %copy-done.14) | copy-start | bytes 172
  84.0 24.3 %collective-permute-start.4 = (bf16[128,896]{1,0:T(8,128)(2,1)}, bf16[128,896]{1,0:T(8,128)(2,1)S(1)}, u32[]{:S(2)}, u32[]{:S(2)}) collective-permute-start(bf16[128,896]{1,0:T(8,128)(2,1)} %get-tuple-element.27), channel_id=1, source_target_pairs={{8,16},{16,24},{24,0},{9,17},{17,25},{25,1},{10,18},{18,26},{26,2}... | collective-permute-start | bytes 688136 | tf_op jit(solution)/shard_map/ppermute | solution.py:435
  85.3 23.7 %collective-permute-start.5 = (bf16[128,896]{1,0:T(8,128)(2,1)}, bf16[128,896]{1,0:T(8,128)(2,1)S(1)}, u32[]{:S(2)}, u32[]{:S(2)}) collective-permute-start(bf16[128,896]{1,0:T(8,128)(2,1)} %get-tuple-element.28), channel_id=1, source_target_pairs={{8,24},{16,0},{24,8},{9,25},{17,1},{25,9},{10,26},{18,2},{26,10},{... | collective-permute-start | bytes 688136 | tf_op jit(solution)/shard_map/ppermute | solution.py:434
  86.6 23.2 %copy-start.12 = (bf16[128,1024]{1,0:T(8,128)(2,1)S(1)}, bf16[128,1024]{1,0:T(8,128)(2,1)}, u32[]{:S(2)}) copy-start(bf16[128,1024]{1,0:T(8,128)(2,1)} %get-tuple-element.26.zero_ref) | copy-start | bytes 786436
  86.6 23.2 %copy-start.13 = (bf16[128,512]{1,0:T(8,128)(2,1)S(1)}, bf16[128,512]{1,0:T(8,128)(2,1)}, u32[]{:S(2)}) copy-start(bf16[128,512]{1,0:T(8,128)(2,1)} %get-tuple-element.30.across_groups_ref) | copy-start | bytes 393220
  86.6 23.2 %collective-permute-start.6 = (bf16[128,896]{1,0:T(8,128)(2,1)}, bf16[128,896]{1,0:T(8,128)(2,1)S(1)}, u32[]{:S(2)}, u32[]{:S(2)}) collective-permute-start(bf16[128,896]{1,0:T(8,128)(2,1)} %get-tuple-element.29), channel_id=1, source_target_pairs={{8,0},{16,8},{24,16},{9,1},{17,9},{25,17},{10,2},{18,10},{26,18},{... | collective-permute-start | bytes 688136 | tf_op jit(solution)/shard_map/ppermute | solution.py:436
Sparse Core Ops, SparseCore 0:
  10.7 53.1 all-gather.3

commit v6 on v5

--- a/solution.py
+++ b/solution.py
@@ -12,7 +12,9 @@
 CHILD = 1536
 CHILD_BLOCKS = 12
 CHILD_ROWS = 48
-PART_ROWS = ROWS + 3 * CHILD_ROWS
+HALF = CHILD // 2
+THIRD = 256
+PART_ROWS = 2 * ROWS + 3 * CHILD_ROWS
 MIB = 1024 * 1024
 VMEM_LIMIT = 60 * MIB
 
@@ -68,10 +70,14 @@
 
 def pack_kernel(both_ref, child_ref, parts_ref):
     for k in range(4):
-        parts_ref[k, :ROWS] = both_ref[...]
+        for half in range(2):
+            place = slice(half * ROWS, (half + 1) * ROWS)
+            parts_ref[k, place] = both_ref[:, half * THIRD : (half + 1) * THIRD]
+        first = 0 if k >= 2 else HALF
         for part in range(3):
-            start = ROWS + part * CHILD_ROWS
-            parts_ref[k, start : start + CHILD_ROWS] = child_ref[:, part * WIDTH : (part + 1) * WIDTH]
+            start = 2 * ROWS + part * CHILD_ROWS
+            column = first + part * THIRD
+            parts_ref[k, start : start + CHILD_ROWS] = child_ref[:, column : column + THIRD]
 
 
 def pack(both, child):
@@ -82,8 +88,8 @@
             pl.BlockSpec((ROWS, WIDTH), lambda i: (0, 1)),
             pl.BlockSpec((CHILD_ROWS, CHILD), lambda i: (0, 0)),
         ],
-        out_specs=pl.BlockSpec((4, PART_ROWS, WIDTH), lambda i: (0, 0, 0)),
-        out_shape=jax.ShapeDtypeStruct((4, PART_ROWS, WIDTH), BF16),
+        out_specs=pl.BlockSpec((4, PART_ROWS, THIRD), lambda i: (0, 0, 0)),
+        out_shape=jax.ShapeDtypeStruct((4, PART_ROWS, THIRD), BF16),
         compiler_params=pltpu.CompilerParams(vmem_limit_bytes=8 * MIB),
         name="pack",
     )(both, child)
@@ -192,8 +198,10 @@
         place = rows_at((k - r + 4) % 4)
         part = rows_ref.at[place, pl.ds(0, WIDTH)]
         pltpu.make_async_copy(firsts_ref.at[k], part, sems.at[2]).start()
-        part = nexts_ref.at[k, pl.ds(0, ROWS)]
-        pltpu.make_async_copy(part, next_ref.at[place], sems.at[3]).start()
+        for half in range(2):
+            source = nexts_ref.at[k, pl.ds(half * ROWS, ROWS), :]
+            part = next_ref.at[place, pl.ds(half * THIRD, THIRD)]
+            pltpu.make_async_copy(source, part, sems.at[3]).start()
     for j in range(8):
         place = rows_at((j - z + 7) % 8)
         part = column_ref.at[j, :, pl.ds(0, WIDTH)]
@@ -260,6 +268,7 @@
         ),
         out_shape=[jax.ShapeDtypeStruct((ROWS, width), BF16) for width in widths],
         compiler_params=pltpu.CompilerParams(vmem_limit_bytes=58 * MIB),
+        cost_estimate=pl.CostEstimate(flops=2**35, bytes_accessed=2**20, transcendentals=0),
         name="products",
     )(where, inverses, firsts, nexts, columns, *relay)
 
@@ -271,17 +280,69 @@
 )
 
 
-def final_kernel(
-    where_ref, front_ref, zero_ref, one_ref, two_ref, three_ref, across_groups_ref, child_ref, schur_ref,
-    held_ref, product_ref, block_ref, read_sems, child_sems, write_sems,
-):
-    r, z = where_ref[0], where_ref[1]
-    target = r * 8 + z
+def wanted_child(where_ref, target):
     found, child = jnp.int32(0), jnp.int32(0)
     for b in range(CHILD_BLOCKS):
         hit = (where_ref[2 + b] == target).astype(jnp.int32)
         found, child = found + hit, child + hit * b
-    turn = child % 3
+    return found > 0, child
+
+
+def carried_group(r):
+    return jnp.where((r == 0) | (r == 3), 3, 2)
+
+
+def join_kernel(where_ref, child_ref, half_ref, sems):
+    r, z = where_ref[0], where_ref[1]
+    found, child = wanted_child(where_ref, carried_group(r) * 8 + z)
+
+    def copies(j):
+        return [
+            pltpu.make_async_copy(
+                child_ref.at[z_from, pl.ds(part * CHILD_ROWS + start, rows), :],
+                half_ref.at[pl.ds(place, rows), pl.ds(part * THIRD, THIRD)],
+                sems.at[i, part],
+            )
+            for i, (z_from, start, rows, place) in enumerate(PIECES[j])
+            for part in range(3)
+        ]
+
+    half_ref[...] = jnp.zeros_like(half_ref)
+    for j in range(3):
+        @pl.when(found & (child % 3 == j))
+        def _():
+            for copy in copies(j):
+                copy.start()
+            for copy in copies(j):
+                copy.wait()
+
+
+def join(where, children):
+    return pl.pallas_call(
+        join_kernel,
+        grid_spec=pltpu.PrefetchScalarGridSpec(
+            num_scalar_prefetch=1,
+            grid=(1,),
+            in_specs=[pl.BlockSpec(memory_space=pl.ANY)],
+            out_specs=pl.BlockSpec((ROWS, HALF), lambda i, w: (0, 0)),
+            scratch_shapes=[pltpu.SemaphoreType.DMA((4, 3))],
+        ),
+        out_shape=jax.ShapeDtypeStruct((ROWS, HALF), BF16),
+        compiler_params=pltpu.CompilerParams(vmem_limit_bytes=8 * MIB),
+        name="join",
+    )(where, children)
+
+
+def final_kernel(
+    where_ref, front_ref, zero_ref, one_ref, two_ref, three_ref, across_groups_ref, left_ref, right_ref, schur_ref,
+    held_ref, product_ref, block_ref, read_sems, child_sems, write_sems,
+):
+    r, z = where_ref[0], where_ref[1]
+    found, _ = wanted_child(where_ref, r * 8 + z)
+    halves = [
+        pltpu.make_async_copy(ref, block_ref.at[:, pl.ds(half * HALF, HALF)], child_sems.at[half])
+        for half, ref in enumerate((left_ref, right_ref))
+    ]
 
     def read_front(g):
         place = pl.ds((g + 1) * GROUP, GROUP)
@@ -302,17 +363,6 @@
         place = pl.ds(g * GROUP, GROUP)
         return pltpu.make_async_copy(held_ref.at[g], schur_ref.at[0, :, place], write_sems.at[g])
 
-    def read_child(j):
-        return [
-            pltpu.make_async_copy(
-                child_ref.at[z_from, pl.ds(part * CHILD_ROWS + start, rows), :],
-                block_ref.at[pl.ds(place, rows), pl.ds(part * WIDTH, WIDTH)],
-                child_sems.at[i, part],
-            )
-            for i, (z_from, start, rows, place) in enumerate(PIECES[j])
-            for part in range(3)
-        ]
-
     for g in range(3):
         read_front(g).start()
         for k in range(4):
@@ -320,11 +370,8 @@
             def _():
                 for copy in read_product(g, k):
                     copy.start()
-    for j in range(3):
-        @pl.when((found > 0) & (turn == j))
-        def _():
-            for copy in read_child(j):
-                copy.start()
+    for copy in halves:
+        copy.start()
 
     for g in range(3):
         read_front(g).wait()
@@ -333,15 +380,12 @@
             place = pl.ds(pl.multiple_of((z + 1 + i) % 8 * ROWS, ROWS), ROWS)
             held_ref[g, :, place] -= product_ref[g, :, i * ROWS : (i + 1) * ROWS].astype(F32)
         if g == 1:
-            for j in range(3):
-                @pl.when((found > 0) & (turn == j))
-                def _():
-                    for copy in read_child(j):
-                        copy.wait()
+            for copy in halves:
+                copy.wait()
         if g >= 1:
             for b in range(CHILD_BLOCKS):
                 parent = where_ref[2 + b]
-                @pl.when((found > 0) & (parent // 8 == g + 1))
+                @pl.when(found & (parent // 8 == g + 1))
                 def _():
                     place = pl.ds(pl.multiple_of((parent % 8) * ROWS, ROWS), ROWS)
                     held_ref[g, :, place] += block_ref[:, b * ROWS : (b + 1) * ROWS].astype(F32)
@@ -350,37 +394,35 @@
         write(g).wait()
 
 
-def final(where, assembled, pieces, children):
+def final(where, assembled, pieces, halves):
     return pl.pallas_call(
         final_kernel,
         grid_spec=pltpu.PrefetchScalarGridSpec(
             num_scalar_prefetch=1,
             grid=(1,),
-            in_specs=[pl.BlockSpec(memory_space=pl.ANY)] * 7,
+            in_specs=[pl.BlockSpec(memory_space=pl.ANY)] * 8,
             out_specs=pl.BlockSpec(memory_space=pl.ANY),
             scratch_shapes=[
                 pltpu.VMEM((3, ROWS, GROUP), F32),
                 pltpu.VMEM((3, ROWS, GROUP), BF16),
                 pltpu.VMEM((ROWS, CHILD), BF16),
                 pltpu.SemaphoreType.DMA((2, 3)),
-                pltpu.SemaphoreType.DMA((4, 3)),
+                pltpu.SemaphoreType.DMA((2,)),
                 pltpu.SemaphoreType.DMA((3,)),
             ],
         ),
         out_shape=jax.ShapeDtypeStruct((1, ROWS, 3 * GROUP), F32),
         compiler_params=pltpu.CompilerParams(vmem_limit_bytes=8 * MIB),
         name="final",
-    )(where, assembled, *pieces, children)
+    )(where, assembled, *pieces, *halves)
 
 
 def wanted_kernel(where_ref, parts_ref, out_ref, sems):
-    r = where_ref[0]
+    group = carried_group(where_ref[0])
     copies = []
     for z in range(8):
-        child = jnp.int32(0)
-        for b in range(CHILD_BLOCKS):
-            child = child + jnp.where(where_ref[2 + b] == r * 8 + z, b, 0)
-        source = parts_ref.at[jnp.minimum(child // 3, 3), pl.ds(ROWS, 3 * CHILD_ROWS), :]
+        _, child = wanted_child(where_ref, group * 8 + z)
+        source = parts_ref.at[jnp.minimum(child // 3, 3), pl.ds(2 * ROWS, 3 * CHILD_ROWS), :]
         copies.append(pltpu.make_async_copy(source, out_ref.at[z], sems.at[z]))
         copies[z].start()
     for copy in copies:
@@ -393,11 +435,11 @@
         grid_spec=pltpu.PrefetchScalarGridSpec(
             num_scalar_prefetch=1,
             grid=(1,),
-            in_specs=[pl.BlockSpec((4, PART_ROWS, WIDTH), lambda i, w: (0, 0, 0))],
+            in_specs=[pl.BlockSpec((4, PART_ROWS, THIRD), lambda i, w: (0, 0, 0))],
             out_specs=pl.BlockSpec(memory_space=pl.ANY),
             scratch_shapes=[pltpu.SemaphoreType.DMA((8,))],
         ),
-        out_shape=jax.ShapeDtypeStruct((8, 3 * CHILD_ROWS, WIDTH), BF16),
+        out_shape=jax.ShapeDtypeStruct((8, 3 * CHILD_ROWS, THIRD), BF16),
         compiler_params=pltpu.CompilerParams(vmem_limit_bytes=8 * MIB),
         name="wanted",
     )(where, parts)
@@ -426,7 +468,7 @@
     )
     relay = mine, beside, across
     pieces = wanted(where, parts)
-    relay, pieces = lax.optimization_barrier((relay, pieces))
+    beside, pieces = lax.optimization_barrier((beside, pieces))
     children = lax.all_to_all(pieces, "col", 0, 0)
 
     zero, one, two, three, across_groups = products(where, inverses, firsts, parts, columns, relay)
@@ -435,7 +477,9 @@
     one = lax.ppermute(one, "row", [(i, (i + 1) % 4) for i in range(1, 4)])
     three = lax.ppermute(three, "row", [(i, (i + 3) % 4) for i in range(1, 4)])
     pieces = zero, one, two, three, across_groups
-    return factor, final(where, assembled, pieces, children)
+    left = join(where, children)
+    right = lax.ppermute(left, "row", [(1, 2), (0, 3)])
+    return factor, final(where, assembled, pieces, (left, right))
 
 
 def solution(mesh):

time: 120 us -> 116 us (0.967)
  waiting for transfers between devices: 37.3 us -> 24.3 us
  starting transfers between devices: 34.7 us -> 39.5 us
  local copies, waits for them, and re-layouts: 0.78 us -> 4.42 us
    all_to_all x1, waiting for transfers between devices: 18.3 us -> 5.63 us  [on_device(): children = lax.all_to_all(pieces, 'col', 0, 0)]
    ppermute x1, waiting for transfers between devices: 0.69 us -> 7.56 us  [on_device(): two = lax.ppermute(two, 'row', [(i, (i + 2) % 4) for i in range(1, 4)])]
    all_to_all x1, waiting for transfers between devices: 5.28 us -> 0.01 us  [on_device(): parts = lax.all_to_all(pack(both, child), 'row', 0, 0)]
    ppermute x0 -> x1, starting transfers between devices: none -> 4.84 us  [on_device(): right = lax.ppermute(left, 'row', [(1, 2), (0, 3)])]
    unnamed x36, local copies, waits for them, and re-layouts: 0.77 us -> 4.41 us
  transfers between devices with their start and end apart: 10 -> 11, of which waited for: 6 -> 4; matrix products, arithmetic and copies ran while one was open for 0% -> 0% of each run, Pallas kernels for 11% -> 11%
where the time goes in v6:
time: 116 us; the launch traced here: 115 us
  starting transfers between devices  39.5 us (34%)
  waiting for transfers between devices  24.3 us (21%)
  Pallas kernels  18.7 us (16%)
  between operations  14.3 us (12%)
  blocking collectives  14.1 us (12%)
  local copies, waits for them, and re-layouts  4.42 us (4%)
    all_gather x1, blocking collectives, on_device(): firsts = lax.all_gather(first, 'row', axis=0)  14.1 us
    ppermute x1, starting transfers between devices, on_device(): child = lax.ppermute(update[0], 'front', [(i, i ^ 1) for i in range(16)])  8.79 us
    all_to_all x1, starting transfers between devices, on_device(): children = lax.all_to_all(pieces, 'col', 0, 0)  8.29 us
    pallas_call x1, Pallas kernels, products(): pl.pallas_call(product_kernel, grid_spec=pltpu.PrefetchScalarGridSpec(num...  7.57 us
    ppermute x1, waiting for transfers between devices, on_device(): two = lax.ppermute(two, 'row', [(i, (i + 2) % 4) for i in range(1, 4)])  7.56 us
    ppermute x1, waiting for transfers between devices, on_device(): passed = lax.ppermute(top, 'col', [(4, 1), (5, 0), (6, 3), (7, 2)])  6.62 us
    all_to_all x1, waiting for transfers between devices, on_device(): children = lax.all_to_all(pieces, 'col', 0, 0)  5.63 us
    ppermute x1, starting transfers between devices, on_device(): right = lax.ppermute(left, 'row', [(1, 2), (0, 3)])  4.84 us
  transfers between devices with their start and end apart: 11, of which 4 were waited for; matrix products, arithmetic and copies ran while one was open for 0% of the time, Pallas kernels for 11%

profile of v6, /device:TPU:1, one launch (start us, length us, event | category | flops | bytes accessed | tf_op | source)
XLA Modules:
  0.0 115.5 jit_solution(12946774802205276125)
XLA Ops:
  7.2 0.0 copy-start.17
  7.2 0.0 copy-start.16
  7.2 0.0 all-gather.4.cloned.1.call-start
  7.2 2.4 %first_panel.1 = (bf16[128,1024]{1,0:T(8,128)(2,1)}, bf16[128,512]{1,0:T(8,128)(2,1)}) custom-call(f32[1,128,4096]{2,1,0:T(8,128)} %front_ref.5, bf16[1,2,512,512]{3,2,1,0:T(8,128)(2,1)} %inverse_ref.5), custom_call_target="tpu_custom_call" | custom-call | tf_op jit(solution)/shard_map/first_panel/pallas_call | solution.py:51
  9.6 0.0 all-gather.4.cloned.1.call-update
  9.6 0.0 copy-done.17
  9.6 8.8 %collective-permute-start = (bf16[48,1536]{1,0:T(8,128)(2,1)S(1)}, bf16[48,1536]{1,0:T(8,128)(2,1)S(1)}, u32[]{:S(2)}, u32[]{:S(2)}) collective-permute-start(bf16[48,1536]{1,0:T(8,128)(2,1)S(1)} %bitcast.10), channel_id=1, source_target_pairs={{0,32},{32,0},{64,96},{96,64},{128,160},{160,128},{192,224},{224,1... | collective-permute-start | bytes 442376 | tf_op jit(solution)/shard_map/ppermute | solution.py:455
  18.4 14.1 %all-gather = bf16[512,512]{1,0:T(8,128)(2,1)S(1)} all-gather(bf16[128,512]{1,0:T(8,128)(2,1)} %get-tuple-element.15.first_ref), channel_id=2, replica_groups=mesh['front'=16,'row'=4,'col'=8] {'row'}, dimensions={0}, use_global_device_ids=true | all-gather | bytes 655360 | tf_op jit(solution)/shard_map/all_gather | solution.py:456
  32.5 0.0 collective-permute-done.child_ref
  32.5 1.3 %collective-permute-start.1 = (bf16[128,512]{1,0:T(8,128)(2,1)S(1)}, bf16[128,512]{1,0:T(8,128)(2,1)S(1)}, u32[]{:S(2)}, u32[]{:S(2)}) collective-permute-start(bf16[128,512]{1,0:T(8,128)(2,1)S(1)} %slice.5), channel_id=1, source_target_pairs={{4,1},{5,0},{6,3},{7,2},{12,9},{13,8},{14,11},{15,10},{20,17},{21,... | collective-permute-start | bytes 393224 | tf_op jit(solution)/shard_map/ppermute | solution.py:461
  33.9 0.0 copy-done.16
  33.9 0.1 pad_add_fusion.where_ref
  33.9 0.9 copy-done.3
  34.9 0.9 pack.1
  35.8 3.6 %all-to-all-start = ((bf16[4,400,256]{2,1,0:T(8,128)(2,1)}), bf16[4,400,256]{2,1,0:T(8,128)(2,1)S(1)}, u32[]{:S(2)}, u32[]{:S(2)}) async-start(bf16[4,400,256]{2,1,0:T(8,128)(2,1)} %pack.1), calls=%async_computation | async-start | bytes 1638400 | tf_op jit(solution)/shard_map/all_to_all | solution.py:460
  39.5 6.6 %collective-permute-done.1.passed_ref = bf16[128,512]{1,0:T(8,128)(2,1)S(1)} collective-permute-done((bf16[128,512]{1,0:T(8,128)(2,1)S(1)}, bf16[128,512]{1,0:T(8,128)(2,1)S(1)}, u32[]{:S(2)}, u32[]{:S(2)}) %collective-permute-start.1) | collective-permute-done | bytes 131104 | tf_op jit(solution)/shard_map/ppermute | solution.py:461
  46.1 0.6 first_relay.1.mine_ref
  46.7 0.0 copy-done.4
  46.7 0.0 copy-start.6
  46.7 4.4 %collective-permute-start.2 = (bf16[128,512]{1,0:T(8,128)(2,1)S(1)}, bf16[128,512]{1,0:T(8,128)(2,1)S(1)}, u32[]{:S(2)}, u32[]{:S(2)}) collective-permute-start(bf16[128,512]{1,0:T(8,128)(2,1)S(1)} %first_relay.1.mine_ref), channel_id=1, source_target_pairs={{0,1},{1,0},{2,3},{3,2},{4,5},{5,4},{6,7},{7,6},{8,9},{9,8},{10,11... | collective-permute-start | bytes 393224 | tf_op jit(solution)/shard_map/ppermute | solution.py:463
  51.1 4.4 %collective-permute-done.2.beside_ref = bf16[128,512]{1,0:T(8,128)(2,1)S(1)} collective-permute-done((bf16[128,512]{1,0:T(8,128)(2,1)S(1)}, bf16[128,512]{1,0:T(8,128)(2,1)S(1)}, u32[]{:S(2)}, u32[]{:S(2)}) %collective-permute-start.2) | collective-permute-done | bytes 131104 | tf_op jit(solution)/shard_map/ppermute | solution.py:463
  55.6 4.3 %collective-permute-start.3 = (bf16[256,512]{1,0:T(8,128)(2,1)S(1)}, bf16[256,512]{1,0:T(8,128)(2,1)S(1)}, u32[]{:S(2)}, u32[]{:S(2)}) collective-permute-start(bf16[256,512]{1,0:T(8,128)(2,1)S(1)} %pad_maximum_fusion), channel_id=1, source_target_pairs={{0,7},{1,2},{2,1},{3,4},{4,3},{5,6},{6,5},{7,0},{8,15},{9,10},{10,... | collective-permute-start | bytes 786440 | tf_op jit(solution)/shard_map/ppermute | solution.py:464
  59.9 0.0 all-to-all-done.nexts_ref.parts_ref
  59.9 0.0 copy-done.14
  59.9 0.0 copy-start.2
  59.9 1.5 %wanted.1 = bf16[8,144,256]{2,1,0:T(8,128)(2,1)} custom-call(s32[14]{0:T(128)S(1)} %pad_add_fusion.where_ref, bf16[4,400,256]{2,1,0:T(8,128)(2,1)S(1)} %all-to-all-done.nexts_ref.parts_ref), custom_call_target="tpu_custom_call" | custom-call | tf_op jit(solution)/shard_map/wanted/pallas_call | solution.py:433
  61.4 8.3 %all-to-all-start.1 = ((bf16[8,144,256]{2,1,0:T(8,128)(2,1)}), bf16[8,144,256]{2,1,0:T(8,128)(2,1)}, u32[]{:S(2)}, u32[]{:S(2)}) async-start(bf16[8,144,256]{2,1,0:T(8,128)(2,1)} %wanted.1), calls=%async_computation.1 | async-start | bytes 1179648 | tf_op jit(solution)/shard_map/all_to_all | solution.py:472
  69.7 0.0 collective-permute-done.3.across_ref
  69.7 0.0 all-gather.4.cloned.1.call-done
  69.8 0.0 copy-done.2
  69.8 0.7 copy-done.10
  70.4 0.0 copy-start.1
  70.5 7.6 %products.1 = (bf16[128,1024]{1,0:T(8,128)(2,1)}, bf16[128,896]{1,0:T(8,128)(2,1)}, bf16[128,896]{1,0:T(8,128)(2,1)}, bf16[128,896]{1,0:T(8,128)(2,1)}, bf16[128,512]{1,0:T(8,128)(2,1)}) custom-call(s32[14]{0:T(128)} %copy-done.14, bf16[1,2,512,512]{3,2,1,0:T(8,128)(2,1)} %inverse_ref.5, bf16[4,128,512]{2,1,0:T(8,128)(2,1)} %bitcast.7, ...), custom_call_target="tpu_custom_call" | custom-call | flops 34359738368 | bytes 1048576 | tf_op jit(solution)/shard_map/products/pallas_call | solution.py:251
  78.0 1.3 %collective-permute-start.4 = (bf16[128,896]{1,0:T(8,128)(2,1)}, bf16[128,896]{1,0:T(8,128)(2,1)S(1)}, u32[]{:S(2)}, u32[]{:S(2)}) collective-permute-start(bf16[128,896]{1,0:T(8,128)(2,1)} %get-tuple-element.21), channel_id=1, source_target_pairs={{8,16},{16,24},{24,0},{9,17},{17,25},{25,1},{10,18},{18,26},{26,2}... | collective-permute-start | bytes 688136 | tf_op jit(solution)/shard_map/ppermute | solution.py:477
  79.3 1.3 %collective-permute-start.5 = (bf16[128,896]{1,0:T(8,128)(2,1)}, bf16[128,896]{1,0:T(8,128)(2,1)}, u32[]{:S(2)}, u32[]{:S(2)}) collective-permute-start(bf16[128,896]{1,0:T(8,128)(2,1)} %get-tuple-element.22), channel_id=1, source_target_pairs={{8,24},{16,0},{24,8},{9,25},{17,1},{25,9},{10,26},{18,2},{26,10},{... | collective-permute-start | bytes 688136 | tf_op jit(solution)/shard_map/ppermute | solution.py:476
  80.6 1.3 %collective-permute-start.6 = (bf16[128,896]{1,0:T(8,128)(2,1)}, bf16[128,896]{1,0:T(8,128)(2,1)}, u32[]{:S(2)}, u32[]{:S(2)}) collective-permute-start(bf16[128,896]{1,0:T(8,128)(2,1)} %get-tuple-element.23), channel_id=1, source_target_pairs={{8,0},{16,8},{24,16},{9,1},{17,9},{25,17},{10,2},{18,10},{26,18},{... | collective-permute-start | bytes 688136 | tf_op jit(solution)/shard_map/ppermute | solution.py:478
  81.9 5.6 %all-to-all-done.1.child_ref = bf16[8,144,256]{2,1,0:T(8,128)(2,1)} async-done(((bf16[8,144,256]{2,1,0:T(8,128)(2,1)}), bf16[8,144,256]{2,1,0:T(8,128)(2,1)}, u32[]{:S(2)}, u32[]{:S(2)}) %all-to-all-start.1) | async-done | bytes 589856 | tf_op jit(solution)/shard_map/all_to_all | solution.py:472
  87.6 0.7 join.1.left_ref
  88.3 4.8 %collective-permute-start.7 = (bf16[128,768]{1,0:T(8,128)(2,1)S(1)}, bf16[128,768]{1,0:T(8,128)(2,1)S(1)}, u32[]{:S(2)}, u32[]{:S(2)}) collective-permute-start(bf16[128,768]{1,0:T(8,128)(2,1)S(1)} %join.1.left_ref), channel_id=1, source_target_pairs={{8,16},{0,24},{9,17},{1,25},{10,18},{2,26},{11,19},{3,27},{12,20},... | collective-permute-start | bytes 589832 | tf_op jit(solution)/shard_map/ppermute | solution.py:481
  93.2 0.9 copy-done.7
  94.1 0.9 copy-done.9
  95.0 0.9 copy-done.11
  96.0 1.9 %own_factor.1 = bf16[1,128,1024]{2,1,0:T(8,128)(2,1)} custom-call(s32[14]{0:T(128)S(1)} %copy-done.15, f32[1,128,4096]{2,1,0:T(8,128)S(1)} %copy-done, bf16[1,2,512,512]{3,2,1,0:T(8,128)(2,1)S(1)} %copy-done.1, bf16[128,512]{1,0:T(8,128)(2,1)S(1)} %copy-done.5, bf16[128,512]{1,0:T(8,128)(2,1)S(1)} %copy-done.7, bf16[128,512]{1,0:T(8,128)(2,1)S(1)} %copy-done.9, ...), custom_call_target="tpu_custom_call" | custom-call | flops 268435456 | bytes 2097152 | tf_op jit(solution)/shard_map/own_factor/pallas_call | solution.py:151
  97.9 0.0 collective-permute-done.7.right_ref
  97.9 0.0 collective-permute-done.4.one_ref
  97.9 7.6 %collective-permute-done.5.two_ref = bf16[128,896]{1,0:T(8,128)(2,1)} collective-permute-done((bf16[128,896]{1,0:T(8,128)(2,1)}, bf16[128,896]{1,0:T(8,128)(2,1)}, u32[]{:S(2)}, u32[]{:S(2)}) %collective-permute-start.5) | collective-permute-done | bytes 229408 | tf_op jit(solution)/shard_map/ppermute | solution.py:476
  105.5 0.0 collective-permute-done.6.three_ref
  105.5 3.1 %final.1 = f32[1,128,3072]{2,1,0:T(8,128)} custom-call(s32[14]{0:T(128)S(1)} %copy-done.15, f32[1,128,4096]{2,1,0:T(8,128)S(1)} %copy-done, bf16[128,1024]{1,0:T(8,128)(2,1)S(1)} %copy-done.12, bf16[128,896]{1,0:T(8,128)(2,1)S(1)} %collective-permute-done.4.one_ref, bf16[128,896]{1,0:T(8,128)(2,1)} %collective-permute-done.5.two_ref, ...), custom_call_target="tpu_custom_call" | custom-call | tf_op jit(solution)/shard_map/final/pallas_call | solution.py:398
  (23 shorter events, 0.1 us)
Async XLA Ops:
  7.2 2.4 %copy-start.17 = (bf16[1,48,1536]{2,1,0:T(8,128)(2,1)S(1)}, bf16[1,48,1536]{2,1,0:T(8,128)(2,1)}, u32[]{:S(2)}) copy-start(bf16[1,48,1536]{2,1,0:T(8,128)(2,1)} %param.5) | copy-start | bytes 442372
  7.2 26.7 %copy-start.16 = (s32[1,12]{1,0:T(1,128)S(1)}, s32[1,12]{1,0:T(1,128)}, u32[]{:S(2)}) copy-start(s32[1,12]{1,0:T(1,128)} %param.6) | copy-start | bytes 148
  7.2 62.6 %all-gather.4.cloned.1.call-start = ((), (), s32[]{:S(2)}) async-start(), calls=%async_computation.2 | async-start | bytes 2359296 | tf_op jit(solution)/shard_map/all_gather | solution.py:453
  9.6 22.9 %collective-permute-start = (bf16[48,1536]{1,0:T(8,128)(2,1)S(1)}, bf16[48,1536]{1,0:T(8,128)(2,1)S(1)}, u32[]{:S(2)}, u32[]{:S(2)}) collective-permute-start(bf16[48,1536]{1,0:T(8,128)(2,1)S(1)} %bitcast.10), channel_id=1, source_target_pairs={{0,32},{32,0},{64,96},{96,64},{128,160},{160,128},{192,224},{224,1... | collective-permute-start | bytes 442376 | tf_op jit(solution)/shard_map/ppermute | solution.py:455
  32.5 14.1 %copy-start.4 = (bf16[512,512]{1,0:T(8,128)(2,1)}, bf16[512,512]{1,0:T(8,128)(2,1)S(1)}, u32[]{:S(2)}) copy-start(bf16[512,512]{1,0:T(8,128)(2,1)S(1)} %all-gather) | copy-start | bytes 1572868
  32.5 13.6 %collective-permute-start.1 = (bf16[128,512]{1,0:T(8,128)(2,1)S(1)}, bf16[128,512]{1,0:T(8,128)(2,1)S(1)}, u32[]{:S(2)}, u32[]{:S(2)}) collective-permute-start(bf16[128,512]{1,0:T(8,128)(2,1)S(1)} %slice.5), channel_id=1, source_target_pairs={{4,1},{5,0},{6,3},{7,2},{12,9},{13,8},{14,11},{15,10},{20,17},{21,... | collective-permute-start | bytes 393224 | tf_op jit(solution)/shard_map/ppermute | solution.py:461
  33.9 1.0 copy-start.3
  34.9 25.0 %copy-start.14 = (s32[14]{0:T(128)}, s32[14]{0:T(128)S(1)}, u32[]{:S(2)}) copy-start(s32[14]{0:T(128)S(1)} %pad_add_fusion.where_ref) | copy-start | bytes 172
  35.8 24.1 %all-to-all-start = ((bf16[4,400,256]{2,1,0:T(8,128)(2,1)}), bf16[4,400,256]{2,1,0:T(8,128)(2,1)S(1)}, u32[]{:S(2)}, u32[]{:S(2)}) async-start(bf16[4,400,256]{2,1,0:T(8,128)(2,1)} %pack.1), calls=%async_computation | async-start | bytes 1638400 | tf_op jit(solution)/shard_map/all_to_all | solution.py:460
  46.7 23.7 %copy-start.6 = (bf16[128,512]{1,0:T(8,128)(2,1)}, bf16[128,512]{1,0:T(8,128)(2,1)S(1)}, u32[]{:S(2)}) copy-start(bf16[128,512]{1,0:T(8,128)(2,1)S(1)} %first_relay.1.mine_ref) | copy-start | bytes 393220
  46.7 8.9 %collective-permute-start.2 = (bf16[128,512]{1,0:T(8,128)(2,1)S(1)}, bf16[128,512]{1,0:T(8,128)(2,1)S(1)}, u32[]{:S(2)}, u32[]{:S(2)}) collective-permute-start(bf16[128,512]{1,0:T(8,128)(2,1)S(1)} %first_relay.1.mine_ref), channel_id=1, source_target_pairs={{0,1},{1,0},{2,3},{3,2},{4,5},{5,4},{6,7},{7,6},{8,9},{9,8},{10,11... | collective-permute-start | bytes 393224 | tf_op jit(solution)/shard_map/ppermute | solution.py:463
  55.6 14.9 %copy-start.8 = (bf16[128,512]{1,0:T(8,128)(2,1)}, bf16[128,512]{1,0:T(8,128)(2,1)S(1)}, u32[]{:S(2)}) copy-start(bf16[128,512]{1,0:T(8,128)(2,1)S(1)} %collective-permute-done.2.beside_ref) | copy-start | bytes 393220
  55.6 14.1 %collective-permute-start.3 = (bf16[256,512]{1,0:T(8,128)(2,1)S(1)}, bf16[256,512]{1,0:T(8,128)(2,1)S(1)}, u32[]{:S(2)}, u32[]{:S(2)}) collective-permute-start(bf16[256,512]{1,0:T(8,128)(2,1)S(1)} %pad_maximum_fusion), channel_id=1, source_target_pairs={{0,7},{1,2},{2,1},{3,4},{4,3},{5,6},{6,5},{7,0},{8,15},{9,10},{10,... | collective-permute-start | bytes 786440 | tf_op jit(solution)/shard_map/ppermute | solution.py:464
  59.9 9.8 %copy-start.2 = (bf16[4,400,256]{2,1,0:T(8,128)(2,1)}, bf16[4,400,256]{2,1,0:T(8,128)(2,1)S(1)}, u32[]{:S(2)}) copy-start(bf16[4,400,256]{2,1,0:T(8,128)(2,1)S(1)} %all-to-all-done.nexts_ref.parts_ref) | copy-start | bytes 2457604
  61.4 26.1 %all-to-all-start.1 = ((bf16[8,144,256]{2,1,0:T(8,128)(2,1)}), bf16[8,144,256]{2,1,0:T(8,128)(2,1)}, u32[]{:S(2)}, u32[]{:S(2)}) async-start(bf16[8,144,256]{2,1,0:T(8,128)(2,1)} %wanted.1), calls=%async_computation.1 | async-start | bytes 1179648 | tf_op jit(solution)/shard_map/all_to_all | solution.py:472
  69.7 0.7 copy-start.10
  70.4 17.1 %copy-start.15 = (s32[14]{0:T(128)S(1)}, s32[14]{0:T(128)}, u32[]{:S(2)}) copy-start(s32[14]{0:T(128)} %copy-done.14) | copy-start | bytes 172
  70.4 22.7 %copy-start = (f32[1,128,4096]{2,1,0:T(8,128)S(1)}, f32[1,128,4096]{2,1,0:T(8,128)}, u32[]{:S(2)}) copy-start(f32[1,128,4096]{2,1,0:T(8,128)} %front_ref.5) | copy-start | bytes 6291460
  70.4 22.7 %copy-start.1 = (bf16[1,2,512,512]{3,2,1,0:T(8,128)(2,1)S(1)}, bf16[1,2,512,512]{3,2,1,0:T(8,128)(2,1)}, u32[]{:S(2)}) copy-start(bf16[1,2,512,512]{3,2,1,0:T(8,128)(2,1)} %inverse_ref.5) | copy-start | bytes 3145732
  70.4 22.7 %copy-start.5 = (bf16[128,512]{1,0:T(8,128)(2,1)S(1)}, bf16[128,512]{1,0:T(8,128)(2,1)}, u32[]{:S(2)}) copy-start(bf16[128,512]{1,0:T(8,128)(2,1)} %get-tuple-element.15.first_ref) | copy-start | bytes 393220
  78.0 19.9 %collective-permute-start.4 = (bf16[128,896]{1,0:T(8,128)(2,1)}, bf16[128,896]{1,0:T(8,128)(2,1)S(1)}, u32[]{:S(2)}, u32[]{:S(2)}) collective-permute-start(bf16[128,896]{1,0:T(8,128)(2,1)} %get-tuple-element.21), channel_id=1, source_target_pairs={{8,16},{16,24},{24,0},{9,17},{17,25},{25,1},{10,18},{18,26},{26,2}... | collective-permute-start | bytes 688136 | tf_op jit(solution)/shard_map/ppermute | solution.py:477
  79.3 26.1 %collective-permute-start.5 = (bf16[128,896]{1,0:T(8,128)(2,1)}, bf16[128,896]{1,0:T(8,128)(2,1)}, u32[]{:S(2)}, u32[]{:S(2)}) collective-permute-start(bf16[128,896]{1,0:T(8,128)(2,1)} %get-tuple-element.22), channel_id=1, source_target_pairs={{8,24},{16,0},{24,8},{9,25},{17,1},{25,9},{10,26},{18,2},{26,10},{... | collective-permute-start | bytes 688136 | tf_op jit(solution)/shard_map/ppermute | solution.py:476
  80.6 24.8 %collective-permute-start.6 = (bf16[128,896]{1,0:T(8,128)(2,1)}, bf16[128,896]{1,0:T(8,128)(2,1)}, u32[]{:S(2)}, u32[]{:S(2)}) collective-permute-start(bf16[128,896]{1,0:T(8,128)(2,1)} %get-tuple-element.23), channel_id=1, source_target_pairs={{8,0},{16,8},{24,16},{9,1},{17,9},{25,17},{10,2},{18,10},{26,18},{... | collective-permute-start | bytes 688136 | tf_op jit(solution)/shard_map/ppermute | solution.py:478
  88.3 9.6 %collective-permute-start.7 = (bf16[128,768]{1,0:T(8,128)(2,1)S(1)}, bf16[128,768]{1,0:T(8,128)(2,1)S(1)}, u32[]{:S(2)}, u32[]{:S(2)}) collective-permute-start(bf16[128,768]{1,0:T(8,128)(2,1)S(1)} %join.1.left_ref), channel_id=1, source_target_pairs={{8,16},{0,24},{9,17},{1,25},{10,18},{2,26},{11,19},{3,27},{12,20},... | collective-permute-start | bytes 589832 | tf_op jit(solution)/shard_map/ppermute | solution.py:481
  93.2 0.9 copy-start.7
  94.1 0.9 copy-start.9
  95.0 0.9 copy-start.11
  96.0 9.5 %copy-start.12 = (bf16[128,1024]{1,0:T(8,128)(2,1)S(1)}, bf16[128,1024]{1,0:T(8,128)(2,1)}, u32[]{:S(2)}) copy-start(bf16[128,1024]{1,0:T(8,128)(2,1)} %get-tuple-element.20.zero_ref) | copy-start | bytes 786436
  96.0 9.5 %copy-start.13 = (bf16[128,512]{1,0:T(8,128)(2,1)S(1)}, bf16[128,512]{1,0:T(8,128)(2,1)}, u32[]{:S(2)}) copy-start(bf16[128,512]{1,0:T(8,128)(2,1)} %get-tuple-element.24.across_groups_ref) | copy-start | bytes 393220
Sparse Core Ops, SparseCore 0:
  10.7 53.1 all-gather.3

commit v7 on v6

--- a/solution.py
+++ b/solution.py
@@ -40,8 +40,15 @@
     return total
 
 
+def upper(product, a, b):
+    half = WIDTH // 2
+    left = product(a[..., :half], b[:half, :half])
+    return jnp.concatenate([left, product(a, b[:, half:])], axis=1)
+
+
 def first_kernel(front_ref, inverse_ref, both_ref, first_ref):
-    first = dot_split(front_ref[0, :, :WIDTH], inverse_ref[0, 0], 3).astype(BF16)
+    split = lambda a, b: dot_split(a, b, 3)
+    first = upper(split, front_ref[0, :, :WIDTH], inverse_ref[0, 0]).astype(BF16)
     both_ref[:, :WIDTH] = first
     both_ref[:, WIDTH:] = front_ref[0, :, WIDTH:].astype(BF16)
     first_ref[...] = first
@@ -221,28 +228,35 @@
 
     def panel_of(first, following):
         lost = dot(first, weight_ref[0]) + dot(first, weight_ref[1])
-        return dot(following, inverse) - lost
+        return upper(dot, following, inverse) - lost
 
     await_all(rows_ref.at[:, pl.ds(0, WIDTH)], sems.at[2])
     await_all(next_ref, sems.at[3])
-    panel = panel_of(rows_ref[:, :WIDTH], next_ref[...])
-    top = jnp.where(z < 4, (4 - r) % 4, 4)
-    above = lax.broadcasted_iota(jnp.int32, (4 * ROWS, WIDTH), 0) // ROWS == top
-    rows_ref[:, WIDTH:] = jnp.where(above, jnp.zeros_like(panel), panel).astype(BF16)
+    panel = panel_of(rows_ref[ROWS:, :WIDTH], next_ref[ROWS:, :])
+    above = lax.broadcasted_iota(jnp.int32, (3 * ROWS, WIDTH), 0) // ROWS == jnp.where(z < 4, 3 - r, 4)
+    rows_ref[ROWS:, WIDTH:] = jnp.where(above, jnp.zeros_like(panel), panel).astype(BF16)
     await_all(columns_ref.at[:, pl.ds(0, WIDTH)], sems.at[4])
     await_all(following_ref, sems.at[5])
     for half in range(2):
         place = pl.ds(half * 4 * ROWS, 4 * ROWS)
         panel = panel_of(columns_ref[place, :WIDTH], following_ref[place, :])
+        if half == 1:
+            last = lax.broadcasted_iota(jnp.int32, (4 * ROWS, WIDTH), 0) // ROWS
+            above = last == jnp.where((r == 0) & (z < 4), 3, 4)
+            panel = jnp.where(above, jnp.zeros_like(panel), panel)
         columns_ref[place, WIDTH:] = panel.astype(BF16)
+    rows_ref[:ROWS, WIDTH:] = columns_ref[7 * ROWS :, WIDTH:]
     for part in range(4):
         place = pl.ds(part * 256, 256)
-        total = dot_t(rows_ref[...], columns_ref[place, :]).astype(BF16)
+        exact = dot_t(rows_ref[...], columns_ref[place, :])
+        total = exact.astype(BF16)
         zero_ref[:, place] = total[:ROWS]
         width = min(256, SENT - part * 256)
         for k, ref in enumerate((one_ref, two_ref, three_ref), 1):
             ref[:, part * 256 : part * 256 + width] = total[k * ROWS : (k + 1) * ROWS, :width]
-    across_groups_ref[...] = dot_t(rows_ref[:ROWS, :], rows_ref[...]).astype(BF16)
+    for k in range(4):
+        place = slice(k * ROWS, (k + 1) * ROWS)
+        across_groups_ref[:, place] = exact[place, ROWS:].T.astype(BF16)
 
 
 def products(where, inverses, firsts, nexts, columns, relay):

time: 116 us -> 118 us (1.017)
  the two profiles are of different devices: /device:TPU:1 before, /device:TPU:68 now
where the time goes in v7:
time: 118 us; the launch traced here: 117 us
  waiting for transfers between devices  31.5 us (27%)
  starting transfers between devices  28.2 us (24%)
  blocking collectives  20.1 us (17%)
  Pallas kernels  18.5 us (16%)
  between operations  14.3 us (12%)
  local copies, waits for them, and re-layouts  4.42 us (4%)
    all_gather x1, blocking collectives, on_device(): firsts = lax.all_gather(first, 'row', axis=0)  20.1 us
    ppermute x1, waiting for transfers between devices, on_device(): passed = lax.ppermute(top, 'col', [(4, 1), (5, 0), (6, 3), (7, 2)])  10 us
    ppermute x1, waiting for transfers between devices, on_device(): two = lax.ppermute(two, 'row', [(i, (i + 2) % 4) for i in range(1, 4)])  8.71 us
    ppermute x1, waiting for transfers between devices, on_device(): beside = lax.ppermute(mine, 'col', [(i, i ^ 1) for i in range(8)])  7.8 us
    pallas_call x1, Pallas kernels, products(): pl.pallas_call(product_kernel, grid_spec=pltpu.PrefetchScalarGridSpec(num...  7.46 us
    ppermute x1, starting transfers between devices, on_device(): right = lax.ppermute(left, 'row', [(1, 2), (0, 3)])  6.39 us
    all_to_all x1, waiting for transfers between devices, on_device(): children = lax.all_to_all(pieces, 'col', 0, 0)  4.6 us
    ppermute x1, starting transfers between devices, on_device(): lax.ppermute(jnp.concatenate([mine, beside]), 'col', [(i, (i + 1) % 8 if...  4.58 us
  transfers between devices with their start and end apart: 11, of which 5 were waited for; matrix products, arithmetic and copies ran while one was open for 0% of the time, Pallas kernels for 11%

profile of v7, /device:TPU:68, one launch (start us, length us, event | category | flops | bytes accessed | tf_op | source)
XLA Modules:
  0.0 117.1 jit_solution(16555692148848388358)
XLA Ops:
  7.2 0.0 copy-start.17
  7.2 0.0 all-gather.4.cloned.1.call-start
  7.2 2.3 %first_panel.1 = (bf16[128,1024]{1,0:T(8,128)(2,1)}, bf16[128,512]{1,0:T(8,128)(2,1)}) custom-call(f32[1,128,4096]{2,1,0:T(8,128)} %front_ref.5, bf16[1,2,512,512]{3,2,1,0:T(8,128)(2,1)} %inverse_ref.5), custom_call_target="tpu_custom_call" | custom-call | tf_op jit(solution)/shard_map/first_panel/pallas_call | solution.py:58
  9.5 0.0 all-gather.4.cloned.1.call-update
  9.6 1.9 %collective-permute-start = (bf16[48,1536]{1,0:T(8,128)(2,1)S(1)}, bf16[48,1536]{1,0:T(8,128)(2,1)S(1)}, u32[]{:S(2)}, u32[]{:S(2)}) collective-permute-start(bf16[48,1536]{1,0:T(8,128)(2,1)S(1)} %bitcast.10), channel_id=1, source_target_pairs={{0,32},{32,0},{64,96},{96,64},{128,160},{160,128},{192,224},{224,1... | collective-permute-start | bytes 442376 | tf_op jit(solution)/shard_map/ppermute | solution.py:469
  11.5 20.1 %all-gather = bf16[512,512]{1,0:T(8,128)(2,1)S(1)} all-gather(bf16[128,512]{1,0:T(8,128)(2,1)} %get-tuple-element.15.first_ref), channel_id=2, replica_groups=mesh['front'=16,'row'=4,'col'=8] {'row'}, dimensions={0}, use_global_device_ids=true | all-gather | bytes 655360 | tf_op jit(solution)/shard_map/all_gather | solution.py:470
  31.6 0.0 collective-permute-done.child_ref
  31.6 1.3 %collective-permute-start.1 = (bf16[128,512]{1,0:T(8,128)(2,1)S(1)}, bf16[128,512]{1,0:T(8,128)(2,1)S(1)}, u32[]{:S(2)}, u32[]{:S(2)}) collective-permute-start(bf16[128,512]{1,0:T(8,128)(2,1)S(1)} %slice.5), channel_id=1, source_target_pairs={{4,1},{5,0},{6,3},{7,2},{12,9},{13,8},{14,11},{15,10},{20,17},{21,... | collective-permute-start | bytes 393224 | tf_op jit(solution)/shard_map/ppermute | solution.py:475
  32.9 0.1 pad_add_fusion.where_ref
  33.0 1.0 copy-done.3
  34.0 0.9 pack.1
  34.9 3.6 %all-to-all-start = ((bf16[4,400,256]{2,1,0:T(8,128)(2,1)}), bf16[4,400,256]{2,1,0:T(8,128)(2,1)S(1)}, u32[]{:S(2)}, u32[]{:S(2)}) async-start(bf16[4,400,256]{2,1,0:T(8,128)(2,1)} %pack.1), calls=%async_computation | async-start | bytes 1638400 | tf_op jit(solution)/shard_map/all_to_all | solution.py:474
  38.5 10.0 %collective-permute-done.1.passed_ref = bf16[128,512]{1,0:T(8,128)(2,1)S(1)} collective-permute-done((bf16[128,512]{1,0:T(8,128)(2,1)S(1)}, bf16[128,512]{1,0:T(8,128)(2,1)S(1)}, u32[]{:S(2)}, u32[]{:S(2)}) %collective-permute-start.1) | collective-permute-done | bytes 131104 | tf_op jit(solution)/shard_map/ppermute | solution.py:475
  48.6 0.6 first_relay.1.mine_ref
  49.1 0.0 copy-done.4
  49.2 0.0 copy-start.6
  49.2 1.9 %collective-permute-start.2 = (bf16[128,512]{1,0:T(8,128)(2,1)S(1)}, bf16[128,512]{1,0:T(8,128)(2,1)S(1)}, u32[]{:S(2)}, u32[]{:S(2)}) collective-permute-start(bf16[128,512]{1,0:T(8,128)(2,1)S(1)} %first_relay.1.mine_ref), channel_id=1, source_target_pairs={{0,1},{1,0},{2,3},{3,2},{4,5},{5,4},{6,7},{7,6},{8,9},{9,8},{10,11... | collective-permute-start | bytes 393224 | tf_op jit(solution)/shard_map/ppermute | solution.py:477
  51.1 7.8 %collective-permute-done.2.beside_ref = bf16[128,512]{1,0:T(8,128)(2,1)S(1)} collective-permute-done((bf16[128,512]{1,0:T(8,128)(2,1)S(1)}, bf16[128,512]{1,0:T(8,128)(2,1)S(1)}, u32[]{:S(2)}, u32[]{:S(2)}) %collective-permute-start.2) | collective-permute-done | bytes 131104 | tf_op jit(solution)/shard_map/ppermute | solution.py:477
  58.9 4.6 %collective-permute-start.3 = (bf16[256,512]{1,0:T(8,128)(2,1)S(1)}, bf16[256,512]{1,0:T(8,128)(2,1)S(1)}, u32[]{:S(2)}, u32[]{:S(2)}) collective-permute-start(bf16[256,512]{1,0:T(8,128)(2,1)S(1)} %pad_maximum_fusion), channel_id=1, source_target_pairs={{0,7},{1,2},{2,1},{3,4},{4,3},{5,6},{6,5},{7,0},{8,15},{9,10},{10,... | collective-permute-start | bytes 786440 | tf_op jit(solution)/shard_map/ppermute | solution.py:478
  63.5 0.0 all-to-all-done.nexts_ref.parts_ref
  63.5 0.0 copy-start.2
  63.5 1.5 %wanted.1 = bf16[8,144,256]{2,1,0:T(8,128)(2,1)} custom-call(s32[14]{0:T(128)S(1)} %pad_add_fusion.where_ref, bf16[4,400,256]{2,1,0:T(8,128)(2,1)S(1)} %all-to-all-done.nexts_ref.parts_ref), custom_call_target="tpu_custom_call" | custom-call | tf_op jit(solution)/shard_map/wanted/pallas_call | solution.py:447
  65.0 4.5 %all-to-all-start.1 = ((bf16[8,144,256]{2,1,0:T(8,128)(2,1)}), bf16[8,144,256]{2,1,0:T(8,128)(2,1)}, u32[]{:S(2)}, u32[]{:S(2)}) async-start(bf16[8,144,256]{2,1,0:T(8,128)(2,1)} %wanted.1), calls=%async_computation.1 | async-start | bytes 1179648 | tf_op jit(solution)/shard_map/all_to_all | solution.py:486
  69.6 0.0 collective-permute-done.3.across_ref
  69.6 0.0 all-gather.4.cloned.1.call-done
  69.6 0.7 copy-done.10
  70.3 0.0 copy-start.1
  70.3 7.5 %products.1 = (bf16[128,1024]{1,0:T(8,128)(2,1)}, bf16[128,896]{1,0:T(8,128)(2,1)}, bf16[128,896]{1,0:T(8,128)(2,1)}, bf16[128,896]{1,0:T(8,128)(2,1)}, bf16[128,512]{1,0:T(8,128)(2,1)}) custom-call(s32[14]{0:T(128)} %copy-done.14, bf16[1,2,512,512]{3,2,1,0:T(8,128)(2,1)} %inverse_ref.5, bf16[4,128,512]{2,1,0:T(8,128)(2,1)} %bitcast.7, ...), custom_call_target="tpu_custom_call" | custom-call | flops 34359738368 | bytes 1048576 | tf_op jit(solution)/shard_map/products/pallas_call | solution.py:265
  77.8 1.3 %collective-permute-start.4 = (bf16[128,896]{1,0:T(8,128)(2,1)}, bf16[128,896]{1,0:T(8,128)(2,1)S(1)}, u32[]{:S(2)}, u32[]{:S(2)}) collective-permute-start(bf16[128,896]{1,0:T(8,128)(2,1)} %get-tuple-element.21), channel_id=1, source_target_pairs={{8,16},{16,24},{24,0},{9,17},{17,25},{25,1},{10,18},{18,26},{26,2}... | collective-permute-start | bytes 688136 | tf_op jit(solution)/shard_map/ppermute | solution.py:491
  79.1 1.3 %collective-permute-start.5 = (bf16[128,896]{1,0:T(8,128)(2,1)}, bf16[128,896]{1,0:T(8,128)(2,1)}, u32[]{:S(2)}, u32[]{:S(2)}) collective-permute-start(bf16[128,896]{1,0:T(8,128)(2,1)} %get-tuple-element.22), channel_id=1, source_target_pairs={{8,24},{16,0},{24,8},{9,25},{17,1},{25,9},{10,26},{18,2},{26,10},{... | collective-permute-start | bytes 688136 | tf_op jit(solution)/shard_map/ppermute | solution.py:490
  80.4 1.3 %collective-permute-start.6 = (bf16[128,896]{1,0:T(8,128)(2,1)}, bf16[128,896]{1,0:T(8,128)(2,1)}, u32[]{:S(2)}, u32[]{:S(2)}) collective-permute-start(bf16[128,896]{1,0:T(8,128)(2,1)} %get-tuple-element.23), channel_id=1, source_target_pairs={{8,0},{16,8},{24,16},{9,1},{17,9},{25,17},{10,2},{18,10},{26,18},{... | collective-permute-start | bytes 688136 | tf_op jit(solution)/shard_map/ppermute | solution.py:492
  81.7 4.6 %all-to-all-done.1.child_ref = bf16[8,144,256]{2,1,0:T(8,128)(2,1)} async-done(((bf16[8,144,256]{2,1,0:T(8,128)(2,1)}), bf16[8,144,256]{2,1,0:T(8,128)(2,1)}, u32[]{:S(2)}, u32[]{:S(2)}) %all-to-all-start.1) | async-done | bytes 589856 | tf_op jit(solution)/shard_map/all_to_all | solution.py:486
  86.3 0.7 join.1.left_ref
  87.0 6.4 %collective-permute-start.7 = (bf16[128,768]{1,0:T(8,128)(2,1)S(1)}, bf16[128,768]{1,0:T(8,128)(2,1)S(1)}, u32[]{:S(2)}, u32[]{:S(2)}) collective-permute-start(bf16[128,768]{1,0:T(8,128)(2,1)S(1)} %join.1.left_ref), channel_id=1, source_target_pairs={{8,16},{0,24},{9,17},{1,25},{10,18},{2,26},{11,19},{3,27},{12,20},... | collective-permute-start | bytes 589832 | tf_op jit(solution)/shard_map/ppermute | solution.py:495
  93.4 0.0 copy-done
  93.4 0.0 copy-done.1
  93.4 0.0 copy-done.5
  93.4 0.0 copy-start.7
  93.5 0.9 copy-done.7
  94.4 0.9 copy-done.9
  95.3 0.9 copy-done.11
  96.2 1.9 %own_factor.1 = bf16[1,128,1024]{2,1,0:T(8,128)(2,1)} custom-call(s32[14]{0:T(128)S(1)} %copy-done.15, f32[1,128,4096]{2,1,0:T(8,128)S(1)} %copy-done, bf16[1,2,512,512]{3,2,1,0:T(8,128)(2,1)S(1)} %copy-done.1, bf16[128,512]{1,0:T(8,128)(2,1)S(1)} %copy-done.5, bf16[128,512]{1,0:T(8,128)(2,1)S(1)} %copy-done.7, bf16[128,512]{1,0:T(8,128)(2,1)S(1)} %copy-done.9, ...), custom_call_target="tpu_custom_call" | custom-call | flops 268435456 | bytes 2097152 | tf_op jit(solution)/shard_map/own_factor/pallas_call | solution.py:158
  98.2 0.3 collective-permute-done.7.right_ref
  98.4 0.0 collective-permute-done.4.one_ref
  98.4 8.7 %collective-permute-done.5.two_ref = bf16[128,896]{1,0:T(8,128)(2,1)} collective-permute-done((bf16[128,896]{1,0:T(8,128)(2,1)}, bf16[128,896]{1,0:T(8,128)(2,1)}, u32[]{:S(2)}, u32[]{:S(2)}) %collective-permute-start.5) | collective-permute-done | bytes 229408 | tf_op jit(solution)/shard_map/ppermute | solution.py:490
  107.2 0.0 collective-permute-done.6.three_ref
  107.2 0.0 copy-done.12
  107.2 3.1 %final.1 = f32[1,128,3072]{2,1,0:T(8,128)} custom-call(s32[14]{0:T(128)S(1)} %copy-done.15, f32[1,128,4096]{2,1,0:T(8,128)S(1)} %copy-done, bf16[128,1024]{1,0:T(8,128)(2,1)S(1)} %copy-done.12, bf16[128,896]{1,0:T(8,128)(2,1)S(1)} %collective-permute-done.4.one_ref, bf16[128,896]{1,0:T(8,128)(2,1)} %collective-permute-done.5.two_ref, ...), custom_call_target="tpu_custom_call" | custom-call | tf_op jit(solution)/shard_map/final/pallas_call | solution.py:412
  (23 shorter events, 0.1 us)
Async XLA Ops:
  7.2 2.4 %copy-start.17 = (bf16[1,48,1536]{2,1,0:T(8,128)(2,1)S(1)}, bf16[1,48,1536]{2,1,0:T(8,128)(2,1)}, u32[]{:S(2)}) copy-start(bf16[1,48,1536]{2,1,0:T(8,128)(2,1)} %param.5) | copy-start | bytes 442372
  7.2 25.8 %copy-start.16 = (s32[1,12]{1,0:T(1,128)S(1)}, s32[1,12]{1,0:T(1,128)}, u32[]{:S(2)}) copy-start(s32[1,12]{1,0:T(1,128)} %param.6) | copy-start | bytes 148
  7.2 62.4 %all-gather.4.cloned.1.call-start = ((), (), s32[]{:S(2)}) async-start(), calls=%async_computation.2 | async-start | bytes 2359296 | tf_op jit(solution)/shard_map/all_gather | solution.py:467
  9.6 22.0 %collective-permute-start = (bf16[48,1536]{1,0:T(8,128)(2,1)S(1)}, bf16[48,1536]{1,0:T(8,128)(2,1)S(1)}, u32[]{:S(2)}, u32[]{:S(2)}) collective-permute-start(bf16[48,1536]{1,0:T(8,128)(2,1)S(1)} %bitcast.10), channel_id=1, source_target_pairs={{0,32},{32,0},{64,96},{96,64},{128,160},{160,128},{192,224},{224,1... | collective-permute-start | bytes 442376 | tf_op jit(solution)/shard_map/ppermute | solution.py:469
  31.6 17.6 %copy-start.4 = (bf16[512,512]{1,0:T(8,128)(2,1)}, bf16[512,512]{1,0:T(8,128)(2,1)S(1)}, u32[]{:S(2)}) copy-start(bf16[512,512]{1,0:T(8,128)(2,1)S(1)} %all-gather) | copy-start | bytes 1572868
  31.6 17.0 %collective-permute-start.1 = (bf16[128,512]{1,0:T(8,128)(2,1)S(1)}, bf16[128,512]{1,0:T(8,128)(2,1)S(1)}, u32[]{:S(2)}, u32[]{:S(2)}) collective-permute-start(bf16[128,512]{1,0:T(8,128)(2,1)S(1)} %slice.5), channel_id=1, source_target_pairs={{4,1},{5,0},{6,3},{7,2},{12,9},{13,8},{14,11},{15,10},{20,17},{21,... | collective-permute-start | bytes 393224 | tf_op jit(solution)/shard_map/ppermute | solution.py:475
  33.0 1.0 copy-start.3
  34.0 29.6 %copy-start.14 = (s32[14]{0:T(128)}, s32[14]{0:T(128)S(1)}, u32[]{:S(2)}) copy-start(s32[14]{0:T(128)S(1)} %pad_add_fusion.where_ref) | copy-start | bytes 172
  34.9 28.6 %all-to-all-start = ((bf16[4,400,256]{2,1,0:T(8,128)(2,1)}), bf16[4,400,256]{2,1,0:T(8,128)(2,1)S(1)}, u32[]{:S(2)}, u32[]{:S(2)}) async-start(bf16[4,400,256]{2,1,0:T(8,128)(2,1)} %pack.1), calls=%async_computation | async-start | bytes 1638400 | tf_op jit(solution)/shard_map/all_to_all | solution.py:474
  49.2 21.1 %copy-start.6 = (bf16[128,512]{1,0:T(8,128)(2,1)}, bf16[128,512]{1,0:T(8,128)(2,1)S(1)}, u32[]{:S(2)}) copy-start(bf16[128,512]{1,0:T(8,128)(2,1)S(1)} %first_relay.1.mine_ref) | copy-start | bytes 393220
  49.2 9.7 %collective-permute-start.2 = (bf16[128,512]{1,0:T(8,128)(2,1)S(1)}, bf16[128,512]{1,0:T(8,128)(2,1)S(1)}, u32[]{:S(2)}, u32[]{:S(2)}) collective-permute-start(bf16[128,512]{1,0:T(8,128)(2,1)S(1)} %first_relay.1.mine_ref), channel_id=1, source_target_pairs={{0,1},{1,0},{2,3},{3,2},{4,5},{5,4},{6,7},{7,6},{8,9},{9,8},{10,11... | collective-permute-start | bytes 393224 | tf_op jit(solution)/shard_map/ppermute | solution.py:477
  58.9 11.4 %copy-start.8 = (bf16[128,512]{1,0:T(8,128)(2,1)}, bf16[128,512]{1,0:T(8,128)(2,1)S(1)}, u32[]{:S(2)}) copy-start(bf16[128,512]{1,0:T(8,128)(2,1)S(1)} %collective-permute-done.2.beside_ref) | copy-start | bytes 393220
  58.9 10.6 %collective-permute-start.3 = (bf16[256,512]{1,0:T(8,128)(2,1)S(1)}, bf16[256,512]{1,0:T(8,128)(2,1)S(1)}, u32[]{:S(2)}, u32[]{:S(2)}) collective-permute-start(bf16[256,512]{1,0:T(8,128)(2,1)S(1)} %pad_maximum_fusion), channel_id=1, source_target_pairs={{0,7},{1,2},{2,1},{3,4},{4,3},{5,6},{6,5},{7,0},{8,15},{9,10},{10,... | collective-permute-start | bytes 786440 | tf_op jit(solution)/shard_map/ppermute | solution.py:478
  63.5 6.1 %copy-start.2 = (bf16[4,400,256]{2,1,0:T(8,128)(2,1)}, bf16[4,400,256]{2,1,0:T(8,128)(2,1)S(1)}, u32[]{:S(2)}) copy-start(bf16[4,400,256]{2,1,0:T(8,128)(2,1)S(1)} %all-to-all-done.nexts_ref.parts_ref) | copy-start | bytes 2457604
  65.0 21.2 %all-to-all-start.1 = ((bf16[8,144,256]{2,1,0:T(8,128)(2,1)}), bf16[8,144,256]{2,1,0:T(8,128)(2,1)}, u32[]{:S(2)}, u32[]{:S(2)}) async-start(bf16[8,144,256]{2,1,0:T(8,128)(2,1)} %wanted.1), calls=%async_computation.1 | async-start | bytes 1179648 | tf_op jit(solution)/shard_map/all_to_all | solution.py:486
  69.6 0.7 copy-start.10
  70.3 16.0 %copy-start.15 = (s32[14]{0:T(128)S(1)}, s32[14]{0:T(128)}, u32[]{:S(2)}) copy-start(s32[14]{0:T(128)} %copy-done.14) | copy-start | bytes 172
  70.3 23.1 %copy-start = (f32[1,128,4096]{2,1,0:T(8,128)S(1)}, f32[1,128,4096]{2,1,0:T(8,128)}, u32[]{:S(2)}) copy-start(f32[1,128,4096]{2,1,0:T(8,128)} %front_ref.5) | copy-start | bytes 6291460
  70.3 23.1 %copy-start.1 = (bf16[1,2,512,512]{3,2,1,0:T(8,128)(2,1)S(1)}, bf16[1,2,512,512]{3,2,1,0:T(8,128)(2,1)}, u32[]{:S(2)}) copy-start(bf16[1,2,512,512]{3,2,1,0:T(8,128)(2,1)} %inverse_ref.5) | copy-start | bytes 3145732
  70.3 23.1 %copy-start.5 = (bf16[128,512]{1,0:T(8,128)(2,1)S(1)}, bf16[128,512]{1,0:T(8,128)(2,1)}, u32[]{:S(2)}) copy-start(bf16[128,512]{1,0:T(8,128)(2,1)} %get-tuple-element.15.first_ref) | copy-start | bytes 393220
  77.8 20.7 %collective-permute-start.4 = (bf16[128,896]{1,0:T(8,128)(2,1)}, bf16[128,896]{1,0:T(8,128)(2,1)S(1)}, u32[]{:S(2)}, u32[]{:S(2)}) collective-permute-start(bf16[128,896]{1,0:T(8,128)(2,1)} %get-tuple-element.21), channel_id=1, source_target_pairs={{8,16},{16,24},{24,0},{9,17},{17,25},{25,1},{10,18},{18,26},{26,2}... | collective-permute-start | bytes 688136 | tf_op jit(solution)/shard_map/ppermute | solution.py:491
  79.1 28.1 %collective-permute-start.5 = (bf16[128,896]{1,0:T(8,128)(2,1)}, bf16[128,896]{1,0:T(8,128)(2,1)}, u32[]{:S(2)}, u32[]{:S(2)}) collective-permute-start(bf16[128,896]{1,0:T(8,128)(2,1)} %get-tuple-element.22), channel_id=1, source_target_pairs={{8,24},{16,0},{24,8},{9,25},{17,1},{25,9},{10,26},{18,2},{26,10},{... | collective-permute-start | bytes 688136 | tf_op jit(solution)/shard_map/ppermute | solution.py:490
  80.4 26.8 %collective-permute-start.6 = (bf16[128,896]{1,0:T(8,128)(2,1)}, bf16[128,896]{1,0:T(8,128)(2,1)}, u32[]{:S(2)}, u32[]{:S(2)}) collective-permute-start(bf16[128,896]{1,0:T(8,128)(2,1)} %get-tuple-element.23), channel_id=1, source_target_pairs={{8,0},{16,8},{24,16},{9,1},{17,9},{25,17},{10,2},{18,10},{26,18},{... | collective-permute-start | bytes 688136 | tf_op jit(solution)/shard_map/ppermute | solution.py:492
  87.0 11.4 %collective-permute-start.7 = (bf16[128,768]{1,0:T(8,128)(2,1)S(1)}, bf16[128,768]{1,0:T(8,128)(2,1)S(1)}, u32[]{:S(2)}, u32[]{:S(2)}) collective-permute-start(bf16[128,768]{1,0:T(8,128)(2,1)S(1)} %join.1.left_ref), channel_id=1, source_target_pairs={{8,16},{0,24},{9,17},{1,25},{10,18},{2,26},{11,19},{3,27},{12,20},... | collective-permute-start | bytes 589832 | tf_op jit(solution)/shard_map/ppermute | solution.py:495
  93.4 0.9 copy-start.7
  94.4 0.9 copy-start.9
  95.3 0.9 copy-start.11
  96.2 11.0 %copy-start.12 = (bf16[128,1024]{1,0:T(8,128)(2,1)S(1)}, bf16[128,1024]{1,0:T(8,128)(2,1)}, u32[]{:S(2)}) copy-start(bf16[128,1024]{1,0:T(8,128)(2,1)} %get-tuple-element.20.zero_ref) | copy-start | bytes 786436
  96.2 11.0 %copy-start.13 = (bf16[128,512]{1,0:T(8,128)(2,1)S(1)}, bf16[128,512]{1,0:T(8,128)(2,1)}, u32[]{:S(2)}) copy-start(bf16[128,512]{1,0:T(8,128)(2,1)} %get-tuple-element.24.across_groups_ref) | copy-start | bytes 393220
Sparse Core Ops, SparseCore 0:
  10.7 52.6 all-gather.3

commit v8 on v6

--- a/solution.py
+++ b/solution.py
@@ -12,9 +12,10 @@
 CHILD = 1536
 CHILD_BLOCKS = 12
 CHILD_ROWS = 48
-HALF = CHILD // 2
+KEPT = 1024
+LENT = CHILD - KEPT
 THIRD = 256
-PART_ROWS = 2 * ROWS + 3 * CHILD_ROWS
+PART_ROWS = 2 * ROWS + 4 * CHILD_ROWS
 MIB = 1024 * 1024
 VMEM_LIMIT = 60 * MIB
 
@@ -73,10 +74,9 @@
         for half in range(2):
             place = slice(half * ROWS, (half + 1) * ROWS)
             parts_ref[k, place] = both_ref[:, half * THIRD : (half + 1) * THIRD]
-        first = 0 if k >= 2 else HALF
-        for part in range(3):
+        for part in range(4):
             start = 2 * ROWS + part * CHILD_ROWS
-            column = first + part * THIRD
+            column = part * THIRD if k >= 2 else KEPT + part % 2 * THIRD
             parts_ref[k, start : start + CHILD_ROWS] = child_ref[:, column : column + THIRD]
 
 
@@ -292,7 +292,7 @@
     return jnp.where((r == 0) | (r == 3), 3, 2)
 
 
-def join_kernel(where_ref, child_ref, half_ref, sems):
+def join_kernel(where_ref, child_ref, half_ref, lent_ref, sems):
     r, z = where_ref[0], where_ref[1]
     found, child = wanted_child(where_ref, carried_group(r) * 8 + z)
 
@@ -304,7 +304,7 @@
                 sems.at[i, part],
             )
             for i, (z_from, start, rows, place) in enumerate(PIECES[j])
-            for part in range(3)
+            for part in range(4)
         ]
 
     half_ref[...] = jnp.zeros_like(half_ref)
@@ -315,6 +315,7 @@
                 copy.start()
             for copy in copies(j):
                 copy.wait()
+    lent_ref[...] = half_ref[:, :LENT]
 
 
 def join(where, children):
@@ -324,10 +325,10 @@
             num_scalar_prefetch=1,
             grid=(1,),
             in_specs=[pl.BlockSpec(memory_space=pl.ANY)],
-            out_specs=pl.BlockSpec((ROWS, HALF), lambda i, w: (0, 0)),
-            scratch_shapes=[pltpu.SemaphoreType.DMA((4, 3))],
-        ),
-        out_shape=jax.ShapeDtypeStruct((ROWS, HALF), BF16),
+            out_specs=[pl.BlockSpec((ROWS, width), lambda i, w: (0, 0)) for width in (KEPT, LENT)],
+            scratch_shapes=[pltpu.SemaphoreType.DMA((4, 4))],
+        ),
+        out_shape=[jax.ShapeDtypeStruct((ROWS, width), BF16) for width in (KEPT, LENT)],
         compiler_params=pltpu.CompilerParams(vmem_limit_bytes=8 * MIB),
         name="join",
     )(where, children)
@@ -340,8 +341,8 @@
     r, z = where_ref[0], where_ref[1]
     found, _ = wanted_child(where_ref, r * 8 + z)
     halves = [
-        pltpu.make_async_copy(ref, block_ref.at[:, pl.ds(half * HALF, HALF)], child_sems.at[half])
-        for half, ref in enumerate((left_ref, right_ref))
+        pltpu.make_async_copy(left_ref, block_ref.at[:, pl.ds(0, KEPT)], child_sems.at[0]),
+        pltpu.make_async_copy(right_ref, block_ref.at[:, pl.ds(KEPT, LENT)], child_sems.at[1]),
     ]
 
     def read_front(g):
@@ -422,7 +423,7 @@
     copies = []
     for z in range(8):
         _, child = wanted_child(where_ref, group * 8 + z)
-        source = parts_ref.at[jnp.minimum(child // 3, 3), pl.ds(2 * ROWS, 3 * CHILD_ROWS), :]
+        source = parts_ref.at[jnp.minimum(child // 3, 3), pl.ds(2 * ROWS, 4 * CHILD_ROWS), :]
         copies.append(pltpu.make_async_copy(source, out_ref.at[z], sems.at[z]))
         copies[z].start()
     for copy in copies:
@@ -439,7 +440,7 @@
             out_specs=pl.BlockSpec(memory_space=pl.ANY),
             scratch_shapes=[pltpu.SemaphoreType.DMA((8,))],
         ),
-        out_shape=jax.ShapeDtypeStruct((8, 3 * CHILD_ROWS, THIRD), BF16),
+        out_shape=jax.ShapeDtypeStruct((8, 4 * CHILD_ROWS, THIRD), BF16),
         compiler_params=pltpu.CompilerParams(vmem_limit_bytes=8 * MIB),
         name="wanted",
     )(where, parts)
@@ -477,8 +478,8 @@
     one = lax.ppermute(one, "row", [(i, (i + 1) % 4) for i in range(1, 4)])
     three = lax.ppermute(three, "row", [(i, (i + 3) % 4) for i in range(1, 4)])
     pieces = zero, one, two, three, across_groups
-    left = join(where, children)
-    right = lax.ppermute(left, "row", [(1, 2), (0, 3)])
+    left, lent = join(where, children)
+    right = lax.ppermute(lent, "row", [(1, 2), (0, 3)])
     return factor, final(where, assembled, pieces, (left, right))
 
 

time: 116 us -> 116 us (level)
  starting transfers between devices: 39.5 us -> 37.9 us
    ppermute x1, waiting for transfers between devices: 7.56 us -> 0.3 us  [on_device(): two = lax.ppermute(two, 'row', [(i, (i + 2) % 4) for i in range(1, 4)])]
    all_to_all x1, waiting for transfers between devices: 5.63 us -> 11.4 us  [on_device(): children = lax.all_to_all(pieces, 'col', 0, 0)]
    ppermute x1, starting transfers between devices: 4.84 us -> 1.81 us  [on_device(): right = lax.ppermute(lent, 'row', [(1, 2), (0, 3)])]
    all_to_all x1, starting transfers between devices: 8.29 us -> 9.59 us  [on_device(): children = lax.all_to_all(pieces, 'col', 0, 0)]
  transfers between devices with their start and end apart: 11 -> 11, of which waited for: 4 -> 6; matrix products, arithmetic and copies ran while one was open for 0% -> 0% of each run, Pallas kernels for 11% -> 12%
where the time goes in v8:
time: 116 us; the launch traced here: 115 us
  starting transfers between devices  37.9 us (33%)
  waiting for transfers between devices  24.2 us (21%)
  Pallas kernels  19.7 us (17%)
  between operations  14.3 us (12%)
  blocking collectives  14.1 us (12%)
  local copies, waits for them, and re-layouts  4.43 us (4%)
    all_gather x1, blocking collectives, on_device(): firsts = lax.all_gather(first, 'row', axis=0)  14.1 us
    all_to_all x1, waiting for transfers between devices, on_device(): children = lax.all_to_all(pieces, 'col', 0, 0)  11.4 us
    all_to_all x1, starting transfers between devices, on_device(): children = lax.all_to_all(pieces, 'col', 0, 0)  9.59 us
    ppermute x1, starting transfers between devices, on_device(): child = lax.ppermute(update[0], 'front', [(i, i ^ 1) for i in range(16)])  8.79 us
    pallas_call x1, Pallas kernels, products(): pl.pallas_call(product_kernel, grid_spec=pltpu.PrefetchScalarGridSpec(num...  7.57 us
    ppermute x1, waiting for transfers between devices, on_device(): passed = lax.ppermute(top, 'col', [(4, 1), (5, 0), (6, 3), (7, 2)])  6.6 us
    ppermute x1, starting transfers between devices, on_device(): lax.ppermute(jnp.concatenate([mine, beside]), 'col', [(i, (i + 1) % 8 if...  4.45 us
    unnamed x36, local copies, waits for them, and re-layouts  4.42 us
  transfers between devices with their start and end apart: 11, of which 6 were waited for; matrix products, arithmetic and copies ran while one was open for 0% of the time, Pallas kernels for 12%

profile of v8, /device:TPU:1, one launch (start us, length us, event | category | flops | bytes accessed | tf_op | source)
XLA Modules:
  0.0 114.7 jit_solution(17287388912991996671)
XLA Ops:
  7.2 0.0 copy-start.17
  7.2 0.0 copy-start.16
  7.2 0.0 all-gather.4.cloned.1.call-start
  7.2 2.3 %first_panel.1 = (bf16[128,1024]{1,0:T(8,128)(2,1)}, bf16[128,512]{1,0:T(8,128)(2,1)}) custom-call(f32[1,128,4096]{2,1,0:T(8,128)} %front_ref.5, bf16[1,2,512,512]{3,2,1,0:T(8,128)(2,1)} %inverse_ref.5), custom_call_target="tpu_custom_call" | custom-call | tf_op jit(solution)/shard_map/first_panel/pallas_call | solution.py:52
  9.6 0.0 all-gather.4.cloned.1.call-update
  9.6 0.0 copy-done.17
  9.6 8.8 %collective-permute-start = (bf16[48,1536]{1,0:T(8,128)(2,1)S(1)}, bf16[48,1536]{1,0:T(8,128)(2,1)S(1)}, u32[]{:S(2)}, u32[]{:S(2)}) collective-permute-start(bf16[48,1536]{1,0:T(8,128)(2,1)S(1)} %bitcast.10), channel_id=1, source_target_pairs={{0,32},{32,0},{64,96},{96,64},{128,160},{160,128},{192,224},{224,1... | collective-permute-start | bytes 442376 | tf_op jit(solution)/shard_map/ppermute | solution.py:456
  18.4 14.1 %all-gather = bf16[512,512]{1,0:T(8,128)(2,1)S(1)} all-gather(bf16[128,512]{1,0:T(8,128)(2,1)} %get-tuple-element.17.first_ref), channel_id=2, replica_groups=mesh['front'=16,'row'=4,'col'=8] {'row'}, dimensions={0}, use_global_device_ids=true | all-gather | bytes 655360 | tf_op jit(solution)/shard_map/all_gather | solution.py:457
  32.5 0.0 collective-permute-done.child_ref
  32.5 1.3 %collective-permute-start.1 = (bf16[128,512]{1,0:T(8,128)(2,1)S(1)}, bf16[128,512]{1,0:T(8,128)(2,1)S(1)}, u32[]{:S(2)}, u32[]{:S(2)}) collective-permute-start(bf16[128,512]{1,0:T(8,128)(2,1)S(1)} %slice.5), channel_id=1, source_target_pairs={{4,1},{5,0},{6,3},{7,2},{12,9},{13,8},{14,11},{15,10},{20,17},{21,... | collective-permute-start | bytes 393224 | tf_op jit(solution)/shard_map/ppermute | solution.py:462
  33.8 0.0 copy-done.16
  33.9 0.1 pad_add_fusion.where_ref
  33.9 0.9 copy-done.3
  34.9 1.0 pack.1
  35.9 3.6 %all-to-all-start = ((bf16[4,448,256]{2,1,0:T(8,128)(2,1)}), bf16[4,448,256]{2,1,0:T(8,128)(2,1)S(1)}, u32[]{:S(2)}, u32[]{:S(2)}) async-start(bf16[4,448,256]{2,1,0:T(8,128)(2,1)} %pack.1), calls=%async_computation | async-start | bytes 1835008 | tf_op jit(solution)/shard_map/all_to_all | solution.py:461
  39.5 6.6 %collective-permute-done.1.passed_ref = bf16[128,512]{1,0:T(8,128)(2,1)S(1)} collective-permute-done((bf16[128,512]{1,0:T(8,128)(2,1)S(1)}, bf16[128,512]{1,0:T(8,128)(2,1)S(1)}, u32[]{:S(2)}, u32[]{:S(2)}) %collective-permute-start.1) | collective-permute-done | bytes 131104 | tf_op jit(solution)/shard_map/ppermute | solution.py:462
  46.1 0.6 first_relay.1.mine_ref
  46.7 0.0 copy-done.4
  46.7 0.0 copy-start.6
  46.7 4.4 %collective-permute-start.2 = (bf16[128,512]{1,0:T(8,128)(2,1)S(1)}, bf16[128,512]{1,0:T(8,128)(2,1)S(1)}, u32[]{:S(2)}, u32[]{:S(2)}) collective-permute-start(bf16[128,512]{1,0:T(8,128)(2,1)S(1)} %first_relay.1.mine_ref), channel_id=1, source_target_pairs={{0,1},{1,0},{2,3},{3,2},{4,5},{5,4},{6,7},{7,6},{8,9},{9,8},{10,11... | collective-permute-start | bytes 393224 | tf_op jit(solution)/shard_map/ppermute | solution.py:464
  51.1 4.3 %collective-permute-done.2.beside_ref = bf16[128,512]{1,0:T(8,128)(2,1)S(1)} collective-permute-done((bf16[128,512]{1,0:T(8,128)(2,1)S(1)}, bf16[128,512]{1,0:T(8,128)(2,1)S(1)}, u32[]{:S(2)}, u32[]{:S(2)}) %collective-permute-start.2) | collective-permute-done | bytes 131104 | tf_op jit(solution)/shard_map/ppermute | solution.py:464
  55.5 4.5 %collective-permute-start.3 = (bf16[256,512]{1,0:T(8,128)(2,1)S(1)}, bf16[256,512]{1,0:T(8,128)(2,1)S(1)}, u32[]{:S(2)}, u32[]{:S(2)}) collective-permute-start(bf16[256,512]{1,0:T(8,128)(2,1)S(1)} %pad_maximum_fusion), channel_id=1, source_target_pairs={{0,7},{1,2},{2,1},{3,4},{4,3},{5,6},{6,5},{7,0},{8,15},{9,10},{10,... | collective-permute-start | bytes 786440 | tf_op jit(solution)/shard_map/ppermute | solution.py:465
  59.9 0.8 all-to-all-done.nexts_ref.parts_ref
  60.7 0.0 copy-done.14
  60.7 1.6 %wanted.1 = bf16[8,192,256]{2,1,0:T(8,128)(2,1)} custom-call(s32[14]{0:T(128)S(1)} %pad_add_fusion.where_ref, bf16[4,448,256]{2,1,0:T(8,128)(2,1)S(1)} %all-to-all-done.nexts_ref.parts_ref), custom_call_target="tpu_custom_call" | custom-call | tf_op jit(solution)/shard_map/wanted/pallas_call | solution.py:434
  62.2 9.6 %all-to-all-start.1 = ((bf16[8,192,256]{2,1,0:T(8,128)(2,1)}), bf16[8,192,256]{2,1,0:T(8,128)(2,1)}, u32[]{:S(2)}, u32[]{:S(2)}) async-start(bf16[8,192,256]{2,1,0:T(8,128)(2,1)} %wanted.1), calls=%async_computation.1 | async-start | bytes 1572864 | tf_op jit(solution)/shard_map/all_to_all | solution.py:473
  71.8 0.0 collective-permute-done.3.across_ref
  71.8 0.0 copy-start.10
  71.8 0.0 all-gather.4.cloned.1.call-done
  71.9 0.7 copy-done.10
  72.5 0.0 copy-start.1
  72.6 7.6 %products.1 = (bf16[128,1024]{1,0:T(8,128)(2,1)}, bf16[128,896]{1,0:T(8,128)(2,1)}, bf16[128,896]{1,0:T(8,128)(2,1)}, bf16[128,896]{1,0:T(8,128)(2,1)}, bf16[128,512]{1,0:T(8,128)(2,1)}) custom-call(s32[14]{0:T(128)} %copy-done.14, bf16[1,2,512,512]{3,2,1,0:T(8,128)(2,1)} %inverse_ref.5, bf16[4,128,512]{2,1,0:T(8,128)(2,1)} %bitcast.7, ...), custom_call_target="tpu_custom_call" | custom-call | flops 34359738368 | bytes 1048576 | tf_op jit(solution)/shard_map/products/pallas_call | solution.py:251
  80.2 1.3 %collective-permute-start.4 = (bf16[128,896]{1,0:T(8,128)(2,1)}, bf16[128,896]{1,0:T(8,128)(2,1)S(1)}, u32[]{:S(2)}, u32[]{:S(2)}) collective-permute-start(bf16[128,896]{1,0:T(8,128)(2,1)} %get-tuple-element.23), channel_id=1, source_target_pairs={{8,16},{16,24},{24,0},{9,17},{17,25},{25,1},{10,18},{18,26},{26,2}... | collective-permute-start | bytes 688136 | tf_op jit(solution)/shard_map/ppermute | solution.py:478
  81.5 1.3 %collective-permute-start.5 = (bf16[128,896]{1,0:T(8,128)(2,1)}, bf16[128,896]{1,0:T(8,128)(2,1)}, u32[]{:S(2)}, u32[]{:S(2)}) collective-permute-start(bf16[128,896]{1,0:T(8,128)(2,1)} %get-tuple-element.24), channel_id=1, source_target_pairs={{8,24},{16,0},{24,8},{9,25},{17,1},{25,9},{10,26},{18,2},{26,10},{... | collective-permute-start | bytes 688136 | tf_op jit(solution)/shard_map/ppermute | solution.py:477
  82.8 1.3 %collective-permute-start.6 = (bf16[128,896]{1,0:T(8,128)(2,1)}, bf16[128,896]{1,0:T(8,128)(2,1)}, u32[]{:S(2)}, u32[]{:S(2)}) collective-permute-start(bf16[128,896]{1,0:T(8,128)(2,1)} %get-tuple-element.25), channel_id=1, source_target_pairs={{8,0},{16,8},{24,16},{9,1},{17,9},{25,17},{10,2},{18,10},{26,18},{... | collective-permute-start | bytes 688136 | tf_op jit(solution)/shard_map/ppermute | solution.py:479
  84.1 11.4 %all-to-all-done.1.child_ref = bf16[8,192,256]{2,1,0:T(8,128)(2,1)} async-done(((bf16[8,192,256]{2,1,0:T(8,128)(2,1)}), bf16[8,192,256]{2,1,0:T(8,128)(2,1)}, u32[]{:S(2)}, u32[]{:S(2)}) %all-to-all-start.1) | async-done | bytes 786464 | tf_op jit(solution)/shard_map/all_to_all | solution.py:473
  95.5 0.0 copy-done.15
  95.5 1.7 %join.1 = (bf16[128,1024]{1,0:T(8,128)(2,1)S(1)}, bf16[128,512]{1,0:T(8,128)(2,1)S(1)}) custom-call(s32[14]{0:T(128)S(1)} %copy-done.15, bf16[8,192,256]{2,1,0:T(8,128)(2,1)} %all-to-all-done.1.child_ref), custom_call_target="tpu_custom_call" | custom-call | tf_op jit(solution)/shard_map/join/pallas_call | solution.py:322
  97.2 1.8 %collective-permute-start.7 = (bf16[128,512]{1,0:T(8,128)(2,1)S(1)}, bf16[128,512]{1,0:T(8,128)(2,1)S(1)}, u32[]{:S(2)}, u32[]{:S(2)}) collective-permute-start(bf16[128,512]{1,0:T(8,128)(2,1)S(1)} %get-tuple-element.29), channel_id=1, source_target_pairs={{8,16},{0,24},{9,17},{1,25},{10,18},{2,26},{11,19},{3,27},{12,20},... | collective-permute-start | bytes 393224 | tf_op jit(solution)/shard_map/ppermute | solution.py:482
  99.0 0.9 copy-done.7
  99.9 0.9 copy-done.9
  100.8 0.9 copy-done.11
  101.8 1.9 %own_factor.1 = bf16[1,128,1024]{2,1,0:T(8,128)(2,1)} custom-call(s32[14]{0:T(128)S(1)} %copy-done.15, f32[1,128,4096]{2,1,0:T(8,128)S(1)} %copy-done, bf16[1,2,512,512]{3,2,1,0:T(8,128)(2,1)S(1)} %copy-done.1, bf16[128,512]{1,0:T(8,128)(2,1)S(1)} %copy-done.5, bf16[128,512]{1,0:T(8,128)(2,1)S(1)} %copy-done.7, bf16[128,512]{1,0:T(8,128)(2,1)S(1)} %copy-done.9, ...), custom_call_target="tpu_custom_call" | custom-call | flops 268435456 | bytes 2097152 | tf_op jit(solution)/shard_map/own_factor/pallas_call | solution.py:151
  103.7 0.0 collective-permute-done.7.right_ref
  103.7 0.0 collective-permute-done.4.one_ref
  103.7 0.3 collective-permute-done.5.two_ref
  104.0 0.7 collective-permute-done.6.three_ref
  104.7 3.1 %final.1 = f32[1,128,3072]{2,1,0:T(8,128)} custom-call(s32[14]{0:T(128)S(1)} %copy-done.15, f32[1,128,4096]{2,1,0:T(8,128)S(1)} %copy-done, bf16[128,1024]{1,0:T(8,128)(2,1)S(1)} %copy-done.12, bf16[128,896]{1,0:T(8,128)(2,1)S(1)} %collective-permute-done.4.one_ref, bf16[128,896]{1,0:T(8,128)(2,1)} %collective-permute-done.5.two_ref, ...), custom_call_target="tpu_custom_call" | custom-call | tf_op jit(solution)/shard_map/final/pallas_call | solution.py:399
  (23 shorter events, 0.1 us)
Async XLA Ops:
  7.2 2.4 %copy-start.17 = (bf16[1,48,1536]{2,1,0:T(8,128)(2,1)S(1)}, bf16[1,48,1536]{2,1,0:T(8,128)(2,1)}, u32[]{:S(2)}) copy-start(bf16[1,48,1536]{2,1,0:T(8,128)(2,1)} %param.5) | copy-start | bytes 442372
  7.2 26.7 %copy-start.16 = (s32[1,12]{1,0:T(1,128)S(1)}, s32[1,12]{1,0:T(1,128)}, u32[]{:S(2)}) copy-start(s32[1,12]{1,0:T(1,128)} %param.6) | copy-start | bytes 148
  7.2 64.7 %all-gather.4.cloned.1.call-start = ((), (), s32[]{:S(2)}) async-start(), calls=%async_computation.2 | async-start | bytes 2359296 | tf_op jit(solution)/shard_map/all_gather | solution.py:454
  9.6 22.9 %collective-permute-start = (bf16[48,1536]{1,0:T(8,128)(2,1)S(1)}, bf16[48,1536]{1,0:T(8,128)(2,1)S(1)}, u32[]{:S(2)}, u32[]{:S(2)}) collective-permute-start(bf16[48,1536]{1,0:T(8,128)(2,1)S(1)} %bitcast.10), channel_id=1, source_target_pairs={{0,32},{32,0},{64,96},{96,64},{128,160},{160,128},{192,224},{224,1... | collective-permute-start | bytes 442376 | tf_op jit(solution)/shard_map/ppermute | solution.py:456
  32.5 14.2 %copy-start.4 = (bf16[512,512]{1,0:T(8,128)(2,1)}, bf16[512,512]{1,0:T(8,128)(2,1)S(1)}, u32[]{:S(2)}) copy-start(bf16[512,512]{1,0:T(8,128)(2,1)S(1)} %all-gather) | copy-start | bytes 1572868
  32.5 13.6 %collective-permute-start.1 = (bf16[128,512]{1,0:T(8,128)(2,1)S(1)}, bf16[128,512]{1,0:T(8,128)(2,1)S(1)}, u32[]{:S(2)}, u32[]{:S(2)}) collective-permute-start(bf16[128,512]{1,0:T(8,128)(2,1)S(1)} %slice.5), channel_id=1, source_target_pairs={{4,1},{5,0},{6,3},{7,2},{12,9},{13,8},{14,11},{15,10},{20,17},{21,... | collective-permute-start | bytes 393224 | tf_op jit(solution)/shard_map/ppermute | solution.py:462
  33.9 1.0 copy-start.3
  34.9 25.8 %copy-start.14 = (s32[14]{0:T(128)}, s32[14]{0:T(128)S(1)}, u32[]{:S(2)}) copy-start(s32[14]{0:T(128)S(1)} %pad_add_fusion.where_ref) | copy-start | bytes 172
  35.9 24.8 %all-to-all-start = ((bf16[4,448,256]{2,1,0:T(8,128)(2,1)}), bf16[4,448,256]{2,1,0:T(8,128)(2,1)S(1)}, u32[]{:S(2)}, u32[]{:S(2)}) async-start(bf16[4,448,256]{2,1,0:T(8,128)(2,1)} %pack.1), calls=%async_computation | async-start | bytes 1835008 | tf_op jit(solution)/shard_map/all_to_all | solution.py:461
  46.7 25.9 %copy-start.6 = (bf16[128,512]{1,0:T(8,128)(2,1)}, bf16[128,512]{1,0:T(8,128)(2,1)S(1)}, u32[]{:S(2)}) copy-start(bf16[128,512]{1,0:T(8,128)(2,1)S(1)} %first_relay.1.mine_ref) | copy-start | bytes 393220
  46.7 8.7 %collective-permute-start.2 = (bf16[128,512]{1,0:T(8,128)(2,1)S(1)}, bf16[128,512]{1,0:T(8,128)(2,1)S(1)}, u32[]{:S(2)}, u32[]{:S(2)}) collective-permute-start(bf16[128,512]{1,0:T(8,128)(2,1)S(1)} %first_relay.1.mine_ref), channel_id=1, source_target_pairs={{0,1},{1,0},{2,3},{3,2},{4,5},{5,4},{6,7},{7,6},{8,9},{9,8},{10,11... | collective-permute-start | bytes 393224 | tf_op jit(solution)/shard_map/ppermute | solution.py:464
  55.4 17.1 %copy-start.8 = (bf16[128,512]{1,0:T(8,128)(2,1)}, bf16[128,512]{1,0:T(8,128)(2,1)S(1)}, u32[]{:S(2)}) copy-start(bf16[128,512]{1,0:T(8,128)(2,1)S(1)} %collective-permute-done.2.beside_ref) | copy-start | bytes 393220
  55.5 16.4 %collective-permute-start.3 = (bf16[256,512]{1,0:T(8,128)(2,1)S(1)}, bf16[256,512]{1,0:T(8,128)(2,1)S(1)}, u32[]{:S(2)}, u32[]{:S(2)}) collective-permute-start(bf16[256,512]{1,0:T(8,128)(2,1)S(1)} %pad_maximum_fusion), channel_id=1, source_target_pairs={{0,7},{1,2},{2,1},{3,4},{4,3},{5,6},{6,5},{7,0},{8,15},{9,10},{10,... | collective-permute-start | bytes 786440 | tf_op jit(solution)/shard_map/ppermute | solution.py:465
  60.7 11.2 %copy-start.2 = (bf16[4,448,256]{2,1,0:T(8,128)(2,1)}, bf16[4,448,256]{2,1,0:T(8,128)(2,1)S(1)}, u32[]{:S(2)}) copy-start(bf16[4,448,256]{2,1,0:T(8,128)(2,1)S(1)} %all-to-all-done.nexts_ref.parts_ref) | copy-start | bytes 2752516
  62.2 33.3 %all-to-all-start.1 = ((bf16[8,192,256]{2,1,0:T(8,128)(2,1)}), bf16[8,192,256]{2,1,0:T(8,128)(2,1)}, u32[]{:S(2)}, u32[]{:S(2)}) async-start(bf16[8,192,256]{2,1,0:T(8,128)(2,1)} %wanted.1), calls=%async_computation.1 | async-start | bytes 1572864 | tf_op jit(solution)/shard_map/all_to_all | solution.py:473
  71.8 0.7 copy-start.10
  72.5 23.0 %copy-start.15 = (s32[14]{0:T(128)S(1)}, s32[14]{0:T(128)}, u32[]{:S(2)}) copy-start(s32[14]{0:T(128)} %copy-done.14) | copy-start | bytes 172
  72.5 26.4 %copy-start = (f32[1,128,4096]{2,1,0:T(8,128)S(1)}, f32[1,128,4096]{2,1,0:T(8,128)}, u32[]{:S(2)}) copy-start(f32[1,128,4096]{2,1,0:T(8,128)} %front_ref.5) | copy-start | bytes 6291460
  72.5 26.4 %copy-start.1 = (bf16[1,2,512,512]{3,2,1,0:T(8,128)(2,1)S(1)}, bf16[1,2,512,512]{3,2,1,0:T(8,128)(2,1)}, u32[]{:S(2)}) copy-start(bf16[1,2,512,512]{3,2,1,0:T(8,128)(2,1)} %inverse_ref.5) | copy-start | bytes 3145732
  72.6 26.4 %copy-start.5 = (bf16[128,512]{1,0:T(8,128)(2,1)S(1)}, bf16[128,512]{1,0:T(8,128)(2,1)}, u32[]{:S(2)}) copy-start(bf16[128,512]{1,0:T(8,128)(2,1)} %get-tuple-element.17.first_ref) | copy-start | bytes 393220
  80.2 23.6 %collective-permute-start.4 = (bf16[128,896]{1,0:T(8,128)(2,1)}, bf16[128,896]{1,0:T(8,128)(2,1)S(1)}, u32[]{:S(2)}, u32[]{:S(2)}) collective-permute-start(bf16[128,896]{1,0:T(8,128)(2,1)} %get-tuple-element.23), channel_id=1, source_target_pairs={{8,16},{16,24},{24,0},{9,17},{17,25},{25,1},{10,18},{18,26},{26,2}... | collective-permute-start | bytes 688136 | tf_op jit(solution)/shard_map/ppermute | solution.py:478
  81.5 22.6 %collective-permute-start.5 = (bf16[128,896]{1,0:T(8,128)(2,1)}, bf16[128,896]{1,0:T(8,128)(2,1)}, u32[]{:S(2)}, u32[]{:S(2)}) collective-permute-start(bf16[128,896]{1,0:T(8,128)(2,1)} %get-tuple-element.24), channel_id=1, source_target_pairs={{8,24},{16,0},{24,8},{9,25},{17,1},{25,9},{10,26},{18,2},{26,10},{... | collective-permute-start | bytes 688136 | tf_op jit(solution)/shard_map/ppermute | solution.py:477
  82.8 22.0 %collective-permute-start.6 = (bf16[128,896]{1,0:T(8,128)(2,1)}, bf16[128,896]{1,0:T(8,128)(2,1)}, u32[]{:S(2)}, u32[]{:S(2)}) collective-permute-start(bf16[128,896]{1,0:T(8,128)(2,1)} %get-tuple-element.25), channel_id=1, source_target_pairs={{8,0},{16,8},{24,16},{9,1},{17,9},{25,17},{10,2},{18,10},{26,18},{... | collective-permute-start | bytes 688136 | tf_op jit(solution)/shard_map/ppermute | solution.py:479
  95.5 9.2 %copy-start.12 = (bf16[128,1024]{1,0:T(8,128)(2,1)S(1)}, bf16[128,1024]{1,0:T(8,128)(2,1)}, u32[]{:S(2)}) copy-start(bf16[128,1024]{1,0:T(8,128)(2,1)} %get-tuple-element.22.zero_ref) | copy-start | bytes 786436
  95.5 9.2 %copy-start.13 = (bf16[128,512]{1,0:T(8,128)(2,1)S(1)}, bf16[128,512]{1,0:T(8,128)(2,1)}, u32[]{:S(2)}) copy-start(bf16[128,512]{1,0:T(8,128)(2,1)} %get-tuple-element.26.across_groups_ref) | copy-start | bytes 393220
  97.2 6.5 %collective-permute-start.7 = (bf16[128,512]{1,0:T(8,128)(2,1)S(1)}, bf16[128,512]{1,0:T(8,128)(2,1)S(1)}, u32[]{:S(2)}, u32[]{:S(2)}) collective-permute-start(bf16[128,512]{1,0:T(8,128)(2,1)S(1)} %get-tuple-element.29), channel_id=1, source_target_pairs={{8,16},{0,24},{9,17},{1,25},{10,18},{2,26},{11,19},{3,27},{12,20},... | collective-permute-start | bytes 393224 | tf_op jit(solution)/shard_map/ppermute | solution.py:482
  99.0 0.9 copy-start.7
  99.9 0.9 copy-start.9
  100.8 0.9 copy-start.11
Sparse Core Ops, SparseCore 0:
  10.7 53.1 all-gather.3
